TPU v7x, 512 devices: a whole 4x4x16 slice. The times are simulated.
512 devices in a mesh: group: 8 (over x, core), expert: 64 (over z, y).
Axes of the slice: x: 4, y: 4, z: 16, core: 2. Of those that a mesh axis runs over, the one named last changes fastest.
Arguments:
- layer_in: bfloat16 [16384, 1536], P(('group', 'expert')), may hold values from -6 to 6
- grad_out: bfloat16 [16384, 1536], P(('group', 'expert')), may hold values from -6 to 6
- expert_ids: int32 [16384, 8], P(('group', 'expert')), may hold values from 0 to 63, as said below
- gate_probs: bfloat16 [16384, 8], P(('group', 'expert')), may hold values from 0.049804688 to 0.5
- gate_weight: bfloat16 [64, 1536, 384], P('expert'), may hold values from -0.15625 to 0.15625
- up_weight: bfloat16 [64, 1536, 384], P('expert'), may hold values from -0.15625 to 0.15625
- down_weight: bfloat16 [64, 384, 1536], P('expert'), may hold values from -0.3125 to 0.3125
Outputs:
- grad_in: bfloat16 [16384, 1536], P(('group', 'expert'))
- grad_probs: bfloat16 [16384, 8], P(('group', 'expert'))
- grad_gate: float32 [64, 1536, 384], P('expert', 'group')
- grad_up: float32 [64, 1536, 384], P('expert', 'group')
- grad_down: float32 [64, 384, 1536], P('expert', 'group')
Inputs may be any that keep to these rules, and one draw needn't show every extreme that they name: `expert_ids`: each token names 8 different experts. Among the rows of the 32 tokens of one device, no expert is named more than 6 times, and one expert, the same for every device, is named exactly 6 times on each device.
All inputs are finite; a program needn't handle non-finite values.
Results may differ from a plain program's by a relative error of at most 0.015.
Values may be sent and summed in bfloat16 or wider, within the bound.
No kernel may reach another device: no remote copies, remote signals or barrier semaphores. Data moves between devices by JAX's collectives and lax.ppermute only.
A program may use at most 64 MiB of HBM per device.

v0:
```python
import jax
import jax.numpy as jnp
from jax import lax
from jax.sharding import PartitionSpec as P


def expert_rows(rows_in, rows_grad, rows_prob, gate_mat, up_mat, down_mat):
    pre_gate = jnp.dot(rows_in, gate_mat, preferred_element_type=jnp.float32)
    pre_up = jnp.dot(rows_in, up_mat, preferred_element_type=jnp.float32)
    sigmoid_gate = jax.nn.sigmoid(pre_gate)
    silu_gate = pre_gate * sigmoid_gate
    hidden = (silu_gate * pre_up).astype(jnp.bfloat16)
    out_rows = jnp.dot(hidden, down_mat, preferred_element_type=jnp.float32)
    prob_grad = jnp.sum(rows_grad.astype(jnp.float32) * out_rows, axis=1).astype(jnp.bfloat16)
    scaled = (rows_prob.astype(jnp.float32)[:, None] * rows_grad.astype(jnp.float32)).astype(
        jnp.bfloat16
    )
    grad_hidden = lax.dot_general(
        scaled, down_mat, (((1,), (1,)), ((), ())), preferred_element_type=jnp.float32
    )
    gate_grad = (
        grad_hidden * pre_up * sigmoid_gate * (1.0 + pre_gate * (1.0 - sigmoid_gate))
    ).astype(jnp.bfloat16)
    up_grad = (grad_hidden * silu_gate).astype(jnp.bfloat16)
    returned = lax.dot_general(
        gate_grad, gate_mat, (((1,), (1,)), ((), ())), preferred_element_type=jnp.float32
    )
    returned = returned + lax.dot_general(
        up_grad, up_mat, (((1,), (1,)), ((), ())), preferred_element_type=jnp.float32
    )
    gate_up_grad = jnp.concatenate([gate_grad, up_grad], axis=1)
    return (returned.astype(jnp.bfloat16), prob_grad, hidden, gate_up_grad, scaled)


def slot_work(rows_in, rows_grad, rows_prob, weights):
    sources, slot_count, model_width = rows_in.shape
    flat_count = sources * slot_count
    results = expert_rows(
        rows_in.reshape(flat_count, model_width),
        rows_grad.reshape(flat_count, model_width),
        rows_prob.reshape(flat_count),
        *weights
    )
    return tuple((result.reshape((sources, slot_count) + result.shape[1:]) for result in results))


def per_device(layer_in, grad_out, expert_ids, gate_probs, gate_weight, up_weight, down_weight):
    experts = lax.axis_size("expert")
    tokens_here, choices = expert_ids.shape
    model_width = layer_in.shape[1]
    hidden_width = gate_weight.shape[2]
    capacity = 3 * tokens_here * choices // (2 * experts)
    weights = (gate_weight[0], up_weight[0], down_weight[0])
    flat_ids = expert_ids.reshape(-1)
    one_hot = (flat_ids[:, None] == jnp.arange(experts, dtype=jnp.int32)[None, :]).astype(jnp.int32)
    before = jnp.cumsum(one_hot, axis=0) - one_hot
    slot_rank = jnp.sum(before * one_hot, axis=1)
    slot_index = flat_ids * capacity + slot_rank
    source = (
        jnp.full((experts * capacity,), -1, jnp.int32)
        .at[slot_index]
        .set(jnp.arange(tokens_here * choices, dtype=jnp.int32))
    )
    filled = source >= 0
    safe_row = jnp.where(filled, source, 0)
    token_row = safe_row // choices
    send_rows = jnp.where(
        filled[:, None], layer_in[token_row], jnp.zeros((), layer_in.dtype)
    ).reshape(experts, capacity, model_width)
    send_grad = jnp.where(
        filled[:, None], grad_out[token_row], jnp.zeros((), grad_out.dtype)
    ).reshape(experts, capacity, model_width)
    send_prob = jnp.where(
        filled, gate_probs.reshape(-1)[safe_row], jnp.zeros((), gate_probs.dtype)
    ).reshape(experts, capacity)
    rows_in, rows_grad, rows_prob = (
        lax.all_to_all(send_rows, "expert", split_axis=0, concat_axis=0, tiled=True),
        lax.all_to_all(send_grad, "expert", split_axis=0, concat_axis=0, tiled=True),
        lax.all_to_all(send_prob, "expert", split_axis=0, concat_axis=0, tiled=True),
    )
    returned, prob_grad, hidden, gate_up_grad, scaled = slot_work(
        rows_in, rows_grad, rows_prob, weights
    )
    back_rows, back_prob = (
        lax.all_to_all(returned, "expert", split_axis=0, concat_axis=0, tiled=True),
        lax.all_to_all(prob_grad, "expert", split_axis=0, concat_axis=0, tiled=True),
    )
    flat_in = rows_in.reshape(-1, model_width)
    flat_hidden = hidden.reshape(-1, hidden_width)
    flat_gate_up = gate_up_grad.reshape(-1, 2 * hidden_width)
    flat_scaled = scaled.reshape(-1, model_width)
    gate_share = model_width // lax.axis_size("group")
    down_share = hidden_width // lax.axis_size("group")
    columns = flat_in
    gate_up_sum = lax.psum_scatter(
        lax.dot_general(
            columns, flat_gate_up, (((0,), (0,)), ((), ())), preferred_element_type=jnp.float32
        ).astype(jnp.bfloat16),
        "group",
        scatter_dimension=0,
        tiled=True,
    ).astype(jnp.float32)
    columns = flat_hidden
    down_sum = lax.psum_scatter(
        lax.dot_general(
            columns, flat_scaled, (((0,), (0,)), ((), ())), preferred_element_type=jnp.float32
        ).astype(jnp.bfloat16),
        "group",
        scatter_dimension=0,
        tiled=True,
    ).astype(jnp.float32)
    flat_back = back_rows.reshape(experts * capacity, model_width)
    picked = flat_back[slot_index].reshape(tokens_here, choices, model_width)
    grad_in = jnp.sum(picked.astype(jnp.float32), axis=1).astype(jnp.bfloat16)
    grad_probs = back_prob.reshape(-1)[slot_index].reshape(tokens_here, choices)
    grad_gate = gate_up_sum[:, :hidden_width].reshape(1, gate_share, hidden_width)
    grad_up = gate_up_sum[:, hidden_width:].reshape(1, gate_share, hidden_width)
    grad_down = down_sum.reshape(1, down_share, model_width)
    return (grad_in, grad_probs, grad_gate, grad_up, grad_down)


def solution(mesh):
    in_specs = (
        P(("group", "expert"), None),
        P(("group", "expert"), None),
        P(("group", "expert"), None),
        P(("group", "expert"), None),
        P("expert", None, None),
        P("expert", None, None),
        P("expert", None, None),
    )
    out_specs = (
        P(("group", "expert"), None),
        P(("group", "expert"), None),
        P("expert", "group", None),
        P("expert", "group", None),
        P("expert", "group", None),
    )
    return jax.shard_map(
        per_device, mesh=mesh, in_specs=in_specs, out_specs=out_specs, check_vma=False
    )
```

profile of v0, /device:TPU:6, one launch (start us, length us, event | category | flops | bytes accessed | tf_op | source)
XLA Modules:
  0.0 353.4 jit_solution(10618872645668020162)
XLA Ops:
  7.2 0.9 copy.19
  8.3 0.7 broadcast_multiply_fusion
  9.0 0.6 reduce-window.6
  9.6 0.2 slice_reduce_fusion
  10.1 1.4 scatter_custom_fusion
  11.5 0.8 copy.22
  12.4 2.7 gather_fusion
  15.1 0.8 all_to_all.25
  15.9 18.7 %all-to-all-start = ((bf16[64,1,6]{2,1,0:T(2,128)(2,1)}), bf16[64,1,6]{2,1,0:T(2,128)(2,1)S(1)}, u32[]{:S(2)}, u32[]{:S(2)}) async-start(bf16[64,1,6]{2,1,0:T(2,128)(2,1)} %all_to_all.25), calls=%async_computation | async-start | bytes 65536 | tf_op jit(solution)/shard_map/all_to_all | solution.py:79
  34.7 0.1 broadcast_in_dim.44
  34.8 2.8 gather_fusion.1
  37.6 2.2 gather.21
  39.9 2.8 gather_fusion.2
  42.7 3.1 gather.23
  45.8 3.4 broadcast_select_fusion.1
  49.2 92.3 %all_to_all.31 = bf16[64,6,1536]{2,1,0:T(8,128)(2,1)S(1)} all-to-all(bf16[64,6,1536]{2,1,0:T(8,128)(2,1)} %get-tuple-element.22), channel_id=1, replica_groups=mesh['group'=8,'expert'=64] {'expert'}, dimensions={0} | all-to-all | bytes 2359296 | tf_op jit(solution)/shard_map/all_to_all | solution.py:78
  141.5 6.1 %all-to-all-start.2 = ((bf16[64,6,1536]{2,1,0:T(8,128)(2,1)}), bf16[64,6,1536]{2,1,0:T(8,128)(2,1)}, u32[]{:S(2)}, u32[]{:S(2)}) async-start(bf16[64,6,1536]{2,1,0:T(8,128)(2,1)} %get-tuple-element.23), calls=%async_computation.2 | async-start | bytes 3145728 | tf_op jit(solution)/shard_map/all_to_all | solution.py:77
  147.5 0.2 reduce-scatter.5.cloned.1.call-start
  148.1 1.5 multiply_convert_fusion
  149.6 2.4 convert_element_type.85
  152.0 1.6 fusion.10
  153.6 70.7 %all-to-all-done.2 = bf16[64,6,1536]{2,1,0:T(8,128)(2,1)} async-done(((bf16[64,6,1536]{2,1,0:T(8,128)(2,1)}), bf16[64,6,1536]{2,1,0:T(8,128)(2,1)}, u32[]{:S(2)}, u32[]{:S(2)}) %all-to-all-start.2) | async-done | bytes 1179680 | tf_op jit(solution)/shard_map/all_to_all | solution.py:77
  224.3 2.3 reshape.147
  226.7 0.8 fusion.4
  227.5 0.2 copy-done.6
  227.7 0.5 copy-done.10
  228.1 1.9 multiply_convert_fusion.3
  230.0 2.3 reshape.158
  232.3 2.8 convolution_convert_fusion.1
  235.1 2.3 fusion.1
  237.4 0.8 convert_element_type.103
  238.2 5.8 %all-to-all-start.4 = ((bf16[64,1,6]{2,1,0:T(2,128)(2,1)}), bf16[64,1,6]{2,1,0:T(2,128)(2,1)S(1)}, u32[]{:S(2)}, u32[]{:S(2)}) async-start(bf16[64,1,6]{2,1,0:T(2,128)(2,1)} %convert_element_type.103), calls=%async_computation.4 | async-start | bytes 65536 | tf_op jit(solution)/shard_map/all_to_all | solution.py:86
  244.0 2.2 fusion.2
  246.3 0.8 fusion
  247.1 1.4 reshape.148
  248.5 10.1 %all-to-all-done.4 = bf16[64,1,6]{2,1,0:T(2,128)(2,1)S(1)} async-done(((bf16[64,1,6]{2,1,0:T(2,128)(2,1)}), bf16[64,1,6]{2,1,0:T(2,128)(2,1)S(1)}, u32[]{:S(2)}, u32[]{:S(2)}) %all-to-all-start.4) | async-done | bytes 800 | tf_op jit(solution)/shard_map/all_to_all | solution.py:86
  258.6 5.5 %all-to-all-start.3 = ((bf16[64,6,1536]{2,1,0:T(8,128)(2,1)}), bf16[64,6,1536]{2,1,0:T(8,128)(2,1)}, u32[]{:S(2)}, u32[]{:S(2)}) async-start(bf16[64,6,1536]{2,1,0:T(8,128)(2,1)} %reshape.148), calls=%async_computation.3 | async-start | bytes 3145728 | tf_op jit(solution)/shard_map/all_to_all | solution.py:85
  264.1 0.3 reduce-scatter.3.cloned.1.call-start
  264.4 2.8 convolution_convert_fusion
  267.5 1.9 gather_fusion.4
  269.5 0.7 copy.25
  270.2 1.6 bitcast_convert_fusion
  271.9 68.1 %all-to-all-done.3 = bf16[64,6,1536]{2,1,0:T(8,128)(2,1)} async-done(((bf16[64,6,1536]{2,1,0:T(8,128)(2,1)}), bf16[64,6,1536]{2,1,0:T(8,128)(2,1)}, u32[]{:S(2)}, u32[]{:S(2)}) %all-to-all-start.3) | async-done | bytes 1179680 | tf_op jit(solution)/shard_map/all_to_all | solution.py:85
  339.9 2.3 reshape.149
  342.2 1.3 gather_fusion.3
  343.5 1.2 bitcast_reduce_fusion
  344.7 1.0 convert_element_type.95
  345.7 0.9 slice_bitcast_fusion
  (48 shorter events, 1.3 us)
Async XLA Ops:
  7.2 220.5 %copy-start = (bf16[1,1536,384]{2,1,0:T(8,128)(2,1)S(1)}, bf16[1,1536,384]{2,1,0:T(8,128)(2,1)}, u32[]{:S(2)}) copy-start(bf16[1,1536,384]{2,1,0:T(8,128)(2,1)} %param.12) | copy-start | bytes 3538948
  7.2 27.6 %copy-start.1 = (bf16[32,1536]{1,0:T(8,128)(2,1)S(1)}, bf16[32,1536]{1,0:T(8,128)(2,1)}, u32[]{:S(2)}) copy-start(bf16[32,1536]{1,0:T(8,128)(2,1)} %param.8) | copy-start | bytes 294916
  15.9 33.3 %all-to-all-start = ((bf16[64,1,6]{2,1,0:T(2,128)(2,1)}), bf16[64,1,6]{2,1,0:T(2,128)(2,1)S(1)}, u32[]{:S(2)}, u32[]{:S(2)}) async-start(bf16[64,1,6]{2,1,0:T(2,128)(2,1)} %all_to_all.25), calls=%async_computation | async-start | bytes 65536 | tf_op jit(solution)/shard_map/all_to_all | solution.py:79
  37.6 2.2 copy-start.2
  141.5 6.6 %copy-start.3 = (bf16[64,6,1536]{2,1,0:T(8,128)(2,1)}, bf16[64,6,1536]{2,1,0:T(8,128)(2,1)S(1)}, u32[]{:S(2)}) copy-start(bf16[64,6,1536]{2,1,0:T(8,128)(2,1)S(1)} %all_to_all.31) | copy-start | bytes 3538948
  141.5 82.9 %all-to-all-start.2 = ((bf16[64,6,1536]{2,1,0:T(8,128)(2,1)}), bf16[64,6,1536]{2,1,0:T(8,128)(2,1)}, u32[]{:S(2)}, u32[]{:S(2)}) async-start(bf16[64,6,1536]{2,1,0:T(8,128)(2,1)} %get-tuple-element.23), calls=%async_computation.2 | async-start | bytes 3145728 | tf_op jit(solution)/shard_map/all_to_all | solution.py:77
  147.5 122.7 %reduce-scatter.5.cloned.1.call-start = ((), (), s32[]{:S(2)}) async-start(), calls=%async_computation.8 | async-start | bytes 1327104 | tf_op jit(solution)/shard_map/reduce_scatter | solution.py:104
  149.6 2.4 copy-start.4
  153.6 73.0 %copy-start.5 = (bf16[1,1536,384]{2,1,0:T(8,128)(2,1)S(1)}, bf16[1,1536,384]{2,1,0:T(8,128)(2,1)}, u32[]{:S(2)}) copy-start(bf16[1,1536,384]{2,1,0:T(8,128)(2,1)} %param.11) | copy-start | bytes 3538948
  226.6 1.0 copy-start.6
  226.7 1.5 copy-start.10
  238.2 20.4 %all-to-all-start.4 = ((bf16[64,1,6]{2,1,0:T(2,128)(2,1)}), bf16[64,1,6]{2,1,0:T(2,128)(2,1)S(1)}, u32[]{:S(2)}, u32[]{:S(2)}) async-start(bf16[64,1,6]{2,1,0:T(2,128)(2,1)} %convert_element_type.103), calls=%async_computation.4 | async-start | bytes 65536 | tf_op jit(solution)/shard_map/all_to_all | solution.py:86
  244.0 2.2 copy-start.8
  248.5 15.9 %copy-start.7 = (bf16[384,1536]{1,0:T(8,128)(2,1)S(1)}, bf16[384,1536]{1,0:T(8,128)(2,1)}, u32[]{:S(2)}) copy-start(bf16[384,1536]{1,0:T(8,128)(2,1)} %copy-done.6) | copy-start | bytes 3538948
  248.5 15.9 %copy-start.9 = (bf16[384,384]{0,1:T(8,128)(2,1)S(1)}, bf16[384,384]{0,1:T(8,128)(2,1)}, u32[]{:S(2)}) copy-start(bf16[384,384]{0,1:T(8,128)(2,1)} %get-tuple-element.18) | copy-start | bytes 884740
  258.6 81.4 %all-to-all-start.3 = ((bf16[64,6,1536]{2,1,0:T(8,128)(2,1)}), bf16[64,6,1536]{2,1,0:T(8,128)(2,1)}, u32[]{:S(2)}, u32[]{:S(2)}) async-start(bf16[64,6,1536]{2,1,0:T(8,128)(2,1)} %reshape.148), calls=%async_computation.3 | async-start | bytes 3145728 | tf_op jit(solution)/shard_map/all_to_all | solution.py:85
  264.1 80.6 %reduce-scatter.3.cloned.1.call-start = ((), (), s32[]{:S(2)}) async-start(), calls=%async_computation.7 | async-start | bytes 2654208 | tf_op jit(solution)/shard_map/reduce_scatter | solution.py:95
Sparse Core Ops, SparseCore 0:
  235.3 28.4 reduce-scatter.4
  267.8 40.0 reduce-scatter.2
where the time goes:
time: 354 us; the launch traced here: 353 us
  waiting for transfers between devices  149 us (42%)
  blocking collectives  92.3 us (26%)
  starting transfers between devices  36.6 us (10%)
  local copies, waits for them, and re-layouts  35.4 us (10%)
  matrix products  15.3 us (4%)
  between operations  14.4 us (4%)
  other arithmetic  10.5 us (3%)
    all_to_all x1, blocking collectives, per_device(): lax.all_to_all(send_grad, 'expert', split_axis=0, concat_axis=0, tiled=True)  92.3 us
    all_to_all x1, waiting for transfers between devices, per_device(): lax.all_to_all(send_rows, 'expert', split_axis=0, concat_axis=0, tiled=True)  70.7 us
    all_to_all x1, waiting for transfers between devices, per_device(): lax.all_to_all(returned, 'expert', split_axis=0, concat_axis=0, tiled=True)  68.1 us
    all_to_all x1, starting transfers between devices, per_device(): lax.all_to_all(send_prob, 'expert', split_axis=0, concat_axis=0, tiled=True)  18.7 us
    all_to_all x1, waiting for transfers between devices, per_device(): lax.all_to_all(prob_grad, 'expert', split_axis=0, concat_axis=0, tiled=True)  10.1 us
  transfers between devices with their start and end apart: 6, of which 3 were waited for; matrix products, arithmetic and copies ran while one was open for 11% of the time, Pallas kernels for 0%

commit v1 on v0

v1 whole, which is shorter than its diff:
```python
import functools

import jax
import jax.numpy as jnp
from jax import lax
from jax.experimental import pallas as pl
from jax.experimental.pallas import tpu as pltpu
from jax.sharding import Mesh, PartitionSpec as P

F32 = jnp.float32
BF16 = jnp.bfloat16
LANES = 128
CAP = 6
FAR = 4
NEAR = 16
TOP = 8
MIB = 1 << 20


def iota(shape, dim):
    return lax.broadcasted_iota(jnp.int32, shape, dim)


def dot(a, b, contract=((1,), (0,))):
    return lax.dot_general(a, b, (contract, ((), ())), preferred_element_type=F32)


def whole(n):
    return [pl.BlockSpec(memory_space=pltpu.VMEM)] * n


def slot_parts(i):
    sixth = lax.shift_right_logical(i * 10923, 16)
    expert = lax.shift_right_logical(i * 2731, 16)
    return expert, sixth - FAR * expert, i - CAP * sixth


def select_kernel(base_ref, tok_ref, send_ref, pick_ref):
    tokens = tok_ref.shape[0]
    slots = send_ref.shape[0]
    width = send_ref.shape[1] // 2
    block = tokens // FAR
    extras = tok_ref[:, 2 * width :].astype(F32)
    lane = iota((tokens, LANES), 1)
    expert_lane = jnp.where(lane < NEAR, lane + base_ref[0], -1).astype(F32)
    member = jnp.zeros((tokens, LANES), F32)
    prob = jnp.zeros((tokens, LANES), F32)
    for k in range(TOP):
        hit = extras[:, k : k + 1] == expert_lane
        member = jnp.where(hit, 1.0, member)
        prob = jnp.where(hit, extras[:, TOP + k : TOP + k + 1], prob)
    row, col = iota((tokens, tokens), 0), iota((tokens, tokens), 1)
    shift = block.bit_length() - 1
    same = lax.shift_right_logical(row, shift) == lax.shift_right_logical(col, shift)
    earlier = jnp.where(same & (col < row), 1.0, 0.0).astype(BF16)
    rank = dot(earlier, member.astype(BF16))
    code = jnp.where(member > 0.0, rank, -1.0).astype(BF16)
    eye = jnp.where(row == col, 1.0, 0.0).astype(BF16)
    code_t = dot(code, eye, ((0,), (0,))).astype(BF16)
    prob_t = dot(prob.astype(BF16), eye, ((0,), (0,))).astype(BF16)

    expert, home, place = slot_parts(iota((slots, LANES), 0))
    spread = jnp.where(iota((slots, LANES), 1) == expert, 1.0, 0.0).astype(BF16)
    code_row = dot(spread, code_t)
    token_block = lax.shift_right_logical(iota((slots, tokens), 1), shift)
    chosen = (code_row == place.astype(F32)) & (token_block == home)
    select = jnp.where(chosen, 1.0, 0.0).astype(BF16)
    prob_row = jnp.sum(jnp.where(chosen, dot(spread, prob_t), 0.0), axis=1, keepdims=True)
    send_ref[:, :width] = dot(select, tok_ref[:, :width]).astype(BF16)
    grads = dot(select, tok_ref[:, width : 2 * width])
    send_ref[:, width:] = (prob_row * grads).astype(BF16)

    expert, home, place = slot_parts(iota((LANES, slots), 1))
    spread = jnp.where(iota((LANES, slots), 0) == expert, 1.0, 0.0).astype(BF16)
    code_col = dot(code, spread)
    token_block = lax.shift_right_logical(iota((tokens, slots), 0), shift)
    chosen = (code_col == place.astype(F32)) & (token_block == home)
    pick_ref[...] = jnp.where(chosen, 1.0, 0.0).astype(BF16)


def expert_kernel(rows_ref, gate_ref, up_ref, down_ref, ret_ref, part_ref):
    width, hidden_width = gate_ref.shape
    groups = part_ref.shape[0]
    share = width // groups
    down_share = hidden_width // groups
    rows = rows_ref[:, :width]
    scaled = rows_ref[:, width:]
    gate, up, down = gate_ref[...], up_ref[...], down_ref[...]
    pre_gate = dot(rows, gate)
    pre_up = dot(rows, up)
    grad_hidden = dot(scaled, down, ((1,), (1,)))
    sig = jax.nn.sigmoid(pre_gate)
    silu = pre_gate * sig
    hidden = (silu * pre_up).astype(BF16)
    prob_grad = jnp.sum(hidden.astype(F32) * grad_hidden, axis=1, keepdims=True)
    gate_grad = (grad_hidden * pre_up * sig * (1.0 + pre_gate * (1.0 - sig))).astype(BF16)
    up_grad = (grad_hidden * silu).astype(BF16)
    back = dot(gate_grad, gate, ((1,), (1,))) + dot(up_grad, up, ((1,), (1,)))
    ret_ref[:, :width] = back.astype(BF16)
    ret_ref[:, width:] = jnp.broadcast_to(prob_grad, (rows.shape[0], LANES)).astype(BF16)
    both = jnp.concatenate([gate_grad, up_grad], axis=1)
    for pair in range(groups // 2):
        columns = rows_ref[:, pair * 2 * share : (pair + 1) * 2 * share]
        part = dot(columns, both, ((0,), (0,))).astype(BF16)
        part_ref[2 * pair, :share, :] = part[:share]
        part_ref[2 * pair + 1, :share, :] = part[share:]
    half = width // 2
    for side in range(2):
        part = dot(hidden, scaled[:, side * half : (side + 1) * half], ((0,), (0,))).astype(BF16)
        for g in range(groups):
            low = share + side * down_share
            part_ref[g, low : low + down_share, :] = part[g * down_share : (g + 1) * down_share]


def combine_kernel(base_ref, back_ref, pick_ref, extra_ref, sum_ref):
    slots = back_ref.shape[0]
    width = back_ref.shape[1] - LANES
    tokens = sum_ref.shape[0]
    pick = pick_ref[...]
    sum_ref[:, :width] = dot(pick, back_ref[:, :width]).astype(BF16)
    expert, _, _ = slot_parts(iota((slots, LANES), 0))
    own = iota((slots, LANES), 1) == expert
    spread = jnp.where(own, back_ref[:, width:].astype(F32), 0.0).astype(BF16)
    by_expert = dot(pick, spread)
    extras = extra_ref[...].astype(F32)
    lane = iota((tokens, LANES), 1)
    expert_lane = jnp.where(lane < NEAR, lane + base_ref[0], -1).astype(F32)
    result = jnp.zeros((tokens, LANES), F32)
    for k in range(TOP):
        hit = extras[:, k : k + 1] == expert_lane
        value = jnp.sum(jnp.where(hit, by_expert, 0.0), axis=1, keepdims=True)
        value = value / extras[:, TOP + k : TOP + k + 1]
        result = jnp.where(lane == k, value, result)
    sum_ref[:, width:] = result.astype(BF16)


def finish_kernel(sums_ref, part_ref, in_ref, prob_ref, gate_ref, up_ref, down_ref):
    width = in_ref.shape[1]
    total = sums_ref[0].astype(F32)
    for s in range(1, FAR):
        total = total + sums_ref[s].astype(F32)
    in_ref[...] = total[:, :width].astype(BF16)
    prob_ref[...] = total[:, width : width + TOP].astype(BF16)
    share, hidden_width = gate_ref.shape
    down_share = down_ref.shape[0]
    gate_ref[...] = part_ref[:share, :hidden_width].astype(F32)
    up_ref[...] = part_ref[:share, hidden_width:].astype(F32)
    half = width // 2
    down_ref[:, :half] = part_ref[share : share + down_share, :].astype(F32)
    down_ref[:, half:] = part_ref[share + down_share :, :].astype(F32)


def params(mib):
    return pltpu.CompilerParams(vmem_limit_bytes=mib * MIB)


def per_device(layer_in, grad_out, expert_ids, gate_probs, gate_weight, up_weight, down_weight):
    block, width = layer_in.shape
    hidden_width = gate_weight.shape[2]
    groups = lax.axis_size("group")
    tokens = FAR * block
    slots = NEAR * FAR * CAP
    share = width // groups
    down_share = hidden_width // groups
    part_rows = share + 2 * down_share
    base = (lax.axis_index("far") * NEAR).astype(jnp.int32).reshape(1)
    scalar = pl.BlockSpec(memory_space=pltpu.SMEM)

    extras = jnp.concatenate([expert_ids.astype(BF16), gate_probs], axis=1)
    extras = jnp.pad(extras, ((0, 0), (0, LANES - 2 * TOP)))
    packed = jnp.concatenate([layer_in, grad_out, extras], axis=1)
    near_tokens = lax.all_gather(packed, "far", tiled=True)

    send, pick = pl.pallas_call(
        select_kernel,
        out_shape=(
            jax.ShapeDtypeStruct((slots, 2 * width), BF16),
            jax.ShapeDtypeStruct((tokens, slots), BF16),
        ),
        in_specs=[scalar] + whole(1),
        out_specs=tuple(whole(2)),
        compiler_params=params(24),
        name="select_rows",
    )(base, near_tokens)

    near = ("near", "y")
    exchange = functools.partial(lax.all_to_all, split_axis=0, concat_axis=0, tiled=True)
    rows = exchange(send.reshape(NEAR, FAR * CAP, 2 * width), near).reshape(slots, 2 * width)

    back, parts = pl.pallas_call(
        expert_kernel,
        out_shape=(
            jax.ShapeDtypeStruct((slots, width + LANES), BF16),
            jax.ShapeDtypeStruct((groups, part_rows, 2 * hidden_width), BF16),
        ),
        in_specs=whole(4),
        out_specs=tuple(whole(2)),
        compiler_params=params(40),
        name="expert_rows",
    )(rows, gate_weight[0], up_weight[0], down_weight[0])

    part_sum = lax.psum_scatter(
        parts.reshape(groups * part_rows, 2 * hidden_width), "group", scatter_dimension=0, tiled=True
    )
    back = exchange(back.reshape(NEAR, FAR * CAP, width + LANES), near).reshape(slots, width + LANES)

    sums = pl.pallas_call(
        combine_kernel,
        out_shape=jax.ShapeDtypeStruct((tokens, width + LANES), BF16),
        in_specs=[scalar] + whole(3),
        out_specs=whole(1)[0],
        compiler_params=params(24),
        name="combine_rows",
    )(base, back, pick, near_tokens[:, 2 * width :])
    sums = exchange(sums.reshape(FAR, block, width + LANES), "far")

    grad_in, grad_probs, grad_gate, grad_up, grad_down = pl.pallas_call(
        finish_kernel,
        out_shape=(
            jax.ShapeDtypeStruct((block, width), BF16),
            jax.ShapeDtypeStruct((block, TOP), BF16),
            jax.ShapeDtypeStruct((share, hidden_width), F32),
            jax.ShapeDtypeStruct((share, hidden_width), F32),
            jax.ShapeDtypeStruct((down_share, width), F32),
        ),
        in_specs=whole(2),
        out_specs=tuple(whole(5)),
        compiler_params=params(24),
        name="finish",
    )(sums, part_sum)
    return grad_in, grad_probs, grad_gate[None], grad_up[None], grad_down[None]


def solution(mesh):
    groups, experts = mesh.devices.shape
    split = Mesh(mesh.devices.reshape(groups, FAR, 4, experts // NEAR), ("group", "far", "near", "y"))
    everywhere = ("group", "far", "near", "y")
    expert = ("far", "near", "y")
    token_spec = P(everywhere, None)
    weight_spec = P(expert, None, None)
    grad_spec = P(expert, "group", None)
    return jax.shard_map(
        per_device,
        mesh=split,
        in_specs=(token_spec,) * 4 + (weight_spec,) * 3,
        out_specs=(token_spec,) * 2 + (grad_spec,) * 3,
        check_vma=False,
    )
```

time: 354 us -> 197 us (0.56)
  the two profiles are of different devices: /device:TPU:6 before, /device:TPU:52 now
where the time goes in v1:
time: 197 us
  blocking collectives  133 us (68%)
  waiting for transfers between devices  28.8 us (15%)
  between operations  14.1 us (7%)
  Pallas kernels  10.3 us (5%)
  starting transfers between devices  6.49 us (3%)
  local copies, waits for them, and re-layouts  2.55 us (1%)
    all_to_all x1, blocking collectives, per_device(): exchange(send.reshape(NEAR, FAR * CAP, 2 * width), near)  63 us
    all_gather x1, blocking collectives, per_device(): near_tokens = lax.all_gather(packed, 'far', tiled=True)  37.6 us
    all_to_all x1, blocking collectives, per_device(): sums = exchange(sums.reshape(FAR, block, width + LANES), 'far')  32.3 us
    all_to_all x1, waiting for transfers between devices, per_device(): exchange(back.reshape(NEAR, FAR * CAP, width + LANES), near)  28.8 us
    pallas_call x1, Pallas kernels, per_device(): pl.pallas_call(expert_kernel, out_shape=(jax.ShapeDtypeStruct((slots, wid...  6.98 us
    all_to_all x1, starting transfers between devices, per_device(): exchange(back.reshape(NEAR, FAR * CAP, width + LANES), near)  6.45 us
  transfers between devices with their start and end apart: 2, of which 1 were waited for; matrix products, arithmetic and copies ran while one was open for 0% of the time, Pallas kernels for 0%

profile of v1, /device:TPU:52, one launch (start us, length us, event | category | flops | bytes accessed | tf_op | source)
XLA Modules:
  0.0 196.9 jit_solution(5575810997839454174)
XLA Ops:
  7.2 0.0 reduce-scatter.2.cloned.1.call-start
  7.2 0.7 convert_element_type.5
  7.9 0.1 copy.15
  8.0 0.8 copy.16
  8.8 0.1 fusion.2
  8.8 1.0 pad_maximum_fusion
  9.8 37.6 %all_gather.3.tok_ref = bf16[128,3200]{1,0:T(8,128)(2,1)S(1)} all-gather(bf16[32,3200]{1,0:T(8,128)(2,1)S(1)} %pad_maximum_fusion), channel_id=1, replica_groups=mesh['group'=8,'far'=4,'near'=4,'y'=4] {'far'}, dimensions={0}, use_global_device_ids=true | all-gather | bytes 1024000 | tf_op jit(solution)/shard_map/all_gather | solution.py:172
  47.4 1.5 select_rows.1
  48.9 0.0 copy-start
  48.9 0.0 copy-start.1
  48.9 0.0 copy-start.2
  48.9 63.0 %all_to_all.15 = bf16[16,24,3072]{2,1,0:T(8,128)(2,1)S(1)} all-to-all(bf16[16,24,3072]{2,1,0:T(8,128)(2,1)S(1)} %bitcast.15), channel_id=1, replica_groups=mesh['group'=8,'far'=4,'near'=4,'y'=4] {'near','y'}, dimensions={0} | all-to-all | bytes 4718592 | tf_op jit(solution)/shard_map/all_to_all | solution.py:188
  112.0 0.0 copy-done
  112.0 0.0 copy-done.1
  112.0 0.0 copy-done.2
  112.0 7.0 %expert_rows.1 = (bf16[384,1664]{1,0:T(8,128)(2,1)}, bf16[8,288,768]{2,1,0:T(8,128)(2,1)}) custom-call(bf16[384,3072]{1,0:T(8,128)(2,1)S(1)} %bitcast.13, bf16[1536,384]{1,0:T(8,128)(2,1)S(1)} %bitcast.17, bf16[1536,384]{1,0:T(8,128)(2,1)S(1)} %bitcast.18, bf16[384,1536]{1,0:T(8,128)(2,1)S(1)} %bitcast.19), custom_call_target="tpu_custom_call" | custom-call | tf_op jit(solution)/shard_map/expert_rows/pallas_call | solution.py:190
  119.0 0.0 reduce-scatter.2.cloned.1.call-update
  119.0 6.4 %all-to-all-start.1 = ((bf16[16,24,1664]{2,1,0:T(8,128)(2,1)}), bf16[16,24,1664]{2,1,0:T(8,128)(2,1)S(1)}, u32[]{:S(2)}, u32[]{:S(2)}) async-start(bf16[16,24,1664]{2,1,0:T(8,128)(2,1)} %bitcast.6), calls=%async_computation.1 | async-start | bytes 2555904 | tf_op jit(solution)/shard_map/all_to_all | solution.py:205
  125.4 28.8 %all-to-all-done.1 = bf16[16,24,1664]{2,1,0:T(8,128)(2,1)S(1)} async-done(((bf16[16,24,1664]{2,1,0:T(8,128)(2,1)}), bf16[16,24,1664]{2,1,0:T(8,128)(2,1)S(1)}, u32[]{:S(2)}, u32[]{:S(2)}) %all-to-all-start.1) | async-done | bytes 1277984 | tf_op jit(solution)/shard_map/all_to_all | solution.py:205
  154.2 0.9 combine_rows.1
  155.1 32.3 %all_to_all.16.sums_ref = bf16[4,32,1664]{2,1,0:T(8,128)(2,1)S(1)} all-to-all(bf16[4,32,1664]{2,1,0:T(8,128)(2,1)S(1)} %bitcast.16), channel_id=1, replica_groups=mesh['group'=8,'far'=4,'near'=4,'y'=4] {'far'}, dimensions={0} | all-to-all | bytes 851968 | tf_op jit(solution)/shard_map/all_to_all | solution.py:215
  187.4 0.0 reduce-scatter.2.cloned.1.call-done.part_ref
  187.4 0.0 copy-start.3
  187.4 1.0 copy-done.3
  188.4 1.0 finish.1
  189.4 0.7 copy.17
  (1 shorter events, 0.0 us)
Async XLA Ops:
  7.2 180.2 %reduce-scatter.2.cloned.1.call-start = ((), (), s32[]{:S(2)}) async-start(), calls=%async_computation.4 | async-start | bytes 3981312 | tf_op jit(solution)/shard_map/reduce_scatter | solution.py:202
  48.9 63.1 %copy-start = (bf16[1,1536,384]{2,1,0:T(8,128)(2,1)S(1)}, bf16[1,1536,384]{2,1,0:T(8,128)(2,1)}, u32[]{:S(2)}) copy-start(bf16[1,1536,384]{2,1,0:T(8,128)(2,1)} %param.11) | copy-start | bytes 3538948
  48.9 63.1 %copy-start.1 = (bf16[1,1536,384]{2,1,0:T(8,128)(2,1)S(1)}, bf16[1,1536,384]{2,1,0:T(8,128)(2,1)}, u32[]{:S(2)}) copy-start(bf16[1,1536,384]{2,1,0:T(8,128)(2,1)} %param.12) | copy-start | bytes 3538948
  48.9 63.1 %copy-start.2 = (bf16[1,384,1536]{2,1,0:T(8,128)(2,1)S(1)}, bf16[1,384,1536]{2,1,0:T(8,128)(2,1)}, u32[]{:S(2)}) copy-start(bf16[1,384,1536]{2,1,0:T(8,128)(2,1)} %param.13) | copy-start | bytes 3538948
  119.0 35.2 %all-to-all-start.1 = ((bf16[16,24,1664]{2,1,0:T(8,128)(2,1)}), bf16[16,24,1664]{2,1,0:T(8,128)(2,1)S(1)}, u32[]{:S(2)}, u32[]{:S(2)}) async-start(bf16[16,24,1664]{2,1,0:T(8,128)(2,1)} %bitcast.6), calls=%async_computation.1 | async-start | bytes 2555904 | tf_op jit(solution)/shard_map/all_to_all | solution.py:205
  187.4 1.0 copy-start.3
Sparse Core Ops, SparseCore 0:
  119.1 35.9 reduce-scatter.1

commit v2 on v1

--- a/solution.py
+++ b/solution.py
@@ -14,6 +14,7 @@
 FAR = 4
 NEAR = 16
 TOP = 8
+EXPERTS = 64
 MIB = 1 << 20
 
 
@@ -33,6 +34,19 @@
     sixth = lax.shift_right_logical(i * 10923, 16)
     expert = lax.shift_right_logical(i * 2731, 16)
     return expert, sixth - FAR * expert, i - CAP * sixth
+
+
+def served(lane, base):
+    return jnp.where(lane < NEAR, (lane + base) & (EXPERTS - 1), -1).astype(F32)
+
+
+def windows(groups, experts):
+    lists = []
+    for g in range(groups):
+        for far in range(FAR):
+            start = far * NEAR + (g % 2) * (NEAR // 2)
+            lists.append([g * experts + (start + j) % experts for j in range(NEAR)])
+    return lists
 
 
 def select_kernel(base_ref, tok_ref, send_ref, pick_ref):
@@ -42,7 +56,7 @@
     block = tokens // FAR
     extras = tok_ref[:, 2 * width :].astype(F32)
     lane = iota((tokens, LANES), 1)
-    expert_lane = jnp.where(lane < NEAR, lane + base_ref[0], -1).astype(F32)
+    expert_lane = served(lane, base_ref[0])
     member = jnp.zeros((tokens, LANES), F32)
     prob = jnp.zeros((tokens, LANES), F32)
     for k in range(TOP):
@@ -124,7 +138,7 @@
     by_expert = dot(pick, spread)
     extras = extra_ref[...].astype(F32)
     lane = iota((tokens, LANES), 1)
-    expert_lane = jnp.where(lane < NEAR, lane + base_ref[0], -1).astype(F32)
+    expert_lane = served(lane, base_ref[0])
     result = jnp.zeros((tokens, LANES), F32)
     for k in range(TOP):
         hit = extras[:, k : k + 1] == expert_lane
@@ -163,7 +177,9 @@
     share = width // groups
     down_share = hidden_width // groups
     part_rows = share + 2 * down_share
-    base = (lax.axis_index("far") * NEAR).astype(jnp.int32).reshape(1)
+    moved = (lax.axis_index("group") & 1) * (NEAR // 2)
+    place = lax.axis_index(("far", "near", "y")) - moved + EXPERTS
+    base = (place // NEAR * NEAR + moved).astype(jnp.int32).reshape(1)
     scalar = pl.BlockSpec(memory_space=pltpu.SMEM)
 
     extras = jnp.concatenate([expert_ids.astype(BF16), gate_probs], axis=1)
@@ -183,9 +199,13 @@
         name="select_rows",
     )(base, near_tokens)
 
-    near = ("near", "y")
     exchange = functools.partial(lax.all_to_all, split_axis=0, concat_axis=0, tiled=True)
-    rows = exchange(send.reshape(NEAR, FAR * CAP, 2 * width), near).reshape(slots, 2 * width)
+    near_exchange = functools.partial(
+        exchange,
+        axis_name=("group", "far", "near", "y"),
+        axis_index_groups=windows(groups, EXPERTS),
+    )
+    rows = near_exchange(send.reshape(NEAR, FAR * CAP, 2 * width)).reshape(slots, 2 * width)
 
     back, parts = pl.pallas_call(
         expert_kernel,
@@ -202,7 +222,7 @@
     part_sum = lax.psum_scatter(
         parts.reshape(groups * part_rows, 2 * hidden_width), "group", scatter_dimension=0, tiled=True
     )
-    back = exchange(back.reshape(NEAR, FAR * CAP, width + LANES), near).reshape(slots, width + LANES)
+    back = near_exchange(back.reshape(NEAR, FAR * CAP, width + LANES)).reshape(slots, width + LANES)
 
     sums = pl.pallas_call(
         combine_kernel,

time: 197 us -> 184 us (0.934)
  the two profiles are of different devices: /device:TPU:52 before, /device:TPU:6 now
where the time goes in v2:
time: 184 us; the launch traced here: 183 us
  blocking collectives  122 us (66%)
  waiting for transfers between devices  26.3 us (14%)
  between operations  14.1 us (8%)
  Pallas kernels  10.3 us (6%)
  starting transfers between devices  6.07 us (3%)
  local copies, waits for them, and re-layouts  2.55 us (1%)
    all_to_all x1, blocking collectives, per_device(): near_exchange(send.reshape(NEAR, FAR * CAP, 2 * width))  46.3 us
    all_gather x1, blocking collectives, per_device(): near_tokens = lax.all_gather(packed, 'far', tiled=True)  44.3 us
    all_to_all x1, blocking collectives, per_device(): sums = exchange(sums.reshape(FAR, block, width + LANES), 'far')  31.8 us
    all_to_all x1, waiting for transfers between devices, per_device(): near_exchange(back.reshape(NEAR, FAR * CAP, width + LANES))  26.3 us
    pallas_call x1, Pallas kernels, per_device(): pl.pallas_call(expert_kernel, out_shape=(jax.ShapeDtypeStruct((slots, wid...  6.98 us
    all_to_all x1, starting transfers between devices, per_device(): near_exchange(back.reshape(NEAR, FAR * CAP, width + LANES))  6.03 us
  transfers between devices with their start and end apart: 2, of which 1 were waited for; matrix products, arithmetic and copies ran while one was open for 0% of the time, Pallas kernels for 0%

profile of v2, /device:TPU:6, one launch (start us, length us, event | category | flops | bytes accessed | tf_op | source)
XLA Modules:
  0.0 183.4 jit_solution(5716178527846217395)
XLA Ops:
  7.2 0.0 reduce-scatter.2.cloned.1.call-start
  7.2 0.7 convert_element_type.5
  7.9 0.1 copy.15
  8.0 0.8 copy.16
  8.8 0.1 fusion.2
  8.9 1.0 pad_maximum_fusion
  9.8 44.3 %all_gather.3.tok_ref = bf16[128,3200]{1,0:T(8,128)(2,1)S(1)} all-gather(bf16[32,3200]{1,0:T(8,128)(2,1)S(1)} %pad_maximum_fusion), channel_id=1, replica_groups=mesh['group'=8,'far'=4,'near'=4,'y'=4] {'far'}, dimensions={0}, use_global_device_ids=true | all-gather | bytes 1024000 | tf_op jit(solution)/shard_map/all_gather | solution.py:188
  54.1 1.5 select_rows.1
  55.5 0.0 copy-start
  55.6 0.0 copy-start.1
  55.6 0.0 copy-start.2
  55.6 46.3 %all_to_all.15 = bf16[16,24,3072]{2,1,0:T(8,128)(2,1)S(1)} all-to-all(bf16[16,24,3072]{2,1,0:T(8,128)(2,1)S(1)} %bitcast.15), channel_id=1, replica_groups={{0,1,2,3,4,5,6,7,8,9,10,11,12,13,14,15},{16,17,18,19,20,21,22,23,24,25,..., dimensions={0} | all-to-all | bytes 4718592 | tf_op jit(solution)/shard_map/all_to_all | solution.py:208
  101.9 0.0 copy-done
  101.9 0.0 copy-done.1
  101.9 0.0 copy-done.2
  101.9 7.0 %expert_rows.1 = (bf16[384,1664]{1,0:T(8,128)(2,1)}, bf16[8,288,768]{2,1,0:T(8,128)(2,1)}) custom-call(bf16[384,3072]{1,0:T(8,128)(2,1)S(1)} %bitcast.13, bf16[1536,384]{1,0:T(8,128)(2,1)S(1)} %bitcast.17, bf16[1536,384]{1,0:T(8,128)(2,1)S(1)} %bitcast.18, bf16[384,1536]{1,0:T(8,128)(2,1)S(1)} %bitcast.19), custom_call_target="tpu_custom_call" | custom-call | tf_op jit(solution)/shard_map/expert_rows/pallas_call | solution.py:210
  108.9 0.0 reduce-scatter.2.cloned.1.call-update
  108.9 6.0 %all-to-all-start.1 = ((bf16[16,24,1664]{2,1,0:T(8,128)(2,1)}), bf16[16,24,1664]{2,1,0:T(8,128)(2,1)S(1)}, u32[]{:S(2)}, u32[]{:S(2)}) async-start(bf16[16,24,1664]{2,1,0:T(8,128)(2,1)} %bitcast.6), calls=%async_computation.1 | async-start | bytes 2555904 | tf_op jit(solution)/shard_map/all_to_all | solution.py:225
  114.9 26.3 %all-to-all-done.1 = bf16[16,24,1664]{2,1,0:T(8,128)(2,1)S(1)} async-done(((bf16[16,24,1664]{2,1,0:T(8,128)(2,1)}), bf16[16,24,1664]{2,1,0:T(8,128)(2,1)S(1)}, u32[]{:S(2)}, u32[]{:S(2)}) %all-to-all-start.1) | async-done | bytes 1277984 | tf_op jit(solution)/shard_map/all_to_all | solution.py:225
  141.2 0.9 combine_rows.1
  142.1 31.8 %all_to_all.16.sums_ref = bf16[4,32,1664]{2,1,0:T(8,128)(2,1)S(1)} all-to-all(bf16[4,32,1664]{2,1,0:T(8,128)(2,1)S(1)} %bitcast.16), channel_id=1, replica_groups=mesh['group'=8,'far'=4,'near'=4,'y'=4] {'far'}, dimensions={0} | all-to-all | bytes 851968 | tf_op jit(solution)/shard_map/all_to_all | solution.py:235
  173.9 0.0 reduce-scatter.2.cloned.1.call-done.part_ref
  173.9 0.0 copy-start.3
  173.9 1.0 copy-done.3
  174.9 1.0 finish.1
  175.9 0.7 copy.17
  (1 shorter events, 0.0 us)
Async XLA Ops:
  7.2 166.7 %reduce-scatter.2.cloned.1.call-start = ((), (), s32[]{:S(2)}) async-start(), calls=%async_computation.4 | async-start | bytes 3981312 | tf_op jit(solution)/shard_map/reduce_scatter | solution.py:222
  55.5 46.3 %copy-start = (bf16[1,1536,384]{2,1,0:T(8,128)(2,1)S(1)}, bf16[1,1536,384]{2,1,0:T(8,128)(2,1)}, u32[]{:S(2)}) copy-start(bf16[1,1536,384]{2,1,0:T(8,128)(2,1)} %param.11) | copy-start | bytes 3538948
  55.6 46.3 %copy-start.1 = (bf16[1,1536,384]{2,1,0:T(8,128)(2,1)S(1)}, bf16[1,1536,384]{2,1,0:T(8,128)(2,1)}, u32[]{:S(2)}) copy-start(bf16[1,1536,384]{2,1,0:T(8,128)(2,1)} %param.12) | copy-start | bytes 3538948
  55.6 46.3 %copy-start.2 = (bf16[1,384,1536]{2,1,0:T(8,128)(2,1)S(1)}, bf16[1,384,1536]{2,1,0:T(8,128)(2,1)}, u32[]{:S(2)}) copy-start(bf16[1,384,1536]{2,1,0:T(8,128)(2,1)} %param.13) | copy-start | bytes 3538948
  108.9 32.3 %all-to-all-start.1 = ((bf16[16,24,1664]{2,1,0:T(8,128)(2,1)}), bf16[16,24,1664]{2,1,0:T(8,128)(2,1)S(1)}, u32[]{:S(2)}, u32[]{:S(2)}) async-start(bf16[16,24,1664]{2,1,0:T(8,128)(2,1)} %bitcast.6), calls=%async_computation.1 | async-start | bytes 2555904 | tf_op jit(solution)/shard_map/all_to_all | solution.py:225
  173.9 1.0 copy-start.3
Sparse Core Ops, SparseCore 0:
  109.0 36.5 reduce-scatter.1

commit v3 on v2

--- a/solution.py
+++ b/solution.py
@@ -47,6 +47,18 @@
             start = far * NEAR + (g % 2) * (NEAR // 2)
             lists.append([g * experts + (start + j) % experts for j in range(NEAR)])
     return lists
+
+
+def pack_kernel(layer_ref, grad_ref, ids_ref, probs_ref, out_ref):
+    width = layer_ref.shape[1]
+    out_ref[:, :width] = layer_ref[...]
+    out_ref[:, width : 2 * width] = grad_ref[...]
+    choice, lane = iota((TOP, LANES), 0), iota((TOP, LANES), 1)
+    ids_lane = jnp.where(lane == choice, 1.0, 0.0).astype(BF16)
+    probs_lane = jnp.where(lane == choice + TOP, 1.0, 0.0).astype(BF16)
+    ids = ids_ref[...].astype(F32).astype(BF16)
+    extras = dot(ids, ids_lane, ((0,), (0,))) + dot(probs_ref[...], probs_lane, ((0,), (0,)))
+    out_ref[:, 2 * width :] = extras.astype(BF16)
 
 
 def select_kernel(base_ref, tok_ref, send_ref, pick_ref):
@@ -92,13 +104,10 @@
     pick_ref[...] = jnp.where(chosen, 1.0, 0.0).astype(BF16)
 
 
-def expert_kernel(rows_ref, gate_ref, up_ref, down_ref, ret_ref, part_ref):
+def expert_kernel(rows_ref, gate_ref, up_ref, down_ref, ret_ref, both_ref, hidden_ref):
     width, hidden_width = gate_ref.shape
-    groups = part_ref.shape[0]
-    share = width // groups
-    down_share = hidden_width // groups
+    scaled = rows_ref[:, width:]
     rows = rows_ref[:, :width]
-    scaled = rows_ref[:, width:]
     gate, up, down = gate_ref[...], up_ref[...], down_ref[...]
     pre_gate = dot(rows, gate)
     pre_up = dot(rows, up)
@@ -112,18 +121,41 @@
     back = dot(gate_grad, gate, ((1,), (1,))) + dot(up_grad, up, ((1,), (1,)))
     ret_ref[:, :width] = back.astype(BF16)
     ret_ref[:, width:] = jnp.broadcast_to(prob_grad, (rows.shape[0], LANES)).astype(BF16)
-    both = jnp.concatenate([gate_grad, up_grad], axis=1)
-    for pair in range(groups // 2):
-        columns = rows_ref[:, pair * 2 * share : (pair + 1) * 2 * share]
-        part = dot(columns, both, ((0,), (0,))).astype(BF16)
-        part_ref[2 * pair, :share, :] = part[:share]
-        part_ref[2 * pair + 1, :share, :] = part[share:]
+    both_ref[:, :hidden_width] = gate_grad
+    both_ref[:, hidden_width:] = up_grad
+    hidden_ref[...] = hidden
+
+
+def part_kernel(core_ref, rows_ref, both_ref, hidden_ref, keep_ref, give_ref):
+    chips, part_rows, columns = keep_ref.shape
+    hidden_width = hidden_ref.shape[1]
+    width = rows_ref.shape[1] // 2
+    share = width // (2 * chips)
+    down_share = hidden_width // (2 * chips)
+    first = core_ref[0] == 0
+
+    def put(chip, low, pair):
+        size = pair.shape[0] // 2
+        keep_ref[chip, low : low + size, :] = jnp.where(first, pair[:size], pair[size:]).astype(BF16)
+        give_ref[chip, low : low + size, :] = jnp.where(first, pair[size:], pair[:size]).astype(BF16)
+
+    both = both_ref[...]
+    for chip in range(chips):
+        rows = rows_ref[:, chip * 2 * share : (chip + 1) * 2 * share]
+        put(chip, 0, dot(rows, both, ((0,), (0,))))
+    hidden = hidden_ref[...]
     half = width // 2
     for side in range(2):
-        part = dot(hidden, scaled[:, side * half : (side + 1) * half], ((0,), (0,))).astype(BF16)
-        for g in range(groups):
-            low = share + side * down_share
-            part_ref[g, low : low + down_share, :] = part[g * down_share : (g + 1) * down_share]
+        part = dot(hidden, rows_ref[:, width + side * half : width + (side + 1) * half], ((0,), (0,)))
+        for chip in range(chips):
+            put(chip, share + side * down_share, part[chip * 2 * down_share : (chip + 1) * 2 * down_share])
+
+
+def chip_sum_kernel(chip_ref, keep_ref, got_ref, *out_refs):
+    chips = keep_ref.shape[0]
+    for s, out_ref in enumerate(out_refs):
+        chip = (chip_ref[0] + s) & (chips - 1)
+        out_ref[...] = (keep_ref[chip].astype(F32) + got_ref[chip].astype(F32)).astype(BF16)
 
 
 def combine_kernel(base_ref, back_ref, pick_ref, extra_ref, sum_ref):
@@ -148,51 +180,74 @@
     sum_ref[:, width:] = result.astype(BF16)
 
 
-def finish_kernel(sums_ref, part_ref, in_ref, prob_ref, gate_ref, up_ref, down_ref):
+def finish_kernel(*refs):
+    sums_ref, part_refs = refs[0], refs[1:-5]
+    in_ref, prob_ref, gate_ref, up_ref, down_ref = refs[-5:]
     width = in_ref.shape[1]
     total = sums_ref[0].astype(F32)
     for s in range(1, FAR):
         total = total + sums_ref[s].astype(F32)
     in_ref[...] = total[:, :width].astype(BF16)
-    prob_ref[...] = total[:, width : width + TOP].astype(BF16)
+    pick = jnp.where(iota((TOP, LANES), 0) == iota((TOP, LANES), 1), 1.0, 0.0).astype(BF16)
+    prob_ref[...] = dot(pick, total[:, width:].astype(BF16), ((1,), (1,))).astype(BF16)
     share, hidden_width = gate_ref.shape
     down_share = down_ref.shape[0]
-    gate_ref[...] = part_ref[:share, :hidden_width].astype(F32)
-    up_ref[...] = part_ref[:share, hidden_width:].astype(F32)
     half = width // 2
-    down_ref[:, :half] = part_ref[share : share + down_share, :].astype(F32)
-    down_ref[:, half:] = part_ref[share + down_share :, :].astype(F32)
+
+    def part(low, size):
+        result = part_refs[0][low : low + size, :].astype(F32)
+        for ref in part_refs[1:]:
+            result = result + ref[low : low + size, :].astype(F32)
+        return result
+
+    gate_up = part(0, share)
+    gate_ref[...] = gate_up[:, :hidden_width]
+    up_ref[...] = gate_up[:, hidden_width:]
+    down_ref[:, :half] = part(share, down_share)
+    down_ref[:, half:] = part(share + down_share, down_share)
 
 
 def params(mib):
     return pltpu.CompilerParams(vmem_limit_bytes=mib * MIB)
+
+
+def cost(flops, nbytes):
+    return pl.CostEstimate(flops=flops, bytes_accessed=nbytes, transcendentals=0)
 
 
 def per_device(layer_in, grad_out, expert_ids, gate_probs, gate_weight, up_weight, down_weight):
     block, width = layer_in.shape
     hidden_width = gate_weight.shape[2]
-    groups = lax.axis_size("group")
+    chips = lax.axis_size("x")
+    groups = 2 * chips
     tokens = FAR * block
     slots = NEAR * FAR * CAP
     share = width // groups
     down_share = hidden_width // groups
     part_rows = share + 2 * down_share
-    moved = (lax.axis_index("group") & 1) * (NEAR // 2)
+    core = lax.axis_index("core").astype(jnp.int32)
+    chip = lax.axis_index("x").astype(jnp.int32)
+    moved = core * (NEAR // 2)
     place = lax.axis_index(("far", "near", "y")) - moved + EXPERTS
-    base = (place // NEAR * NEAR + moved).astype(jnp.int32).reshape(1)
+    base = ((place & -NEAR) + moved).astype(jnp.int32).reshape(1)
     scalar = pl.BlockSpec(memory_space=pltpu.SMEM)
 
-    extras = jnp.concatenate([expert_ids.astype(BF16), gate_probs], axis=1)
-    extras = jnp.pad(extras, ((0, 0), (0, LANES - 2 * TOP)))
-    packed = jnp.concatenate([layer_in, grad_out, extras], axis=1)
+    def shape(*dims):
+        return jax.ShapeDtypeStruct(dims, BF16)
+
+    packed = pl.pallas_call(
+        pack_kernel,
+        out_shape=shape(block, 2 * width + LANES),
+        in_specs=whole(4),
+        out_specs=whole(1)[0],
+        compiler_params=params(8),
+        name="pack_tokens",
+    )(layer_in, grad_out, expert_ids.T, gate_probs.T)
     near_tokens = lax.all_gather(packed, "far", tiled=True)
 
     send, pick = pl.pallas_call(
         select_kernel,
-        out_shape=(
-            jax.ShapeDtypeStruct((slots, 2 * width), BF16),
-            jax.ShapeDtypeStruct((tokens, slots), BF16),
-        ),
+        out_shape=(shape(slots, 2 * width), shape(tokens, slots)),
         in_specs=[scalar] + whole(1),
         out_specs=tuple(whole(2)),
         compiler_params=params(24),
@@ -202,31 +257,49 @@
     exchange = functools.partial(lax.all_to_all, split_axis=0, concat_axis=0, tiled=True)
     near_exchange = functools.partial(
         exchange,
-        axis_name=("group", "far", "near", "y"),
+        axis_name=("x", "core", "far", "near", "y"),
         axis_index_groups=windows(groups, EXPERTS),
     )
     rows = near_exchange(send.reshape(NEAR, FAR * CAP, 2 * width)).reshape(slots, 2 * width)
 
-    back, parts = pl.pallas_call(
+    matmul = 2 * slots * width * hidden_width
+    back, both, hidden = pl.pallas_call(
         expert_kernel,
-        out_shape=(
-            jax.ShapeDtypeStruct((slots, width + LANES), BF16),
-            jax.ShapeDtypeStruct((groups, part_rows, 2 * hidden_width), BF16),
-        ),
+        out_shape=(shape(slots, width + LANES), shape(slots, 2 * hidden_width), shape(slots, hidden_width)),
         in_specs=whole(4),
-        out_specs=tuple(whole(2)),
-        compiler_params=params(40),
+        out_specs=tuple(whole(3)),
+        compiler_params=params(32),
+        cost_estimate=cost(5 * matmul, 8 * MIB),
         name="expert_rows",
     )(rows, gate_weight[0], up_weight[0], down_weight[0])
-
-    part_sum = lax.psum_scatter(
-        parts.reshape(groups * part_rows, 2 * hidden_width), "group", scatter_dimension=0, tiled=True
-    )
     back = near_exchange(back.reshape(NEAR, FAR * CAP, width + LANES)).reshape(slots, width + LANES)
+
+    keep, give = pl.pallas_call(
+        part_kernel,
+        out_shape=(shape(chips, part_rows, 2 * hidden_width),) * 2,
+        in_specs=[scalar] + whole(3),
+        out_specs=tuple(whole(2)),
+        compiler_params=params(32),
+        cost_estimate=cost(3 * matmul, 8 * MIB),
+        name="weight_parts",
+    )(core.reshape(1), rows, both, hidden)
+    got = lax.ppermute(give, "core", [(0, 1), (1, 0)])
+    chip_sums = pl.pallas_call(
+        chip_sum_kernel,
+        out_shape=(shape(part_rows, 2 * hidden_width),) * chips,
+        in_specs=[scalar] + whole(2),
+        out_specs=tuple(whole(chips)),
+        compiler_params=params(16),
+        cost_estimate=cost(MIB, 6 * MIB),
+        name="chip_sums",
+    )(chip.reshape(1), keep, got)
+    parts = [chip_sums[0]] + [
+        lax.ppermute(chip_sums[s], "x", [(i, (i + s) % chips) for i in range(chips)]) for s in range(1, chips)
+    ]
 
     sums = pl.pallas_call(
         combine_kernel,
-        out_shape=jax.ShapeDtypeStruct((tokens, width + LANES), BF16),
+        out_shape=shape(tokens, width + LANES),
         in_specs=[scalar] + whole(3),
         out_specs=whole(1)[0],
         compiler_params=params(24),
@@ -237,28 +310,29 @@
     grad_in, grad_probs, grad_gate, grad_up, grad_down = pl.pallas_call(
         finish_kernel,
         out_shape=(
-            jax.ShapeDtypeStruct((block, width), BF16),
-            jax.ShapeDtypeStruct((block, TOP), BF16),
+            shape(block, width),
+            shape(TOP, block),
             jax.ShapeDtypeStruct((share, hidden_width), F32),
             jax.ShapeDtypeStruct((share, hidden_width), F32),
             jax.ShapeDtypeStruct((down_share, width), F32),
         ),
-        in_specs=whole(2),
+        in_specs=whole(1 + chips),
         out_specs=tuple(whole(5)),
         compiler_params=params(24),
         name="finish",
-    )(sums, part_sum)
-    return grad_in, grad_probs, grad_gate[None], grad_up[None], grad_down[None]
+    )(sums, *parts)
+    return grad_in, grad_probs.T, grad_gate[None], grad_up[None], grad_down[None]
 
 
 def solution(mesh):
     groups, experts = mesh.devices.shape
-    split = Mesh(mesh.devices.reshape(groups, FAR, 4, experts // NEAR), ("group", "far", "near", "y"))
-    everywhere = ("group", "far", "near", "y")
+    split = Mesh(
+        mesh.devices.reshape(groups // 2, 2, FAR, 4, experts // NEAR), ("x", "core", "far", "near", "y")
+    )
     expert = ("far", "near", "y")
-    token_spec = P(everywhere, None)
+    token_spec = P(("x", "core") + expert, None)
     weight_spec = P(expert, None, None)
-    grad_spec = P(expert, "group", None)
+    grad_spec = P(expert, ("x", "core"), None)
     return jax.shard_map(
         per_device,
         mesh=split,

time: 184 us -> 170 us (0.924)
  blocking collectives: 122 us -> 90.6 us
  starting transfers between devices: 6.07 us -> 26.1 us
  between operations: 14.1 us -> 0.77 us
  waiting for transfers between devices: 26.3 us -> 30.9 us
  Pallas kernels: 10.3 us -> 14 us
  local copies, waits for them, and re-layouts: 2.55 us -> 6.06 us
    all_to_all x1 -> x0, blocking collectives: 31.8 us -> none  [per_device(): sums = exchange(sums.reshape(FAR, block, width + LANES), 'far')]
    ppermute x0 -> x4, waiting for transfers between devices: none -> 15.1 us  [the longest x3 15.1 us: per_device(): lax.ppermute(chip_sums[s], 'x', [(i, (i + s) % chips) for i in range(chip...]
    ppermute x0 -> x4, starting transfers between devices: none -> 13 us  [the longest x3 8.64 us: per_device(): lax.ppermute(chip_sums[s], 'x', [(i, (i + s) % chips) for i in range(chip...]
    all_to_all x1, waiting for transfers between devices: 26.3 us -> 15.8 us  [per_device(): near_exchange(back.reshape(NEAR, FAR * CAP, width + LANES))]
    all_to_all x0 -> x1, starting transfers between devices: none -> 7.13 us  [per_device(): sums = exchange(sums.reshape(FAR, block, width + LANES), 'far')]
    pallas_call x4 -> x7, Pallas kernels: 10.3 us -> 14 us  [the longest x1 4.47 us: per_device(): pl.pallas_call(expert_kernel, out_shape=(shape(slots, width + LANES), sha...]
    unnamed x10 -> x22, local copies, waits for them, and re-layouts: 2.45 us -> 6.05 us
  transfers between devices with their start and end apart: 2 -> 6, of which waited for: 1 -> 4; matrix products, arithmetic and copies ran while one was open for 0% -> 0% of each run, Pallas kernels for 0% -> 4%
where the time goes in v3:
time: 170 us; the launch traced here: 168 us
  blocking collectives  90.6 us (53%)
  waiting for transfers between devices  30.9 us (18%)
  starting transfers between devices  26.1 us (15%)
  Pallas kernels  14 us (8%)
  local copies, waits for them, and re-layouts  6.06 us (4%)
    all_to_all x1, blocking collectives, per_device(): near_exchange(send.reshape(NEAR, FAR * CAP, 2 * width))  46.3 us
    all_gather x1, blocking collectives, per_device(): near_tokens = lax.all_gather(packed, 'far', tiled=True)  44.3 us
    all_to_all x1, waiting for transfers between devices, per_device(): near_exchange(back.reshape(NEAR, FAR * CAP, width + LANES))  15.8 us
    ppermute x3, waiting for transfers between devices, per_device(): lax.ppermute(chip_sums[s], 'x', [(i, (i + s) % chips) for i in range(chip...  15.1 us
    ppermute x3, starting transfers between devices, per_device(): lax.ppermute(chip_sums[s], 'x', [(i, (i + s) % chips) for i in range(chip...  8.64 us
    all_to_all x1, starting transfers between devices, per_device(): sums = exchange(sums.reshape(FAR, block, width + LANES), 'far')  7.13 us
    unnamed x22, local copies, waits for them, and re-layouts  6.05 us
    all_to_all x1, starting transfers between devices, per_device(): near_exchange(back.reshape(NEAR, FAR * CAP, width + LANES))  6.03 us
  transfers between devices with their start and end apart: 6, of which 4 were waited for; matrix products, arithmetic and copies ran while one was open for 0% of the time, Pallas kernels for 4%

profile of v3, /device:TPU:6, one launch (start us, length us, event | category | flops | bytes accessed | tf_op | source)
XLA Modules:
  0.0 168.4 jit_solution(15793870875985590368)
XLA Ops:
  0.6 0.0 copy-start.4
  0.7 0.9 copy-done.4
  1.5 0.0 copy-start.5
  1.5 0.9 copy-done.5
  2.4 0.0 copy-start.6
  2.4 0.7 copy-done.6
  3.1 0.0 copy-start.7
  3.1 0.7 copy-done.7
  3.8 0.2 pack_tokens.1
  4.0 44.3 %all_gather.3.tok_ref = bf16[128,3200]{1,0:T(8,128)(2,1)S(1)} all-gather(bf16[32,3200]{1,0:T(8,128)(2,1)S(1)} %pack_tokens.1), channel_id=1, replica_groups=mesh['x'=4,'core'=2,'far'=4,'near'=4,'y'=4] {'far'}, dimensions={0}, use_global_device_ids=true | all-gather | bytes 1024000 | tf_op jit(solution)/shard_map/all_gather | solution.py:246
  48.2 1.5 select_rows.1
  49.7 0.0 copy-start.8
  49.7 0.0 copy-start.9
  49.7 0.0 copy-start.10
  49.7 46.3 %all_to_all.15 = bf16[16,24,3072]{2,1,0:T(8,128)(2,1)S(1)} all-to-all(bf16[16,24,3072]{2,1,0:T(8,128)(2,1)S(1)} %bitcast.20), channel_id=1, replica_groups={{0,1,2,3,4,5,6,7,8,9,10,11,12,13,14,15},{16,17,18,19,20,21,22,23,24,25,..., dimensions={0} | all-to-all | bytes 4718592 | tf_op jit(solution)/shard_map/all_to_all | solution.py:263
  96.0 0.0 copy-start
  96.0 0.0 copy-done.8
  96.0 0.0 copy-done.9
  96.0 0.0 copy-done.10
  96.0 4.5 %expert_rows.1 = (bf16[384,1664]{1,0:T(8,128)(2,1)}, bf16[384,768]{1,0:T(8,128)(2,1)S(1)}, bf16[384,384]{1,0:T(8,128)(2,1)S(1)}) custom-call(bf16[384,3072]{1,0:T(8,128)(2,1)S(1)} %bitcast.18, bf16[1536,384]{1,0:T(8,128)(2,1)S(1)} %bitcast.23, bf16[1536,384]{1,0:T(8,128)(2,1)S(1)} %bitcast.24, bf16[384,1536]{1,0:T(8,128)(2,1)S(1)} %bitcast.25), custom_call_target="tpu_custom_call" | custom-call | flops 2264924160 | bytes 8388608 | tf_op jit(solution)/shard_map/expert_rows/pallas_call | solution.py:266
  100.5 0.0 copy-done
  100.5 6.0 %all-to-all-start.1 = ((bf16[16,24,1664]{2,1,0:T(8,128)(2,1)}), bf16[16,24,1664]{2,1,0:T(8,128)(2,1)S(1)}, u32[]{:S(2)}, u32[]{:S(2)}) async-start(bf16[16,24,1664]{2,1,0:T(8,128)(2,1)} %bitcast.8), calls=%async_computation.1 | async-start | bytes 2555904 | tf_op jit(solution)/shard_map/all_to_all | solution.py:275
  106.6 0.0 copy-start.1
  106.6 1.7 copy-done.1
  108.2 3.3 %weight_parts.1 = (bf16[4,288,768]{2,1,0:T(8,128)(2,1)S(1)}, bf16[4,288,768]{2,1,0:T(8,128)(2,1)}) custom-call(s32[1]{0:T(128)} %bitcast.12.core_ref, bf16[384,3072]{1,0:T(8,128)(2,1)S(1)} %bitcast.19, bf16[384,768]{1,0:T(8,128)(2,1)S(1)} %get-tuple-element.24.both_ref, bf16[384,384]{1,0:T(8,128)(2,1)S(1)} %get-tuple-element.25.hidden_ref), custom_call_target="tpu_custom_call" | custom-call | flops 1358954496 | bytes 8388608 | tf_op jit(solution)/shard_map/weight_parts/pallas_call | solution.py:277
  111.5 0.0 copy-start.2
  111.5 1.2 copy-done.2
  112.7 4.3 %collective-permute-start = (bf16[4,288,768]{2,1,0:T(8,128)(2,1)}, bf16[4,288,768]{2,1,0:T(8,128)(2,1)}, u32[]{:S(2)}, u32[]{:S(2)}) collective-permute-start(bf16[4,288,768]{2,1,0:T(8,128)(2,1)} %get-tuple-element.27), channel_id=1, source_target_pairs={{0,64},{64,0},{1,65},{65,1},{2,66},{66,2},{3,67},{67,3},{4,68},{68... | collective-permute-start | bytes 5308424 | tf_op jit(solution)/shard_map/ppermute | solution.py:286
  117.0 0.0 copy-start.3
  117.1 15.8 %all-to-all-done.1 = bf16[16,24,1664]{2,1,0:T(8,128)(2,1)S(1)} async-done(((bf16[16,24,1664]{2,1,0:T(8,128)(2,1)}), bf16[16,24,1664]{2,1,0:T(8,128)(2,1)S(1)}, u32[]{:S(2)}, u32[]{:S(2)}) %all-to-all-start.1) | async-done | bytes 1277984 | tf_op jit(solution)/shard_map/all_to_all | solution.py:275
  132.8 1.6 combine_rows.1
  134.5 7.1 %all-to-all-start.2 = ((bf16[4,32,1664]{2,1,0:T(8,128)(2,1)}), bf16[4,32,1664]{2,1,0:T(8,128)(2,1)S(1)}, u32[]{:S(2)}, u32[]{:S(2)}) async-start(bf16[4,32,1664]{2,1,0:T(8,128)(2,1)} %bitcast.10), calls=%async_computation.2 | async-start | bytes 851968 | tf_op jit(solution)/shard_map/all_to_all | solution.py:308
  141.6 0.0 collective-permute-done.got_ref
  141.6 0.0 copy-done.3
  141.6 1.9 %chip_sums.1 = (bf16[288,768]{1,0:T(8,128)(2,1)S(1)}, bf16[288,768]{1,0:T(8,128)(2,1)S(1)}, bf16[288,768]{1,0:T(8,128)(2,1)S(1)}, bf16[288,768]{1,0:T(8,128)(2,1)S(1)}) custom-call(s32[1]{0:T(128)} %bitcast.11.chip_ref, bf16[4,288,768]{2,1,0:T(8,128)(2,1)S(1)} %copy-done.3, bf16[4,288,768]{2,1,0:T(8,128)(2,1)} %collective-permute-done.got_ref), custom_call_target="tpu_custom_call" | custom-call | flops 1048576 | bytes 6291456 | tf_op jit(solution)/shard_map/chip_sums/pallas_call | solution.py:287
  143.5 2.4 %collective-permute-start.1 = (bf16[288,768]{1,0:T(8,128)(2,1)S(1)}, bf16[288,768]{1,0:T(8,128)(2,1)S(1)}, u32[]{:S(2)}, u32[]{:S(2)}) collective-permute-start(bf16[288,768]{1,0:T(8,128)(2,1)S(1)} %get-tuple-element.29), channel_id=1, source_target_pairs={{0,128},{128,256},{256,384},{384,0},{1,129},{129,257},{257,385},{3... | collective-permute-start | bytes 1327112 | tf_op jit(solution)/shard_map/ppermute | solution.py:297
  145.9 4.3 %collective-permute-start.2 = (bf16[288,768]{1,0:T(8,128)(2,1)S(1)}, bf16[288,768]{1,0:T(8,128)(2,1)S(1)}, u32[]{:S(2)}, u32[]{:S(2)}) collective-permute-start(bf16[288,768]{1,0:T(8,128)(2,1)S(1)} %get-tuple-element.30), channel_id=1, source_target_pairs={{0,256},{128,384},{256,0},{384,128},{1,257},{129,385},{257,1},{385... | collective-permute-start | bytes 1327112 | tf_op jit(solution)/shard_map/ppermute | solution.py:297
  150.2 1.9 %collective-permute-start.3 = (bf16[288,768]{1,0:T(8,128)(2,1)S(1)}, bf16[288,768]{1,0:T(8,128)(2,1)S(1)}, u32[]{:S(2)}, u32[]{:S(2)}) collective-permute-start(bf16[288,768]{1,0:T(8,128)(2,1)S(1)} %get-tuple-element.31), channel_id=1, source_target_pairs={{0,384},{128,0},{256,128},{384,256},{1,385},{129,1},{257,129},{385... | collective-permute-start | bytes 1327112 | tf_op jit(solution)/shard_map/ppermute | solution.py:297
  152.1 6.3 %collective-permute-done.1.refs_2_ = bf16[288,768]{1,0:T(8,128)(2,1)S(1)} collective-permute-done((bf16[288,768]{1,0:T(8,128)(2,1)S(1)}, bf16[288,768]{1,0:T(8,128)(2,1)S(1)}, u32[]{:S(2)}, u32[]{:S(2)}) %collective-permute-start.1) | collective-permute-done | bytes 442400 | tf_op jit(solution)/shard_map/ppermute | solution.py:297
  158.5 3.9 %collective-permute-done.2.refs_3_ = bf16[288,768]{1,0:T(8,128)(2,1)S(1)} collective-permute-done((bf16[288,768]{1,0:T(8,128)(2,1)S(1)}, bf16[288,768]{1,0:T(8,128)(2,1)S(1)}, u32[]{:S(2)}, u32[]{:S(2)}) %collective-permute-start.2) | collective-permute-done | bytes 442400 | tf_op jit(solution)/shard_map/ppermute | solution.py:297
  162.4 4.9 %collective-permute-done.3.refs_4_ = bf16[288,768]{1,0:T(8,128)(2,1)S(1)} collective-permute-done((bf16[288,768]{1,0:T(8,128)(2,1)S(1)}, bf16[288,768]{1,0:T(8,128)(2,1)S(1)}, u32[]{:S(2)}, u32[]{:S(2)}) %collective-permute-start.3) | collective-permute-done | bytes 442400 | tf_op jit(solution)/shard_map/ppermute | solution.py:297
  167.3 0.0 all-to-all-done.2.refs_0_
  167.3 1.1 finish.1
  (1 shorter events, 0.0 us)
Async XLA Ops:
  0.6 0.9 copy-start.4
  1.5 0.9 copy-start.5
  2.4 0.7 copy-start.6
  3.1 0.7 copy-start.7
  49.7 46.3 %copy-start.8 = (bf16[1,1536,384]{2,1,0:T(8,128)(2,1)S(1)}, bf16[1,1536,384]{2,1,0:T(8,128)(2,1)}, u32[]{:S(2)}) copy-start(bf16[1,1536,384]{2,1,0:T(8,128)(2,1)} %param.11) | copy-start | bytes 3538948
  49.7 46.3 %copy-start.9 = (bf16[1,1536,384]{2,1,0:T(8,128)(2,1)S(1)}, bf16[1,1536,384]{2,1,0:T(8,128)(2,1)}, u32[]{:S(2)}) copy-start(bf16[1,1536,384]{2,1,0:T(8,128)(2,1)} %param.12) | copy-start | bytes 3538948
  49.7 46.3 %copy-start.10 = (bf16[1,384,1536]{2,1,0:T(8,128)(2,1)S(1)}, bf16[1,384,1536]{2,1,0:T(8,128)(2,1)}, u32[]{:S(2)}) copy-start(bf16[1,384,1536]{2,1,0:T(8,128)(2,1)} %param.13) | copy-start | bytes 3538948
  96.0 4.5 %copy-start = (bf16[16,24,3072]{2,1,0:T(8,128)(2,1)}, bf16[16,24,3072]{2,1,0:T(8,128)(2,1)S(1)}, u32[]{:S(2)}) copy-start(bf16[16,24,3072]{2,1,0:T(8,128)(2,1)S(1)} %all_to_all.15) | copy-start | bytes 7077892
  100.5 32.3 %all-to-all-start.1 = ((bf16[16,24,1664]{2,1,0:T(8,128)(2,1)}), bf16[16,24,1664]{2,1,0:T(8,128)(2,1)S(1)}, u32[]{:S(2)}, u32[]{:S(2)}) async-start(bf16[16,24,1664]{2,1,0:T(8,128)(2,1)} %bitcast.8), calls=%async_computation.1 | async-start | bytes 2555904 | tf_op jit(solution)/shard_map/all_to_all | solution.py:275
  106.6 1.7 copy-start.1
  111.5 1.2 copy-start.2
  112.7 28.9 %collective-permute-start = (bf16[4,288,768]{2,1,0:T(8,128)(2,1)}, bf16[4,288,768]{2,1,0:T(8,128)(2,1)}, u32[]{:S(2)}, u32[]{:S(2)}) collective-permute-start(bf16[4,288,768]{2,1,0:T(8,128)(2,1)} %get-tuple-element.27), channel_id=1, source_target_pairs={{0,64},{64,0},{1,65},{65,1},{2,66},{66,2},{3,67},{67,3},{4,68},{68... | collective-permute-start | bytes 5308424 | tf_op jit(solution)/shard_map/ppermute | solution.py:286
  117.0 24.5 %copy-start.3 = (bf16[4,288,768]{2,1,0:T(8,128)(2,1)S(1)}, bf16[4,288,768]{2,1,0:T(8,128)(2,1)}, u32[]{:S(2)}) copy-start(bf16[4,288,768]{2,1,0:T(8,128)(2,1)} %copy-done.2) | copy-start | bytes 5308420
  134.5 32.8 %all-to-all-start.2 = ((bf16[4,32,1664]{2,1,0:T(8,128)(2,1)}), bf16[4,32,1664]{2,1,0:T(8,128)(2,1)S(1)}, u32[]{:S(2)}, u32[]{:S(2)}) async-start(bf16[4,32,1664]{2,1,0:T(8,128)(2,1)} %bitcast.10), calls=%async_computation.2 | async-start | bytes 851968 | tf_op jit(solution)/shard_map/all_to_all | solution.py:308
  143.5 15.0 %collective-permute-start.1 = (bf16[288,768]{1,0:T(8,128)(2,1)S(1)}, bf16[288,768]{1,0:T(8,128)(2,1)S(1)}, u32[]{:S(2)}, u32[]{:S(2)}) collective-permute-start(bf16[288,768]{1,0:T(8,128)(2,1)S(1)} %get-tuple-element.29), channel_id=1, source_target_pairs={{0,128},{128,256},{256,384},{384,0},{1,129},{129,257},{257,385},{3... | collective-permute-start | bytes 1327112 | tf_op jit(solution)/shard_map/ppermute | solution.py:297
  145.9 16.5 %collective-permute-start.2 = (bf16[288,768]{1,0:T(8,128)(2,1)S(1)}, bf16[288,768]{1,0:T(8,128)(2,1)S(1)}, u32[]{:S(2)}, u32[]{:S(2)}) collective-permute-start(bf16[288,768]{1,0:T(8,128)(2,1)S(1)} %get-tuple-element.30), channel_id=1, source_target_pairs={{0,256},{128,384},{256,0},{384,128},{1,257},{129,385},{257,1},{385... | collective-permute-start | bytes 1327112 | tf_op jit(solution)/shard_map/ppermute | solution.py:297
  150.2 17.1 %collective-permute-start.3 = (bf16[288,768]{1,0:T(8,128)(2,1)S(1)}, bf16[288,768]{1,0:T(8,128)(2,1)S(1)}, u32[]{:S(2)}, u32[]{:S(2)}) collective-permute-start(bf16[288,768]{1,0:T(8,128)(2,1)S(1)} %get-tuple-element.31), channel_id=1, source_target_pairs={{0,384},{128,0},{256,128},{384,256},{1,385},{129,1},{257,129},{385... | collective-permute-start | bytes 1327112 | tf_op jit(solution)/shard_map/ppermute | solution.py:297

commit v4 on v3

--- a/solution.py
+++ b/solution.py
@@ -49,16 +49,24 @@
     return lists
 
 
-def pack_kernel(layer_ref, grad_ref, ids_ref, probs_ref, out_ref):
+def pack_kernel(layer_ref, grad_ref, ids_ref, probs_ref, out_ref, ids_vmem, sems):
     width = layer_ref.shape[1]
-    out_ref[:, :width] = layer_ref[...]
-    out_ref[:, width : 2 * width] = grad_ref[...]
+    copies = [
+        pltpu.make_async_copy(ids_ref, ids_vmem, sems.at[0]),
+        pltpu.make_async_copy(layer_ref, out_ref.at[:, :width], sems.at[1]),
+        pltpu.make_async_copy(grad_ref, out_ref.at[:, width : 2 * width], sems.at[2]),
+    ]
+    for copy in copies:
+        copy.start()
     choice, lane = iota((TOP, LANES), 0), iota((TOP, LANES), 1)
     ids_lane = jnp.where(lane == choice, 1.0, 0.0).astype(BF16)
     probs_lane = jnp.where(lane == choice + TOP, 1.0, 0.0).astype(BF16)
-    ids = ids_ref[...].astype(F32).astype(BF16)
+    copies[0].wait()
+    ids = ids_vmem[...].astype(F32).astype(BF16)
     extras = dot(ids, ids_lane, ((0,), (0,))) + dot(probs_ref[...], probs_lane, ((0,), (0,)))
     out_ref[:, 2 * width :] = extras.astype(BF16)
+    copies[1].wait()
+    copies[2].wait()
 
 
 def select_kernel(base_ref, tok_ref, send_ref, pick_ref):
@@ -238,8 +246,9 @@
     packed = pl.pallas_call(
         pack_kernel,
         out_shape=shape(block, 2 * width + LANES),
-        in_specs=whole(4),
+        in_specs=[pl.BlockSpec(memory_space=pltpu.HBM)] * 3 + whole(1),
         out_specs=whole(1)[0],
+        scratch_shapes=[pltpu.VMEM((TOP, block), jnp.int32), pltpu.SemaphoreType.DMA((3,))],
         compiler_params=params(8),
         name="pack_tokens",
     )(layer_in, grad_out, expert_ids.T, gate_probs.T)
@@ -297,6 +306,7 @@
         lax.ppermute(chip_sums[s], "x", [(i, (i + s) % chips) for i in range(chips)]) for s in range(1, chips)
     ]
 
+    back, _ = lax.optimization_barrier((back, chip_sums[0]))
     sums = pl.pallas_call(
         combine_kernel,
         out_shape=shape(tokens, width + LANES),

time: 170 us -> 169 us (level)
  waiting for transfers between devices: 30.9 us -> 26.9 us
    all_to_all x1, waiting for transfers between devices: 15.8 us -> 8.1 us  [per_device(): near_exchange(back.reshape(NEAR, FAR * CAP, width + LANES))]
    ppermute x1, waiting for transfers between devices: 0.01 us -> 3.62 us  [per_device(): got = lax.ppermute(give, 'core', [(0, 1), (1, 0)])]
  transfers between devices with their start and end apart: 6 -> 6, of which waited for: 4 -> 5; matrix products, arithmetic and copies ran while one was open for 0% -> 0% of each run, Pallas kernels for 4% -> 3%
where the time goes in v4:
time: 169 us; the launch traced here: 167 us
  blocking collectives  90.6 us (54%)
  waiting for transfers between devices  26.9 us (16%)
  starting transfers between devices  26.1 us (15%)
  Pallas kernels  14.7 us (9%)
  local copies, waits for them, and re-layouts  7.56 us (4%)
    all_to_all x1, blocking collectives, per_device(): near_exchange(send.reshape(NEAR, FAR * CAP, 2 * width))  46.3 us
    all_gather x1, blocking collectives, per_device(): near_tokens = lax.all_gather(packed, 'far', tiled=True)  44.3 us
    ppermute x3, waiting for transfers between devices, per_device(): lax.ppermute(chip_sums[s], 'x', [(i, (i + s) % chips) for i in range(chip...  15.1 us
    ppermute x3, starting transfers between devices, per_device(): lax.ppermute(chip_sums[s], 'x', [(i, (i + s) % chips) for i in range(chip...  8.62 us
    all_to_all x1, waiting for transfers between devices, per_device(): near_exchange(back.reshape(NEAR, FAR * CAP, width + LANES))  8.1 us
    unnamed x22, local copies, waits for them, and re-layouts  7.55 us
    all_to_all x1, starting transfers between devices, per_device(): sums = exchange(sums.reshape(FAR, block, width + LANES), 'far')  7.14 us
    all_to_all x1, starting transfers between devices, per_device(): near_exchange(back.reshape(NEAR, FAR * CAP, width + LANES))  6.02 us
  transfers between devices with their start and end apart: 6, of which 5 were waited for; matrix products, arithmetic and copies ran while one was open for 0% of the time, Pallas kernels for 3%

profile of v4, /device:TPU:6, one launch (start us, length us, event | category | flops | bytes accessed | tf_op | source)
XLA Modules:
  0.0 166.6 jit_solution(10316417388072696053)
XLA Ops:
  0.6 0.0 copy-start.4
  0.7 0.9 copy-done.4
  1.5 0.0 copy-start.5
  1.5 0.9 copy-done.5
  2.4 0.0 copy-start.6
  2.4 0.7 copy-done.6
  3.1 0.0 copy-start.7
  3.1 0.7 copy-done.7
  3.8 0.3 pack_tokens.1
  4.1 44.3 %all_gather.3.tok_ref = bf16[128,3200]{1,0:T(8,128)(2,1)S(1)} all-gather(bf16[32,3200]{1,0:T(8,128)(2,1)S(1)} %pack_tokens.1), channel_id=1, replica_groups=mesh['x'=4,'core'=2,'far'=4,'near'=4,'y'=4] {'far'}, dimensions={0}, use_global_device_ids=true | all-gather | bytes 1024000 | tf_op jit(solution)/shard_map/all_gather | solution.py:255
  48.3 1.5 select_rows.1
  49.8 0.0 copy-start.8
  49.8 0.0 copy-start.9
  49.8 0.0 copy-start.10
  49.8 46.3 %all_to_all.15 = bf16[16,24,3072]{2,1,0:T(8,128)(2,1)S(1)} all-to-all(bf16[16,24,3072]{2,1,0:T(8,128)(2,1)S(1)} %bitcast.20), channel_id=1, replica_groups={{0,1,2,3,4,5,6,7,8,9,10,11,12,13,14,15},{16,17,18,19,20,21,22,23,24,25,..., dimensions={0} | all-to-all | bytes 4718592 | tf_op jit(solution)/shard_map/all_to_all | solution.py:272
  96.1 0.0 copy-start
  96.1 0.0 copy-done.8
  96.1 0.0 copy-done.9
  96.1 0.0 copy-done.10
  96.2 4.5 %expert_rows.1 = (bf16[384,1664]{1,0:T(8,128)(2,1)}, bf16[384,768]{1,0:T(8,128)(2,1)S(1)}, bf16[384,384]{1,0:T(8,128)(2,1)S(1)}) custom-call(bf16[384,3072]{1,0:T(8,128)(2,1)S(1)} %bitcast.18, bf16[1536,384]{1,0:T(8,128)(2,1)S(1)} %bitcast.23, bf16[1536,384]{1,0:T(8,128)(2,1)S(1)} %bitcast.24, bf16[384,1536]{1,0:T(8,128)(2,1)S(1)} %bitcast.25), custom_call_target="tpu_custom_call" | custom-call | flops 2264924160 | bytes 8388608 | tf_op jit(solution)/shard_map/expert_rows/pallas_call | solution.py:275
  100.6 0.0 copy-done
  100.6 6.0 %all-to-all-start.1 = ((bf16[16,24,1664]{2,1,0:T(8,128)(2,1)}), bf16[16,24,1664]{2,1,0:T(8,128)(2,1)S(1)}, u32[]{:S(2)}, u32[]{:S(2)}) async-start(bf16[16,24,1664]{2,1,0:T(8,128)(2,1)} %bitcast.8), calls=%async_computation.1 | async-start | bytes 2555904 | tf_op jit(solution)/shard_map/all_to_all | solution.py:284
  106.7 0.0 copy-start.1
  106.7 1.7 copy-done.1
  108.3 3.3 %weight_parts.1 = (bf16[4,288,768]{2,1,0:T(8,128)(2,1)S(1)}, bf16[4,288,768]{2,1,0:T(8,128)(2,1)}) custom-call(s32[1]{0:T(128)} %bitcast.11.core_ref, bf16[384,3072]{1,0:T(8,128)(2,1)S(1)} %bitcast.19, bf16[384,768]{1,0:T(8,128)(2,1)S(1)} %get-tuple-element.24.both_ref, bf16[384,384]{1,0:T(8,128)(2,1)S(1)} %get-tuple-element.25.hidden_ref), custom_call_target="tpu_custom_call" | custom-call | flops 1358954496 | bytes 8388608 | tf_op jit(solution)/shard_map/weight_parts/pallas_call | solution.py:286
  111.6 0.0 copy-start.2
  111.6 1.2 copy-done.2
  112.8 4.3 %collective-permute-start = (bf16[4,288,768]{2,1,0:T(8,128)(2,1)}, bf16[4,288,768]{2,1,0:T(8,128)(2,1)}, u32[]{:S(2)}, u32[]{:S(2)}) collective-permute-start(bf16[4,288,768]{2,1,0:T(8,128)(2,1)} %get-tuple-element.27), channel_id=1, source_target_pairs={{0,64},{64,0},{1,65},{65,1},{2,66},{66,2},{3,67},{67,3},{4,68},{68... | collective-permute-start | bytes 5308424 | tf_op jit(solution)/shard_map/ppermute | solution.py:295
  117.2 3.6 %collective-permute-done.got_ref = bf16[4,288,768]{2,1,0:T(8,128)(2,1)} collective-permute-done((bf16[4,288,768]{2,1,0:T(8,128)(2,1)}, bf16[4,288,768]{2,1,0:T(8,128)(2,1)}, u32[]{:S(2)}, u32[]{:S(2)}) %collective-permute-start) | collective-permute-done | bytes 1769504 | tf_op jit(solution)/shard_map/ppermute | solution.py:295
  120.8 0.0 copy-start.3
  120.8 1.5 copy-done.3
  122.3 2.6 %chip_sums.1 = (bf16[288,768]{1,0:T(8,128)(2,1)S(1)}, bf16[288,768]{1,0:T(8,128)(2,1)}, bf16[288,768]{1,0:T(8,128)(2,1)S(1)}, bf16[288,768]{1,0:T(8,128)(2,1)S(1)}) custom-call(s32[1]{0:T(128)} %bitcast.10.chip_ref, bf16[4,288,768]{2,1,0:T(8,128)(2,1)S(1)} %copy-done.3, bf16[4,288,768]{2,1,0:T(8,128)(2,1)} %collective-permute-done.got_ref), custom_call_target="tpu_custom_call" | custom-call | flops 1048576 | bytes 6291456 | tf_op jit(solution)/shard_map/chip_sums/pallas_call | solution.py:296
  124.8 8.1 %all-to-all-done.1 = bf16[16,24,1664]{2,1,0:T(8,128)(2,1)S(1)} async-done(((bf16[16,24,1664]{2,1,0:T(8,128)(2,1)}), bf16[16,24,1664]{2,1,0:T(8,128)(2,1)S(1)}, u32[]{:S(2)}, u32[]{:S(2)}) %all-to-all-start.1) | async-done | bytes 1277984 | tf_op jit(solution)/shard_map/all_to_all | solution.py:284
  132.9 1.6 combine_rows.1
  134.5 7.1 %all-to-all-start.2 = ((bf16[4,32,1664]{2,1,0:T(8,128)(2,1)}), bf16[4,32,1664]{2,1,0:T(8,128)(2,1)S(1)}, u32[]{:S(2)}, u32[]{:S(2)}) async-start(bf16[4,32,1664]{2,1,0:T(8,128)(2,1)} %bitcast.12), calls=%async_computation.2 | async-start | bytes 851968 | tf_op jit(solution)/shard_map/all_to_all | solution.py:318
  141.7 2.4 %collective-permute-start.1 = (bf16[288,768]{1,0:T(8,128)(2,1)}, bf16[288,768]{1,0:T(8,128)(2,1)S(1)}, u32[]{:S(2)}, u32[]{:S(2)}) collective-permute-start(bf16[288,768]{1,0:T(8,128)(2,1)} %get-tuple-element.31), channel_id=1, source_target_pairs={{0,128},{128,256},{256,384},{384,0},{1,129},{129,257},{257,385},{3... | collective-permute-start | bytes 1327112 | tf_op jit(solution)/shard_map/ppermute | solution.py:306
  144.1 4.3 %collective-permute-start.2 = (bf16[288,768]{1,0:T(8,128)(2,1)S(1)}, bf16[288,768]{1,0:T(8,128)(2,1)S(1)}, u32[]{:S(2)}, u32[]{:S(2)}) collective-permute-start(bf16[288,768]{1,0:T(8,128)(2,1)S(1)} %get-tuple-element.32), channel_id=1, source_target_pairs={{0,256},{128,384},{256,0},{384,128},{1,257},{129,385},{257,1},{385... | collective-permute-start | bytes 1327112 | tf_op jit(solution)/shard_map/ppermute | solution.py:306
  148.4 1.9 %collective-permute-start.3 = (bf16[288,768]{1,0:T(8,128)(2,1)S(1)}, bf16[288,768]{1,0:T(8,128)(2,1)S(1)}, u32[]{:S(2)}, u32[]{:S(2)}) collective-permute-start(bf16[288,768]{1,0:T(8,128)(2,1)S(1)} %get-tuple-element.33), channel_id=1, source_target_pairs={{0,384},{128,0},{256,128},{384,256},{1,385},{129,1},{257,129},{385... | collective-permute-start | bytes 1327112 | tf_op jit(solution)/shard_map/ppermute | solution.py:306
  150.3 6.6 %collective-permute-done.1.refs_2_ = bf16[288,768]{1,0:T(8,128)(2,1)S(1)} collective-permute-done((bf16[288,768]{1,0:T(8,128)(2,1)}, bf16[288,768]{1,0:T(8,128)(2,1)S(1)}, u32[]{:S(2)}, u32[]{:S(2)}) %collective-permute-start.1) | collective-permute-done | bytes 442400 | tf_op jit(solution)/shard_map/ppermute | solution.py:306
  156.9 3.7 %collective-permute-done.2.refs_3_ = bf16[288,768]{1,0:T(8,128)(2,1)S(1)} collective-permute-done((bf16[288,768]{1,0:T(8,128)(2,1)S(1)}, bf16[288,768]{1,0:T(8,128)(2,1)S(1)}, u32[]{:S(2)}, u32[]{:S(2)}) %collective-permute-start.2) | collective-permute-done | bytes 442400 | tf_op jit(solution)/shard_map/ppermute | solution.py:306
  160.6 4.9 %collective-permute-done.3.refs_4_ = bf16[288,768]{1,0:T(8,128)(2,1)S(1)} collective-permute-done((bf16[288,768]{1,0:T(8,128)(2,1)S(1)}, bf16[288,768]{1,0:T(8,128)(2,1)S(1)}, u32[]{:S(2)}, u32[]{:S(2)}) %collective-permute-start.3) | collective-permute-done | bytes 442400 | tf_op jit(solution)/shard_map/ppermute | solution.py:306
  165.5 0.0 all-to-all-done.2.refs_0_
  165.5 1.1 finish.1
  (1 shorter events, 0.0 us)
Async XLA Ops:
  0.6 0.9 copy-start.4
  1.5 0.9 copy-start.5
  2.4 0.7 copy-start.6
  3.1 0.7 copy-start.7
  49.8 46.3 %copy-start.8 = (bf16[1,1536,384]{2,1,0:T(8,128)(2,1)S(1)}, bf16[1,1536,384]{2,1,0:T(8,128)(2,1)}, u32[]{:S(2)}) copy-start(bf16[1,1536,384]{2,1,0:T(8,128)(2,1)} %param.11) | copy-start | bytes 3538948
  49.8 46.3 %copy-start.9 = (bf16[1,1536,384]{2,1,0:T(8,128)(2,1)S(1)}, bf16[1,1536,384]{2,1,0:T(8,128)(2,1)}, u32[]{:S(2)}) copy-start(bf16[1,1536,384]{2,1,0:T(8,128)(2,1)} %param.12) | copy-start | bytes 3538948
  49.8 46.3 %copy-start.10 = (bf16[1,384,1536]{2,1,0:T(8,128)(2,1)S(1)}, bf16[1,384,1536]{2,1,0:T(8,128)(2,1)}, u32[]{:S(2)}) copy-start(bf16[1,384,1536]{2,1,0:T(8,128)(2,1)} %param.13) | copy-start | bytes 3538948
  96.1 4.5 %copy-start = (bf16[16,24,3072]{2,1,0:T(8,128)(2,1)}, bf16[16,24,3072]{2,1,0:T(8,128)(2,1)S(1)}, u32[]{:S(2)}) copy-start(bf16[16,24,3072]{2,1,0:T(8,128)(2,1)S(1)} %all_to_all.15) | copy-start | bytes 7077892
  100.6 32.3 %all-to-all-start.1 = ((bf16[16,24,1664]{2,1,0:T(8,128)(2,1)}), bf16[16,24,1664]{2,1,0:T(8,128)(2,1)S(1)}, u32[]{:S(2)}, u32[]{:S(2)}) async-start(bf16[16,24,1664]{2,1,0:T(8,128)(2,1)} %bitcast.8), calls=%async_computation.1 | async-start | bytes 2555904 | tf_op jit(solution)/shard_map/all_to_all | solution.py:284
  106.7 1.7 %copy-start.1 = (bf16[16,24,3072]{2,1,0:T(8,128)(2,1)S(1)}, bf16[16,24,3072]{2,1,0:T(8,128)(2,1)}, u32[]{:S(2)}) copy-start(bf16[16,24,3072]{2,1,0:T(8,128)(2,1)} %copy-done) | copy-start | bytes 7077892
  111.6 1.2 copy-start.2
  112.8 7.9 %collective-permute-start = (bf16[4,288,768]{2,1,0:T(8,128)(2,1)}, bf16[4,288,768]{2,1,0:T(8,128)(2,1)}, u32[]{:S(2)}, u32[]{:S(2)}) collective-permute-start(bf16[4,288,768]{2,1,0:T(8,128)(2,1)} %get-tuple-element.27), channel_id=1, source_target_pairs={{0,64},{64,0},{1,65},{65,1},{2,66},{66,2},{3,67},{67,3},{4,68},{68... | collective-permute-start | bytes 5308424 | tf_op jit(solution)/shard_map/ppermute | solution.py:295
  120.8 1.5 copy-start.3
  134.5 30.9 %all-to-all-start.2 = ((bf16[4,32,1664]{2,1,0:T(8,128)(2,1)}), bf16[4,32,1664]{2,1,0:T(8,128)(2,1)S(1)}, u32[]{:S(2)}, u32[]{:S(2)}) async-start(bf16[4,32,1664]{2,1,0:T(8,128)(2,1)} %bitcast.12), calls=%async_computation.2 | async-start | bytes 851968 | tf_op jit(solution)/shard_map/all_to_all | solution.py:318
  141.7 15.2 %collective-permute-start.1 = (bf16[288,768]{1,0:T(8,128)(2,1)}, bf16[288,768]{1,0:T(8,128)(2,1)S(1)}, u32[]{:S(2)}, u32[]{:S(2)}) collective-permute-start(bf16[288,768]{1,0:T(8,128)(2,1)} %get-tuple-element.31), channel_id=1, source_target_pairs={{0,128},{128,256},{256,384},{384,0},{1,129},{129,257},{257,385},{3... | collective-permute-start | bytes 1327112 | tf_op jit(solution)/shard_map/ppermute | solution.py:306
  144.1 16.5 %collective-permute-start.2 = (bf16[288,768]{1,0:T(8,128)(2,1)S(1)}, bf16[288,768]{1,0:T(8,128)(2,1)S(1)}, u32[]{:S(2)}, u32[]{:S(2)}) collective-permute-start(bf16[288,768]{1,0:T(8,128)(2,1)S(1)} %get-tuple-element.32), channel_id=1, source_target_pairs={{0,256},{128,384},{256,0},{384,128},{1,257},{129,385},{257,1},{385... | collective-permute-start | bytes 1327112 | tf_op jit(solution)/shard_map/ppermute | solution.py:306
  148.4 17.1 %collective-permute-start.3 = (bf16[288,768]{1,0:T(8,128)(2,1)S(1)}, bf16[288,768]{1,0:T(8,128)(2,1)S(1)}, u32[]{:S(2)}, u32[]{:S(2)}) collective-permute-start(bf16[288,768]{1,0:T(8,128)(2,1)S(1)} %get-tuple-element.33), channel_id=1, source_target_pairs={{0,384},{128,0},{256,128},{384,256},{1,385},{129,1},{257,129},{385... | collective-permute-start | bytes 1327112 | tf_op jit(solution)/shard_map/ppermute | solution.py:306

commit v5 on v4

--- a/solution.py
+++ b/solution.py
@@ -159,11 +159,28 @@
             put(chip, share + side * down_share, part[chip * 2 * down_share : (chip + 1) * 2 * down_share])
 
 
-def chip_sum_kernel(chip_ref, keep_ref, got_ref, *out_refs):
-    chips = keep_ref.shape[0]
-    for s, out_ref in enumerate(out_refs):
+def chip_sum_kernel(chip_ref, keep_ref, got_ref, own_ref, right_ref, left_ref, far_low_ref, far_high_ref):
+    chips, part_rows, _ = keep_ref.shape
+    half = part_rows // 2
+
+    def total(s, low, size):
         chip = (chip_ref[0] + s) & (chips - 1)
-        out_ref[...] = (keep_ref[chip].astype(F32) + got_ref[chip].astype(F32)).astype(BF16)
+        rows = pl.ds(low, size)
+        return (keep_ref[chip, rows].astype(F32) + got_ref[chip, rows].astype(F32)).astype(BF16)
+
+    far_low_ref[...] = total(2, 0, half)
+    far_high_ref[...] = total(2, half, half)
+    own_ref[...] = total(0, 0, part_rows)
+    right_ref[...] = total(1, 0, part_rows)
+    left_ref[...] = total(3, 0, part_rows)
+
+
+def relay_kernel(right_ref, left_ref, low_ref, high_ref, to_right_ref, to_left_ref):
+    half = low_ref.shape[0]
+    to_right_ref[:half] = (right_ref[:half].astype(F32) + low_ref[...].astype(F32)).astype(BF16)
+    to_right_ref[half:] = right_ref[half:]
+    to_left_ref[:half] = left_ref[:half]
+    to_left_ref[half:] = (left_ref[half:].astype(F32) + high_ref[...].astype(F32)).astype(BF16)
 
 
 def combine_kernel(base_ref, back_ref, pick_ref, extra_ref, sum_ref):
@@ -249,7 +266,7 @@
         in_specs=[pl.BlockSpec(memory_space=pltpu.HBM)] * 3 + whole(1),
         out_specs=whole(1)[0],
         scratch_shapes=[pltpu.VMEM((TOP, block), jnp.int32), pltpu.SemaphoreType.DMA((3,))],
-        compiler_params=params(8),
+        compiler_params=params(60),
         name="pack_tokens",
     )(layer_in, grad_out, expert_ids.T, gate_probs.T)
     near_tokens = lax.all_gather(packed, "far", tiled=True)
@@ -293,20 +310,30 @@
         name="weight_parts",
     )(core.reshape(1), rows, both, hidden)
     got = lax.ppermute(give, "core", [(0, 1), (1, 0)])
-    chip_sums = pl.pallas_call(
+    share_shape, half_shape = shape(part_rows, 2 * hidden_width), shape(part_rows // 2, 2 * hidden_width)
+    own, right, left, far_low, far_high = pl.pallas_call(
         chip_sum_kernel,
-        out_shape=(shape(part_rows, 2 * hidden_width),) * chips,
+        out_shape=(share_shape,) * 3 + (half_shape,) * 2,
         in_specs=[scalar] + whole(2),
-        out_specs=tuple(whole(chips)),
+        out_specs=tuple(whole(5)),
         compiler_params=params(16),
         cost_estimate=cost(MIB, 6 * MIB),
         name="chip_sums",
     )(chip.reshape(1), keep, got)
-    parts = [chip_sums[0]] + [
-        lax.ppermute(chip_sums[s], "x", [(i, (i + s) % chips) for i in range(chips)]) for s in range(1, chips)
-    ]
-
-    back, _ = lax.optimization_barrier((back, chip_sums[0]))
+    to_right = [(i, (i + 1) % chips) for i in range(chips)]
+    to_left = [(i, (i - 1) % chips) for i in range(chips)]
+    right, left = pl.pallas_call(
+        relay_kernel,
+        out_shape=(share_shape,) * 2,
+        in_specs=whole(4),
+        out_specs=tuple(whole(2)),
+        compiler_params=params(8),
+        cost_estimate=cost(MIB, 2 * MIB),
+        name="relay_sums",
+    )(right, left, lax.ppermute(far_low, "x", to_right), lax.ppermute(far_high, "x", to_left))
+    parts = [own, lax.ppermute(right, "x", to_right), lax.ppermute(left, "x", to_left)]
+
+    back, _ = lax.optimization_barrier((back, right))
     sums = pl.pallas_call(
         combine_kernel,
         out_shape=shape(tokens, width + LANES),
@@ -326,7 +353,7 @@
             jax.ShapeDtypeStruct((share, hidden_width), F32),
             jax.ShapeDtypeStruct((down_share, width), F32),
         ),
-        in_specs=whole(1 + chips),
+        in_specs=whole(1 + len(parts)),
         out_specs=tuple(whole(5)),
         compiler_params=params(24),
         name="finish",

time: 169 us -> 170 us (level)
  starting transfers between devices: 26.1 us -> 29.7 us
  local copies, waits for them, and re-layouts: 7.56 us -> 4.39 us
    all_to_all x1, waiting for transfers between devices: 8.1 us -> 0.01 us  [per_device(): near_exchange(back.reshape(NEAR, FAR * CAP, width + LANES))]
    all_to_all x1, waiting for transfers between devices: 0.01 us -> 6.43 us  [per_device(): sums = exchange(sums.reshape(FAR, block, width + LANES), 'far')]
    ppermute x3 -> x4, starting transfers between devices: 8.62 us -> 12.9 us  [the longest x1 4.8 us: per_device(): lax.ppermute(right, 'x', to_right)]
    unnamed x22 -> x14, local copies, waits for them, and re-layouts: 7.55 us -> 4.39 us
    pallas_call x1, Pallas kernels: 0.26 us -> 2.34 us  [per_device(): pl.pallas_call(pack_kernel, out_shape=shape(block, 2 * width + LANES), in...]
    ppermute x3 -> x4, waiting for transfers between devices: 15.1 us -> 15.3 us  [the longest x1 7.07 us: per_device(): lax.ppermute(left, 'x', to_left)]
  transfers between devices with their start and end apart: 6 -> 7, of which waited for: 5 -> 6; matrix products, arithmetic and copies ran while one was open for 0% -> 0% of each run, Pallas kernels for 3% -> 3%
where the time goes in v5:
time: 170 us; the launch traced here: 167 us
  blocking collectives  90.8 us (53%)
  starting transfers between devices  29.7 us (17%)
  waiting for transfers between devices  25.4 us (15%)
  Pallas kernels  16.2 us (10%)
  local copies, waits for them, and re-layouts  4.39 us (3%)
    all_to_all x1, blocking collectives, per_device(): near_exchange(send.reshape(NEAR, FAR * CAP, 2 * width))  46.3 us
    all_gather x1, blocking collectives, per_device(): near_tokens = lax.all_gather(packed, 'far', tiled=True)  44.5 us
    ppermute x1, waiting for transfers between devices, per_device(): lax.ppermute(left, 'x', to_left)  7.07 us
    all_to_all x1, starting transfers between devices, per_device(): sums = exchange(sums.reshape(FAR, block, width + LANES), 'far')  6.45 us
    all_to_all x1, waiting for transfers between devices, per_device(): sums = exchange(sums.reshape(FAR, block, width + LANES), 'far')  6.43 us
    all_to_all x1, starting transfers between devices, per_device(): near_exchange(back.reshape(NEAR, FAR * CAP, width + LANES))  6.02 us
    ppermute x1, starting transfers between devices, per_device(): lax.ppermute(right, 'x', to_right)  4.8 us
    pallas_call x1, Pallas kernels, per_device(): pl.pallas_call(expert_kernel, out_shape=(shape(slots, width + LANES), sha...  4.49 us
  transfers between devices with their start and end apart: 7, of which 6 were waited for; matrix products, arithmetic and copies ran while one was open for 0% of the time, Pallas kernels for 3%

profile of v5, /device:TPU:6, one launch (start us, length us, event | category | flops | bytes accessed | tf_op | source)
XLA Modules:
  0.0 167.2 jit_solution(2514406063349499710)
XLA Ops:
  0.6 2.3 %pack_tokens.1 = bf16[32,3200]{1,0:T(8,128)(2,1)} custom-call(bf16[32,1536]{1,0:T(8,128)(2,1)} %layer_ref.1, bf16[32,1536]{1,0:T(8,128)(2,1)} %grad_ref.1, s32[8,32]{1,0:T(8,128)} %bitcast.24, bf16[8,32]{1,0:T(8,128)(2,1)} %bitcast.25), custom_call_target="tpu_custom_call" | custom-call | tf_op jit(solution)/shard_map/pack_tokens/pallas_call | solution.py:263
  3.0 44.5 %all_gather.3.tok_ref = bf16[128,3200]{1,0:T(8,128)(2,1)S(1)} all-gather(bf16[32,3200]{1,0:T(8,128)(2,1)} %pack_tokens.1), channel_id=1, replica_groups=mesh['x'=4,'core'=2,'far'=4,'near'=4,'y'=4] {'far'}, dimensions={0}, use_global_device_ids=true | all-gather | bytes 1024000 | tf_op jit(solution)/shard_map/all_gather | solution.py:272
  47.5 1.5 select_rows.1
  48.9 0.0 copy-start.4
  48.9 0.0 copy-start.5
  49.0 0.0 copy-start.6
  49.0 46.3 %all_to_all.15 = bf16[16,24,3072]{2,1,0:T(8,128)(2,1)S(1)} all-to-all(bf16[16,24,3072]{2,1,0:T(8,128)(2,1)S(1)} %bitcast.20), channel_id=1, replica_groups={{0,1,2,3,4,5,6,7,8,9,10,11,12,13,14,15},{16,17,18,19,20,21,22,23,24,25,..., dimensions={0} | all-to-all | bytes 4718592 | tf_op jit(solution)/shard_map/all_to_all | solution.py:289
  95.3 0.0 copy-start
  95.3 0.0 copy-done.4
  95.3 0.0 copy-done.5
  95.3 0.0 copy-done.6
  95.3 4.5 %expert_rows.1 = (bf16[384,1664]{1,0:T(8,128)(2,1)}, bf16[384,768]{1,0:T(8,128)(2,1)S(1)}, bf16[384,384]{1,0:T(8,128)(2,1)S(1)}) custom-call(bf16[384,3072]{1,0:T(8,128)(2,1)S(1)} %bitcast.18, bf16[1536,384]{1,0:T(8,128)(2,1)S(1)} %bitcast.21, bf16[1536,384]{1,0:T(8,128)(2,1)S(1)} %bitcast.22, bf16[384,1536]{1,0:T(8,128)(2,1)S(1)} %bitcast.23), custom_call_target="tpu_custom_call" | custom-call | flops 2264924160 | bytes 8388608 | tf_op jit(solution)/shard_map/expert_rows/pallas_call | solution.py:292
  99.8 0.0 copy-done
  99.8 6.0 %all-to-all-start.1 = ((bf16[16,24,1664]{2,1,0:T(8,128)(2,1)}), bf16[16,24,1664]{2,1,0:T(8,128)(2,1)S(1)}, u32[]{:S(2)}, u32[]{:S(2)}) async-start(bf16[16,24,1664]{2,1,0:T(8,128)(2,1)} %bitcast.8), calls=%async_computation.1 | async-start | bytes 2555904 | tf_op jit(solution)/shard_map/all_to_all | solution.py:301
  105.8 0.0 copy-start.1
  105.8 1.7 copy-done.1
  107.5 3.3 %weight_parts.1 = (bf16[4,288,768]{2,1,0:T(8,128)(2,1)S(1)}, bf16[4,288,768]{2,1,0:T(8,128)(2,1)}) custom-call(s32[1]{0:T(128)} %bitcast.11.core_ref, bf16[384,3072]{1,0:T(8,128)(2,1)S(1)} %bitcast.19, bf16[384,768]{1,0:T(8,128)(2,1)S(1)} %get-tuple-element.27.both_ref, bf16[384,384]{1,0:T(8,128)(2,1)S(1)} %get-tuple-element.28.hidden_ref), custom_call_target="tpu_custom_call" | custom-call | flops 1358954496 | bytes 8388608 | tf_op jit(solution)/shard_map/weight_parts/pallas_call | solution.py:303
  110.8 0.0 copy-start.2
  110.8 1.2 copy-done.2
  112.0 4.3 %collective-permute-start = (bf16[4,288,768]{2,1,0:T(8,128)(2,1)}, bf16[4,288,768]{2,1,0:T(8,128)(2,1)}, u32[]{:S(2)}, u32[]{:S(2)}) collective-permute-start(bf16[4,288,768]{2,1,0:T(8,128)(2,1)} %get-tuple-element.30), channel_id=1, source_target_pairs={{0,64},{64,0},{1,65},{65,1},{2,66},{66,2},{3,67},{67,3},{4,68},{68... | collective-permute-start | bytes 5308424 | tf_op jit(solution)/shard_map/ppermute | solution.py:312
  116.3 3.6 %collective-permute-done.got_ref = bf16[4,288,768]{2,1,0:T(8,128)(2,1)} collective-permute-done((bf16[4,288,768]{2,1,0:T(8,128)(2,1)}, bf16[4,288,768]{2,1,0:T(8,128)(2,1)}, u32[]{:S(2)}, u32[]{:S(2)}) %collective-permute-start) | collective-permute-done | bytes 1769504 | tf_op jit(solution)/shard_map/ppermute | solution.py:312
  119.9 0.0 copy-start.3
  119.9 1.5 copy-done.3
  121.4 1.9 %chip_sums.1 = (bf16[288,768]{1,0:T(8,128)(2,1)S(1)}, bf16[288,768]{1,0:T(8,128)(2,1)S(1)}, bf16[288,768]{1,0:T(8,128)(2,1)S(1)}, bf16[144,768]{1,0:T(8,128)(2,1)S(1)}, bf16[144,768]{1,0:T(8,128)(2,1)S(1)}) custom-call(s32[1]{0:T(128)} %bitcast.10.chip_ref, bf16[4,288,768]{2,1,0:T(8,128)(2,1)S(1)} %copy-done.3, bf16[4,288,768]{2,1,0:T(8,128)(2,1)} %collective-permute-done.got_ref), custom_call_target="tpu_custom_call" | custom-call | flops 1048576 | bytes 6291456 | tf_op jit(solution)/shard_map/chip_sums/pallas_call | solution.py:314
  123.3 2.4 %collective-permute-start.1 = (bf16[144,768]{1,0:T(8,128)(2,1)S(1)}, bf16[144,768]{1,0:T(8,128)(2,1)S(1)}, u32[]{:S(2)}, u32[]{:S(2)}) collective-permute-start(bf16[144,768]{1,0:T(8,128)(2,1)S(1)} %get-tuple-element.33), channel_id=1, source_target_pairs={{0,128},{128,256},{256,384},{384,0},{1,129},{129,257},{257,385},{3... | collective-permute-start | bytes 663560 | tf_op jit(solution)/shard_map/ppermute | solution.py:333
  125.7 3.5 %collective-permute-start.2 = (bf16[144,768]{1,0:T(8,128)(2,1)S(1)}, bf16[144,768]{1,0:T(8,128)(2,1)S(1)}, u32[]{:S(2)}, u32[]{:S(2)}) collective-permute-start(bf16[144,768]{1,0:T(8,128)(2,1)S(1)} %get-tuple-element.34), channel_id=1, source_target_pairs={{0,384},{128,0},{256,128},{384,256},{1,385},{129,1},{257,129},{385... | collective-permute-start | bytes 663560 | tf_op jit(solution)/shard_map/ppermute | solution.py:333
  129.2 3.7 %collective-permute-done.1.low_ref = bf16[144,768]{1,0:T(8,128)(2,1)S(1)} collective-permute-done((bf16[144,768]{1,0:T(8,128)(2,1)S(1)}, bf16[144,768]{1,0:T(8,128)(2,1)S(1)}, u32[]{:S(2)}, u32[]{:S(2)}) %collective-permute-start.1) | collective-permute-done | bytes 221216 | tf_op jit(solution)/shard_map/ppermute | solution.py:333
  132.9 3.3 %collective-permute-done.2.high_ref = bf16[144,768]{1,0:T(8,128)(2,1)S(1)} collective-permute-done((bf16[144,768]{1,0:T(8,128)(2,1)S(1)}, bf16[144,768]{1,0:T(8,128)(2,1)S(1)}, u32[]{:S(2)}, u32[]{:S(2)}) %collective-permute-start.2) | collective-permute-done | bytes 221216 | tf_op jit(solution)/shard_map/ppermute | solution.py:333
  136.2 0.1 relay_sums.1
  136.3 0.0 all-to-all-done.1
  136.4 1.6 combine_rows.1
  138.0 6.4 %all-to-all-start.2 = ((bf16[4,32,1664]{2,1,0:T(8,128)(2,1)}), bf16[4,32,1664]{2,1,0:T(8,128)(2,1)S(1)}, u32[]{:S(2)}, u32[]{:S(2)}) async-start(bf16[4,32,1664]{2,1,0:T(8,128)(2,1)} %bitcast.12), calls=%async_computation.2 | async-start | bytes 851968 | tf_op jit(solution)/shard_map/all_to_all | solution.py:345
  144.4 2.2 %collective-permute-start.4 = (bf16[288,768]{1,0:T(8,128)(2,1)S(1)}, bf16[288,768]{1,0:T(8,128)(2,1)S(1)}, u32[]{:S(2)}, u32[]{:S(2)}) collective-permute-start(bf16[288,768]{1,0:T(8,128)(2,1)S(1)} %get-tuple-element.39), channel_id=1, source_target_pairs={{0,384},{128,0},{256,128},{384,256},{1,385},{129,1},{257,129},{385... | collective-permute-start | bytes 1327112 | tf_op jit(solution)/shard_map/ppermute | solution.py:334
  146.7 4.8 %collective-permute-start.3 = (bf16[288,768]{1,0:T(8,128)(2,1)S(1)}, bf16[288,768]{1,0:T(8,128)(2,1)S(1)}, u32[]{:S(2)}, u32[]{:S(2)}) collective-permute-start(bf16[288,768]{1,0:T(8,128)(2,1)S(1)} %get-tuple-element.35), channel_id=1, source_target_pairs={{0,128},{128,256},{256,384},{384,0},{1,129},{129,257},{257,385},{3... | collective-permute-start | bytes 1327112 | tf_op jit(solution)/shard_map/ppermute | solution.py:334
  151.5 7.1 %collective-permute-done.4.refs_3_ = bf16[288,768]{1,0:T(8,128)(2,1)S(1)} collective-permute-done((bf16[288,768]{1,0:T(8,128)(2,1)S(1)}, bf16[288,768]{1,0:T(8,128)(2,1)S(1)}, u32[]{:S(2)}, u32[]{:S(2)}) %collective-permute-start.4) | collective-permute-done | bytes 442400 | tf_op jit(solution)/shard_map/ppermute | solution.py:334
  158.6 1.2 collective-permute-done.3.refs_2_
  159.7 6.4 %all-to-all-done.2.refs_0_ = bf16[4,32,1664]{2,1,0:T(8,128)(2,1)S(1)} async-done(((bf16[4,32,1664]{2,1,0:T(8,128)(2,1)}), bf16[4,32,1664]{2,1,0:T(8,128)(2,1)S(1)}, u32[]{:S(2)}, u32[]{:S(2)}) %all-to-all-start.2) | async-done | bytes 426016 | tf_op jit(solution)/shard_map/all_to_all | solution.py:345
  166.2 1.1 finish.1
  (1 shorter events, 0.0 us)
Async XLA Ops:
  48.9 46.3 %copy-start.4 = (bf16[1,1536,384]{2,1,0:T(8,128)(2,1)S(1)}, bf16[1,1536,384]{2,1,0:T(8,128)(2,1)}, u32[]{:S(2)}) copy-start(bf16[1,1536,384]{2,1,0:T(8,128)(2,1)} %param.11) | copy-start | bytes 3538948
  48.9 46.3 %copy-start.5 = (bf16[1,1536,384]{2,1,0:T(8,128)(2,1)S(1)}, bf16[1,1536,384]{2,1,0:T(8,128)(2,1)}, u32[]{:S(2)}) copy-start(bf16[1,1536,384]{2,1,0:T(8,128)(2,1)} %param.12) | copy-start | bytes 3538948
  49.0 46.3 %copy-start.6 = (bf16[1,384,1536]{2,1,0:T(8,128)(2,1)S(1)}, bf16[1,384,1536]{2,1,0:T(8,128)(2,1)}, u32[]{:S(2)}) copy-start(bf16[1,384,1536]{2,1,0:T(8,128)(2,1)} %param.13) | copy-start | bytes 3538948
  95.3 4.5 %copy-start = (bf16[16,24,3072]{2,1,0:T(8,128)(2,1)}, bf16[16,24,3072]{2,1,0:T(8,128)(2,1)S(1)}, u32[]{:S(2)}) copy-start(bf16[16,24,3072]{2,1,0:T(8,128)(2,1)S(1)} %all_to_all.15) | copy-start | bytes 7077892
  99.8 36.6 %all-to-all-start.1 = ((bf16[16,24,1664]{2,1,0:T(8,128)(2,1)}), bf16[16,24,1664]{2,1,0:T(8,128)(2,1)S(1)}, u32[]{:S(2)}, u32[]{:S(2)}) async-start(bf16[16,24,1664]{2,1,0:T(8,128)(2,1)} %bitcast.8), calls=%async_computation.1 | async-start | bytes 2555904 | tf_op jit(solution)/shard_map/all_to_all | solution.py:301
  105.8 1.7 copy-start.1
  110.8 1.2 copy-start.2
  112.0 7.9 %collective-permute-start = (bf16[4,288,768]{2,1,0:T(8,128)(2,1)}, bf16[4,288,768]{2,1,0:T(8,128)(2,1)}, u32[]{:S(2)}, u32[]{:S(2)}) collective-permute-start(bf16[4,288,768]{2,1,0:T(8,128)(2,1)} %get-tuple-element.30), channel_id=1, source_target_pairs={{0,64},{64,0},{1,65},{65,1},{2,66},{66,2},{3,67},{67,3},{4,68},{68... | collective-permute-start | bytes 5308424 | tf_op jit(solution)/shard_map/ppermute | solution.py:312
  119.9 1.5 copy-start.3
  123.3 9.6 %collective-permute-start.1 = (bf16[144,768]{1,0:T(8,128)(2,1)S(1)}, bf16[144,768]{1,0:T(8,128)(2,1)S(1)}, u32[]{:S(2)}, u32[]{:S(2)}) collective-permute-start(bf16[144,768]{1,0:T(8,128)(2,1)S(1)} %get-tuple-element.33), channel_id=1, source_target_pairs={{0,128},{128,256},{256,384},{384,0},{1,129},{129,257},{257,385},{3... | collective-permute-start | bytes 663560 | tf_op jit(solution)/shard_map/ppermute | solution.py:333
  125.7 10.5 %collective-permute-start.2 = (bf16[144,768]{1,0:T(8,128)(2,1)S(1)}, bf16[144,768]{1,0:T(8,128)(2,1)S(1)}, u32[]{:S(2)}, u32[]{:S(2)}) collective-permute-start(bf16[144,768]{1,0:T(8,128)(2,1)S(1)} %get-tuple-element.34), channel_id=1, source_target_pairs={{0,384},{128,0},{256,128},{384,256},{1,385},{129,1},{257,129},{385... | collective-permute-start | bytes 663560 | tf_op jit(solution)/shard_map/ppermute | solution.py:333
  138.0 28.2 %all-to-all-start.2 = ((bf16[4,32,1664]{2,1,0:T(8,128)(2,1)}), bf16[4,32,1664]{2,1,0:T(8,128)(2,1)S(1)}, u32[]{:S(2)}, u32[]{:S(2)}) async-start(bf16[4,32,1664]{2,1,0:T(8,128)(2,1)} %bitcast.12), calls=%async_computation.2 | async-start | bytes 851968 | tf_op jit(solution)/shard_map/all_to_all | solution.py:345
  144.4 14.1 %collective-permute-start.4 = (bf16[288,768]{1,0:T(8,128)(2,1)S(1)}, bf16[288,768]{1,0:T(8,128)(2,1)S(1)}, u32[]{:S(2)}, u32[]{:S(2)}) collective-permute-start(bf16[288,768]{1,0:T(8,128)(2,1)S(1)} %get-tuple-element.39), channel_id=1, source_target_pairs={{0,384},{128,0},{256,128},{384,256},{1,385},{129,1},{257,129},{385... | collective-permute-start | bytes 1327112 | tf_op jit(solution)/shard_map/ppermute | solution.py:334
  146.7 13.1 %collective-permute-start.3 = (bf16[288,768]{1,0:T(8,128)(2,1)S(1)}, bf16[288,768]{1,0:T(8,128)(2,1)S(1)}, u32[]{:S(2)}, u32[]{:S(2)}) collective-permute-start(bf16[288,768]{1,0:T(8,128)(2,1)S(1)} %get-tuple-element.35), channel_id=1, source_target_pairs={{0,128},{128,256},{256,384},{384,0},{1,129},{129,257},{257,385},{3... | collective-permute-start | bytes 1327112 | tf_op jit(solution)/shard_map/ppermute | solution.py:334

commit v6 on v5

--- a/solution.py
+++ b/solution.py
@@ -134,45 +134,73 @@
     hidden_ref[...] = hidden
 
 
-def part_kernel(core_ref, rows_ref, both_ref, hidden_ref, keep_ref, give_ref):
-    chips, part_rows, columns = keep_ref.shape
+def part_kernel(core_ref, rows_hbm, both_ref, hidden_ref, keep_hbm, give_hbm, rows, keep, give, in_sems, out_sems):
+    chips, part_rows, columns = keep.shape
     hidden_width = hidden_ref.shape[1]
-    width = rows_ref.shape[1] // 2
+    width = rows.shape[1] // 2
     share = width // (2 * chips)
     down_share = hidden_width // (2 * chips)
+    half = width // 2
     first = core_ref[0] == 0
+
+    spans = [(width + side * half, half) for side in range(2)]
+    spans += [(chip * 2 * share, 2 * share) for chip in range(chips)]
+    loads = [
+        pltpu.make_async_copy(rows_hbm.at[:, pl.ds(*span)], rows.at[:, pl.ds(*span)], in_sems.at[i])
+        for i, span in enumerate(spans)
+    ]
+    for load in loads:
+        load.start()
 
     def put(chip, low, pair):
         size = pair.shape[0] // 2
-        keep_ref[chip, low : low + size, :] = jnp.where(first, pair[:size], pair[size:]).astype(BF16)
-        give_ref[chip, low : low + size, :] = jnp.where(first, pair[size:], pair[:size]).astype(BF16)
-
-    both = both_ref[...]
-    for chip in range(chips):
-        rows = rows_ref[:, chip * 2 * share : (chip + 1) * 2 * share]
-        put(chip, 0, dot(rows, both, ((0,), (0,))))
+        keep[chip, low : low + size, :] = jnp.where(first, pair[:size], pair[size:]).astype(BF16)
+        give[chip, low : low + size, :] = jnp.where(first, pair[size:], pair[:size]).astype(BF16)
+
     hidden = hidden_ref[...]
-    half = width // 2
     for side in range(2):
-        part = dot(hidden, rows_ref[:, width + side * half : width + (side + 1) * half], ((0,), (0,)))
+        loads[side].wait()
+        part = dot(hidden, rows[:, width + side * half : width + (side + 1) * half], ((0,), (0,)))
         for chip in range(chips):
             put(chip, share + side * down_share, part[chip * 2 * down_share : (chip + 1) * 2 * down_share])
-
-
-def chip_sum_kernel(chip_ref, keep_ref, got_ref, own_ref, right_ref, left_ref, far_low_ref, far_high_ref):
-    chips, part_rows, _ = keep_ref.shape
+    both = both_ref[...]
+    stores = []
+    for chip in range(chips):
+        loads[2 + chip].wait()
+        put(chip, 0, dot(rows[:, chip * 2 * share : (chip + 1) * 2 * share], both, ((0,), (0,))))
+        stores.append(pltpu.make_async_copy(give.at[chip], give_hbm.at[chip], out_sems.at[2 * chip]))
+        stores.append(pltpu.make_async_copy(keep.at[chip], keep_hbm.at[chip], out_sems.at[2 * chip + 1]))
+        stores[-2].start()
+        stores[-1].start()
+    for store in stores:
+        store.wait()
+
+
+def chip_sum_kernel(
+    chip_ref, keep_hbm, got_hbm, own_ref, right_ref, left_ref, far_low_ref, far_high_ref, keep, got, sems
+):
+    chips, part_rows, _ = keep.shape
     half = part_rows // 2
+    loads = []
+    for s in (2, 1, 3, 0):
+        chip = (chip_ref[0] + s) & (chips - 1)
+        loads.append(pltpu.make_async_copy(keep_hbm.at[chip], keep.at[s], sems.at[2 * s]))
+        loads.append(pltpu.make_async_copy(got_hbm.at[chip], got.at[s], sems.at[2 * s + 1]))
+    for load in loads:
+        load.start()
 
     def total(s, low, size):
-        chip = (chip_ref[0] + s) & (chips - 1)
         rows = pl.ds(low, size)
-        return (keep_ref[chip, rows].astype(F32) + got_ref[chip, rows].astype(F32)).astype(BF16)
-
+        return (keep[s, rows].astype(F32) + got[s, rows].astype(F32)).astype(BF16)
+
+    loads[0].wait()
+    loads[1].wait()
     far_low_ref[...] = total(2, 0, half)
     far_high_ref[...] = total(2, half, half)
-    own_ref[...] = total(0, 0, part_rows)
-    right_ref[...] = total(1, 0, part_rows)
-    left_ref[...] = total(3, 0, part_rows)
+    for i, (s, ref) in enumerate(((1, right_ref), (3, left_ref), (0, own_ref))):
+        loads[2 * i + 2].wait()
+        loads[2 * i + 3].wait()
+        ref[...] = total(s, 0, part_rows)
 
 
 def relay_kernel(right_ref, left_ref, low_ref, high_ref, to_right_ref, to_left_ref):
@@ -256,6 +284,7 @@
     place = lax.axis_index(("far", "near", "y")) - moved + EXPERTS
     base = ((place & -NEAR) + moved).astype(jnp.int32).reshape(1)
     scalar = pl.BlockSpec(memory_space=pltpu.SMEM)
+    hbm = pl.BlockSpec(memory_space=pltpu.HBM)
 
     def shape(*dims):
         return jax.ShapeDtypeStruct(dims, BF16)
@@ -263,7 +292,7 @@
     packed = pl.pallas_call(
         pack_kernel,
         out_shape=shape(block, 2 * width + LANES),
-        in_specs=[pl.BlockSpec(memory_space=pltpu.HBM)] * 3 + whole(1),
+        in_specs=[hbm] * 3 + whole(1),
         out_specs=whole(1)[0],
         scratch_shapes=[pltpu.VMEM((TOP, block), jnp.int32), pltpu.SemaphoreType.DMA((3,))],
         compiler_params=params(60),
@@ -303,9 +332,16 @@
     keep, give = pl.pallas_call(
         part_kernel,
         out_shape=(shape(chips, part_rows, 2 * hidden_width),) * 2,
-        in_specs=[scalar] + whole(3),
-        out_specs=tuple(whole(2)),
-        compiler_params=params(32),
+        in_specs=[scalar, hbm] + whole(2),
+        out_specs=(hbm, hbm),
+        scratch_shapes=[
+            pltpu.VMEM((slots, 2 * width), BF16),
+            pltpu.VMEM((chips, part_rows, 2 * hidden_width), BF16),
+            pltpu.VMEM((chips, part_rows, 2 * hidden_width), BF16),
+            pltpu.SemaphoreType.DMA((chips + 2,)),
+            pltpu.SemaphoreType.DMA((2 * chips,)),
+        ],
+        compiler_params=params(52),
         cost_estimate=cost(3 * matmul, 8 * MIB),
         name="weight_parts",
     )(core.reshape(1), rows, both, hidden)
@@ -314,9 +350,14 @@
     own, right, left, far_low, far_high = pl.pallas_call(
         chip_sum_kernel,
         out_shape=(share_shape,) * 3 + (half_shape,) * 2,
-        in_specs=[scalar] + whole(2),
+        in_specs=[scalar, hbm, hbm],
         out_specs=tuple(whole(5)),
-        compiler_params=params(16),
+        scratch_shapes=[
+            pltpu.VMEM((chips, part_rows, 2 * hidden_width), BF16),
+            pltpu.VMEM((chips, part_rows, 2 * hidden_width), BF16),
+            pltpu.SemaphoreType.DMA((2 * chips,)),
+        ],
+        compiler_params=params(52),
         cost_estimate=cost(MIB, 6 * MIB),
         name="chip_sums",
     )(chip.reshape(1), keep, got)

time: 170 us -> 170 us (level)
  the two profiles are of different devices: /device:TPU:6 before, /device:TPU:39 now
where the time goes in v6:
time: 170 us; the launch traced here: 169 us
  blocking collectives  89.3 us (53%)
  waiting for transfers between devices  30.6 us (18%)
  starting transfers between devices  29.5 us (17%)
  Pallas kernels  19 us (11%)
    all_to_all x1, blocking collectives, per_device(): near_exchange(send.reshape(NEAR, FAR * CAP, 2 * width))  53.8 us
    all_gather x1, blocking collectives, per_device(): near_tokens = lax.all_gather(packed, 'far', tiled=True)  35.4 us
    all_to_all x1, waiting for transfers between devices, per_device(): sums = exchange(sums.reshape(FAR, block, width + LANES), 'far')  12.5 us
    all_to_all x1, starting transfers between devices, per_device(): near_exchange(back.reshape(NEAR, FAR * CAP, width + LANES))  9.65 us
    ppermute x1, waiting for transfers between devices, per_device(): lax.ppermute(left, 'x', to_left)  6.72 us
    all_to_all x1, starting transfers between devices, per_device(): sums = exchange(sums.reshape(FAR, block, width + LANES), 'far')  6.17 us
    pallas_call x1, Pallas kernels, per_device(): pl.pallas_call(part_kernel, out_shape=(shape(chips, part_rows, 2 * hidden...  5.76 us
    ppermute x1, starting transfers between devices, per_device(): lax.ppermute(right, 'x', to_right)  4.54 us
  transfers between devices with their start and end apart: 7, of which 6 were waited for; matrix products, arithmetic and copies ran while one was open for 0% of the time, Pallas kernels for 5%

profile of v6, /device:TPU:39, one launch (start us, length us, event | category | flops | bytes accessed | tf_op | source)
XLA Modules:
  0.0 169.2 jit_solution(8340673645103474532)
XLA Ops:
  0.6 2.3 %pack_tokens.1 = bf16[32,3200]{1,0:T(8,128)(2,1)} custom-call(bf16[32,1536]{1,0:T(8,128)(2,1)} %layer_ref.1, bf16[32,1536]{1,0:T(8,128)(2,1)} %grad_ref.1, s32[8,32]{1,0:T(8,128)} %bitcast.24, bf16[8,32]{1,0:T(8,128)(2,1)} %bitcast.25), custom_call_target="tpu_custom_call" | custom-call | tf_op jit(solution)/shard_map/pack_tokens/pallas_call | solution.py:292
  3.0 35.4 %all_gather.3.tok_ref = bf16[128,3200]{1,0:T(8,128)(2,1)S(1)} all-gather(bf16[32,3200]{1,0:T(8,128)(2,1)} %pack_tokens.1), channel_id=1, replica_groups=mesh['x'=4,'core'=2,'far'=4,'near'=4,'y'=4] {'far'}, dimensions={0}, use_global_device_ids=true | all-gather | bytes 1024000 | tf_op jit(solution)/shard_map/all_gather | solution.py:301
  38.4 1.5 select_rows.1
  39.9 0.0 copy-start.1
  39.9 0.0 copy-start.2
  39.9 0.0 copy-start.3
  39.9 53.8 %all_to_all.15 = bf16[16,24,3072]{2,1,0:T(8,128)(2,1)S(1)} all-to-all(bf16[16,24,3072]{2,1,0:T(8,128)(2,1)S(1)} %bitcast.20), channel_id=1, replica_groups={{0,1,2,3,4,5,6,7,8,9,10,11,12,13,14,15},{16,17,18,19,20,21,22,23,24,25,..., dimensions={0} | all-to-all | bytes 4718592 | tf_op jit(solution)/shard_map/all_to_all | solution.py:318
  93.8 0.0 copy-start
  93.8 0.0 copy-done.1
  93.8 0.0 copy-done.2
  93.8 0.0 copy-done.3
  93.8 4.5 %expert_rows.1 = (bf16[384,1664]{1,0:T(8,128)(2,1)}, bf16[384,768]{1,0:T(8,128)(2,1)S(1)}, bf16[384,384]{1,0:T(8,128)(2,1)S(1)}) custom-call(bf16[384,3072]{1,0:T(8,128)(2,1)S(1)} %bitcast.18, bf16[1536,384]{1,0:T(8,128)(2,1)S(1)} %bitcast.21, bf16[1536,384]{1,0:T(8,128)(2,1)S(1)} %bitcast.22, bf16[384,1536]{1,0:T(8,128)(2,1)S(1)} %bitcast.23), custom_call_target="tpu_custom_call" | custom-call | flops 2264924160 | bytes 8388608 | tf_op jit(solution)/shard_map/expert_rows/pallas_call | solution.py:321
  98.3 0.0 copy-done
  98.3 9.7 %all-to-all-start.1 = ((bf16[16,24,1664]{2,1,0:T(8,128)(2,1)}), bf16[16,24,1664]{2,1,0:T(8,128)(2,1)S(1)}, u32[]{:S(2)}, u32[]{:S(2)}) async-start(bf16[16,24,1664]{2,1,0:T(8,128)(2,1)} %bitcast.8), calls=%async_computation.1 | async-start | bytes 2555904 | tf_op jit(solution)/shard_map/all_to_all | solution.py:330
  107.9 5.8 %weight_parts.1 = (bf16[4,288,768]{2,1,0:T(8,128)(2,1)}, bf16[4,288,768]{2,1,0:T(8,128)(2,1)}) custom-call(s32[1]{0:T(128)} %bitcast.11.core_ref, bf16[384,3072]{1,0:T(8,128)(2,1)} %bitcast.19, bf16[384,768]{1,0:T(8,128)(2,1)S(1)} %get-tuple-element.27.both_ref, bf16[384,384]{1,0:T(8,128)(2,1)S(1)} %get-tuple-element.28.hidden_ref), custom_call_target="tpu_custom_call" | custom-call | flops 1358954496 | bytes 8388608 | tf_op jit(solution)/shard_map/weight_parts/pallas_call | solution.py:332
  113.7 1.9 %collective-permute-start = (bf16[4,288,768]{2,1,0:T(8,128)(2,1)}, bf16[4,288,768]{2,1,0:T(8,128)(2,1)}, u32[]{:S(2)}, u32[]{:S(2)}) collective-permute-start(bf16[4,288,768]{2,1,0:T(8,128)(2,1)} %get-tuple-element.30), channel_id=1, source_target_pairs={{0,64},{64,0},{1,65},{65,1},{2,66},{66,2},{3,67},{67,3},{4,68},{68... | collective-permute-start | bytes 5308424 | tf_op jit(solution)/shard_map/ppermute | solution.py:348
  115.6 4.0 %collective-permute-done.got_hbm = bf16[4,288,768]{2,1,0:T(8,128)(2,1)} collective-permute-done((bf16[4,288,768]{2,1,0:T(8,128)(2,1)}, bf16[4,288,768]{2,1,0:T(8,128)(2,1)}, u32[]{:S(2)}, u32[]{:S(2)}) %collective-permute-start) | collective-permute-done | bytes 1769504 | tf_op jit(solution)/shard_map/ppermute | solution.py:348
  119.6 2.1 %chip_sums.1 = (bf16[288,768]{1,0:T(8,128)(2,1)S(1)}, bf16[288,768]{1,0:T(8,128)(2,1)S(1)}, bf16[288,768]{1,0:T(8,128)(2,1)S(1)}, bf16[144,768]{1,0:T(8,128)(2,1)S(1)}, bf16[144,768]{1,0:T(8,128)(2,1)S(1)}) custom-call(s32[1]{0:T(128)} %bitcast.10.chip_ref, bf16[4,288,768]{2,1,0:T(8,128)(2,1)} %get-tuple-element.29.keep_hbm, ...), custom_call_target="tpu_custom_call" | custom-call | flops 1048576 | bytes 6291456 | tf_op jit(solution)/shard_map/chip_sums/pallas_call | solution.py:350
  121.8 2.1 %collective-permute-start.1 = (bf16[144,768]{1,0:T(8,128)(2,1)S(1)}, bf16[144,768]{1,0:T(8,128)(2,1)S(1)}, u32[]{:S(2)}, u32[]{:S(2)}) collective-permute-start(bf16[144,768]{1,0:T(8,128)(2,1)S(1)} %get-tuple-element.33), channel_id=1, source_target_pairs={{0,128},{128,256},{256,384},{384,0},{1,129},{129,257},{257,385},{3... | collective-permute-start | bytes 663560 | tf_op jit(solution)/shard_map/ppermute | solution.py:374
  123.9 3.2 %collective-permute-start.2 = (bf16[144,768]{1,0:T(8,128)(2,1)S(1)}, bf16[144,768]{1,0:T(8,128)(2,1)S(1)}, u32[]{:S(2)}, u32[]{:S(2)}) collective-permute-start(bf16[144,768]{1,0:T(8,128)(2,1)S(1)} %get-tuple-element.34), channel_id=1, source_target_pairs={{0,384},{128,0},{256,128},{384,256},{1,385},{129,1},{257,129},{385... | collective-permute-start | bytes 663560 | tf_op jit(solution)/shard_map/ppermute | solution.py:374
  127.1 3.5 %collective-permute-done.1.low_ref = bf16[144,768]{1,0:T(8,128)(2,1)S(1)} collective-permute-done((bf16[144,768]{1,0:T(8,128)(2,1)S(1)}, bf16[144,768]{1,0:T(8,128)(2,1)S(1)}, u32[]{:S(2)}, u32[]{:S(2)}) %collective-permute-start.1) | collective-permute-done | bytes 221216 | tf_op jit(solution)/shard_map/ppermute | solution.py:374
  130.5 3.0 %collective-permute-done.2.high_ref = bf16[144,768]{1,0:T(8,128)(2,1)S(1)} collective-permute-done((bf16[144,768]{1,0:T(8,128)(2,1)S(1)}, bf16[144,768]{1,0:T(8,128)(2,1)S(1)}, u32[]{:S(2)}, u32[]{:S(2)}) %collective-permute-start.2) | collective-permute-done | bytes 221216 | tf_op jit(solution)/shard_map/ppermute | solution.py:374
  133.5 0.1 relay_sums.1
  133.7 0.0 all-to-all-done.1
  133.7 1.7 combine_rows.1
  135.3 6.2 %all-to-all-start.2 = ((bf16[4,32,1664]{2,1,0:T(8,128)(2,1)}), bf16[4,32,1664]{2,1,0:T(8,128)(2,1)S(1)}, u32[]{:S(2)}, u32[]{:S(2)}) async-start(bf16[4,32,1664]{2,1,0:T(8,128)(2,1)} %bitcast.12), calls=%async_computation.2 | async-start | bytes 851968 | tf_op jit(solution)/shard_map/all_to_all | solution.py:386
  141.5 1.9 %collective-permute-start.4 = (bf16[288,768]{1,0:T(8,128)(2,1)S(1)}, bf16[288,768]{1,0:T(8,128)(2,1)S(1)}, u32[]{:S(2)}, u32[]{:S(2)}) collective-permute-start(bf16[288,768]{1,0:T(8,128)(2,1)S(1)} %get-tuple-element.39), channel_id=1, source_target_pairs={{0,384},{128,0},{256,128},{384,256},{1,385},{129,1},{257,129},{385... | collective-permute-start | bytes 1327112 | tf_op jit(solution)/shard_map/ppermute | solution.py:375
  143.5 4.5 %collective-permute-start.3 = (bf16[288,768]{1,0:T(8,128)(2,1)S(1)}, bf16[288,768]{1,0:T(8,128)(2,1)S(1)}, u32[]{:S(2)}, u32[]{:S(2)}) collective-permute-start(bf16[288,768]{1,0:T(8,128)(2,1)S(1)} %get-tuple-element.35), channel_id=1, source_target_pairs={{0,128},{128,256},{256,384},{384,0},{1,129},{129,257},{257,385},{3... | collective-permute-start | bytes 1327112 | tf_op jit(solution)/shard_map/ppermute | solution.py:375
  148.0 6.7 %collective-permute-done.4.refs_3_ = bf16[288,768]{1,0:T(8,128)(2,1)S(1)} collective-permute-done((bf16[288,768]{1,0:T(8,128)(2,1)S(1)}, bf16[288,768]{1,0:T(8,128)(2,1)S(1)}, u32[]{:S(2)}, u32[]{:S(2)}) %collective-permute-start.4) | collective-permute-done | bytes 442400 | tf_op jit(solution)/shard_map/ppermute | solution.py:375
  154.7 0.9 collective-permute-done.3.refs_2_
  155.6 12.5 %all-to-all-done.2.refs_0_ = bf16[4,32,1664]{2,1,0:T(8,128)(2,1)S(1)} async-done(((bf16[4,32,1664]{2,1,0:T(8,128)(2,1)}), bf16[4,32,1664]{2,1,0:T(8,128)(2,1)S(1)}, u32[]{:S(2)}, u32[]{:S(2)}) %all-to-all-start.2) | async-done | bytes 426016 | tf_op jit(solution)/shard_map/all_to_all | solution.py:386
  168.1 1.1 finish.1
  (1 shorter events, 0.0 us)
Async XLA Ops:
  39.9 53.9 %copy-start.1 = (bf16[1,1536,384]{2,1,0:T(8,128)(2,1)S(1)}, bf16[1,1536,384]{2,1,0:T(8,128)(2,1)}, u32[]{:S(2)}) copy-start(bf16[1,1536,384]{2,1,0:T(8,128)(2,1)} %param.11) | copy-start | bytes 3538948
  39.9 53.9 %copy-start.2 = (bf16[1,1536,384]{2,1,0:T(8,128)(2,1)S(1)}, bf16[1,1536,384]{2,1,0:T(8,128)(2,1)}, u32[]{:S(2)}) copy-start(bf16[1,1536,384]{2,1,0:T(8,128)(2,1)} %param.12) | copy-start | bytes 3538948
  39.9 53.9 %copy-start.3 = (bf16[1,384,1536]{2,1,0:T(8,128)(2,1)S(1)}, bf16[1,384,1536]{2,1,0:T(8,128)(2,1)}, u32[]{:S(2)}) copy-start(bf16[1,384,1536]{2,1,0:T(8,128)(2,1)} %param.13) | copy-start | bytes 3538948
  93.8 4.5 %copy-start = (bf16[16,24,3072]{2,1,0:T(8,128)(2,1)}, bf16[16,24,3072]{2,1,0:T(8,128)(2,1)S(1)}, u32[]{:S(2)}) copy-start(bf16[16,24,3072]{2,1,0:T(8,128)(2,1)S(1)} %all_to_all.15) | copy-start | bytes 7077892
  98.3 35.4 %all-to-all-start.1 = ((bf16[16,24,1664]{2,1,0:T(8,128)(2,1)}), bf16[16,24,1664]{2,1,0:T(8,128)(2,1)S(1)}, u32[]{:S(2)}, u32[]{:S(2)}) async-start(bf16[16,24,1664]{2,1,0:T(8,128)(2,1)} %bitcast.8), calls=%async_computation.1 | async-start | bytes 2555904 | tf_op jit(solution)/shard_map/all_to_all | solution.py:330
  113.7 5.9 %collective-permute-start = (bf16[4,288,768]{2,1,0:T(8,128)(2,1)}, bf16[4,288,768]{2,1,0:T(8,128)(2,1)}, u32[]{:S(2)}, u32[]{:S(2)}) collective-permute-start(bf16[4,288,768]{2,1,0:T(8,128)(2,1)} %get-tuple-element.30), channel_id=1, source_target_pairs={{0,64},{64,0},{1,65},{65,1},{2,66},{66,2},{3,67},{67,3},{4,68},{68... | collective-permute-start | bytes 5308424 | tf_op jit(solution)/shard_map/ppermute | solution.py:348
  121.8 8.8 %collective-permute-start.1 = (bf16[144,768]{1,0:T(8,128)(2,1)S(1)}, bf16[144,768]{1,0:T(8,128)(2,1)S(1)}, u32[]{:S(2)}, u32[]{:S(2)}) collective-permute-start(bf16[144,768]{1,0:T(8,128)(2,1)S(1)} %get-tuple-element.33), channel_id=1, source_target_pairs={{0,128},{128,256},{256,384},{384,0},{1,129},{129,257},{257,385},{3... | collective-permute-start | bytes 663560 | tf_op jit(solution)/shard_map/ppermute | solution.py:374
  123.9 9.7 %collective-permute-start.2 = (bf16[144,768]{1,0:T(8,128)(2,1)S(1)}, bf16[144,768]{1,0:T(8,128)(2,1)S(1)}, u32[]{:S(2)}, u32[]{:S(2)}) collective-permute-start(bf16[144,768]{1,0:T(8,128)(2,1)S(1)} %get-tuple-element.34), channel_id=1, source_target_pairs={{0,384},{128,0},{256,128},{384,256},{1,385},{129,1},{257,129},{385... | collective-permute-start | bytes 663560 | tf_op jit(solution)/shard_map/ppermute | solution.py:374
  135.3 32.8 %all-to-all-start.2 = ((bf16[4,32,1664]{2,1,0:T(8,128)(2,1)}), bf16[4,32,1664]{2,1,0:T(8,128)(2,1)S(1)}, u32[]{:S(2)}, u32[]{:S(2)}) async-start(bf16[4,32,1664]{2,1,0:T(8,128)(2,1)} %bitcast.12), calls=%async_computation.2 | async-start | bytes 851968 | tf_op jit(solution)/shard_map/all_to_all | solution.py:386
  141.5 13.2 %collective-permute-start.4 = (bf16[288,768]{1,0:T(8,128)(2,1)S(1)}, bf16[288,768]{1,0:T(8,128)(2,1)S(1)}, u32[]{:S(2)}, u32[]{:S(2)}) collective-permute-start(bf16[288,768]{1,0:T(8,128)(2,1)S(1)} %get-tuple-element.39), channel_id=1, source_target_pairs={{0,384},{128,0},{256,128},{384,256},{1,385},{129,1},{257,129},{385... | collective-permute-start | bytes 1327112 | tf_op jit(solution)/shard_map/ppermute | solution.py:375
  143.5 12.2 %collective-permute-start.3 = (bf16[288,768]{1,0:T(8,128)(2,1)S(1)}, bf16[288,768]{1,0:T(8,128)(2,1)S(1)}, u32[]{:S(2)}, u32[]{:S(2)}) collective-permute-start(bf16[288,768]{1,0:T(8,128)(2,1)S(1)} %get-tuple-element.35), channel_id=1, source_target_pairs={{0,128},{128,256},{256,384},{384,0},{1,129},{129,257},{257,385},{3... | collective-permute-start | bytes 1327112 | tf_op jit(solution)/shard_map/ppermute | solution.py:375

commit v7 on v6

--- a/solution.py
+++ b/solution.py
@@ -176,47 +176,31 @@
         store.wait()
 
 
-def chip_sum_kernel(
-    chip_ref, keep_hbm, got_hbm, own_ref, right_ref, left_ref, far_low_ref, far_high_ref, keep, got, sems
-):
-    chips, part_rows, _ = keep.shape
-    half = part_rows // 2
+def chip_sum_kernel(chip_ref, keep_hbm, got_hbm, *refs):
+    out_refs, (keep, got, sems) = refs[:-3], refs[-3:]
+    chips = keep.shape[0]
+    order = (2, 1, 3, 0)
     loads = []
-    for s in (2, 1, 3, 0):
+    for s in order:
         chip = (chip_ref[0] + s) & (chips - 1)
         loads.append(pltpu.make_async_copy(keep_hbm.at[chip], keep.at[s], sems.at[2 * s]))
         loads.append(pltpu.make_async_copy(got_hbm.at[chip], got.at[s], sems.at[2 * s + 1]))
     for load in loads:
         load.start()
-
-    def total(s, low, size):
-        rows = pl.ds(low, size)
-        return (keep[s, rows].astype(F32) + got[s, rows].astype(F32)).astype(BF16)
-
-    loads[0].wait()
-    loads[1].wait()
-    far_low_ref[...] = total(2, 0, half)
-    far_high_ref[...] = total(2, half, half)
-    for i, (s, ref) in enumerate(((1, right_ref), (3, left_ref), (0, own_ref))):
-        loads[2 * i + 2].wait()
-        loads[2 * i + 3].wait()
-        ref[...] = total(s, 0, part_rows)
-
-
-def relay_kernel(right_ref, left_ref, low_ref, high_ref, to_right_ref, to_left_ref):
-    half = low_ref.shape[0]
-    to_right_ref[:half] = (right_ref[:half].astype(F32) + low_ref[...].astype(F32)).astype(BF16)
-    to_right_ref[half:] = right_ref[half:]
-    to_left_ref[:half] = left_ref[:half]
-    to_left_ref[half:] = (left_ref[half:].astype(F32) + high_ref[...].astype(F32)).astype(BF16)
-
-
-def combine_kernel(base_ref, back_ref, pick_ref, extra_ref, sum_ref):
+    for i, s in enumerate(order):
+        loads[2 * i].wait()
+        loads[2 * i + 1].wait()
+        out_refs[s][...] = (keep[s].astype(F32) + got[s].astype(F32)).astype(BF16)
+
+
+def combine_kernel(base_ref, far_ref, back_ref, pick_ref, extra_ref, *refs):
+    out_refs, sum_ref = refs[:-1], refs[-1]
     slots = back_ref.shape[0]
     width = back_ref.shape[1] - LANES
-    tokens = sum_ref.shape[0]
+    tokens = pick_ref.shape[0]
+    block = tokens // FAR
     pick = pick_ref[...]
-    sum_ref[:, :width] = dot(pick, back_ref[:, :width]).astype(BF16)
+    sum_ref[:, :, :width] = dot(pick, back_ref[:, :width]).astype(BF16).reshape(FAR, block, width)
     expert, _, _ = slot_parts(iota((slots, LANES), 0))
     own = iota((slots, LANES), 1) == expert
     spread = jnp.where(own, back_ref[:, width:].astype(F32), 0.0).astype(BF16)
@@ -230,16 +214,18 @@
         value = jnp.sum(jnp.where(hit, by_expert, 0.0), axis=1, keepdims=True)
         value = value / extras[:, TOP + k : TOP + k + 1]
         result = jnp.where(lane == k, value, result)
-    sum_ref[:, width:] = result.astype(BF16)
+    sum_ref[:, :, width:] = result.astype(BF16).reshape(FAR, block, LANES)
+    for s, out_ref in enumerate(out_refs):
+        out_ref[...] = sum_ref[(far_ref[0] + s) & (FAR - 1)]
 
 
 def finish_kernel(*refs):
-    sums_ref, part_refs = refs[0], refs[1:-5]
+    sum_refs, part_refs = refs[:FAR], refs[FAR:-5]
     in_ref, prob_ref, gate_ref, up_ref, down_ref = refs[-5:]
     width = in_ref.shape[1]
-    total = sums_ref[0].astype(F32)
-    for s in range(1, FAR):
-        total = total + sums_ref[s].astype(F32)
+    total = sum_refs[0][...].astype(F32)
+    for ref in sum_refs[1:]:
+        total = total + ref[...].astype(F32)
     in_ref[...] = total[:, :width].astype(BF16)
     pick = jnp.where(iota((TOP, LANES), 0) == iota((TOP, LANES), 1), 1.0, 0.0).astype(BF16)
     prob_ref[...] = dot(pick, total[:, width:].astype(BF16), ((1,), (1,))).astype(BF16)
@@ -280,6 +266,7 @@
     part_rows = share + 2 * down_share
     core = lax.axis_index("core").astype(jnp.int32)
     chip = lax.axis_index("x").astype(jnp.int32)
+    far = lax.axis_index("far").astype(jnp.int32)
     moved = core * (NEAR // 2)
     place = lax.axis_index(("far", "near", "y")) - moved + EXPERTS
     base = ((place & -NEAR) + moved).astype(jnp.int32).reshape(1)
@@ -346,12 +333,11 @@
         name="weight_parts",
     )(core.reshape(1), rows, both, hidden)
     got = lax.ppermute(give, "core", [(0, 1), (1, 0)])
-    share_shape, half_shape = shape(part_rows, 2 * hidden_width), shape(part_rows // 2, 2 * hidden_width)
-    own, right, left, far_low, far_high = pl.pallas_call(
+    chip_sums = pl.pallas_call(
         chip_sum_kernel,
-        out_shape=(share_shape,) * 3 + (half_shape,) * 2,
+        out_shape=(shape(part_rows, 2 * hidden_width),) * chips,
         in_specs=[scalar, hbm, hbm],
-        out_specs=tuple(whole(5)),
+        out_specs=tuple(whole(chips)),
         scratch_shapes=[
             pltpu.VMEM((chips, part_rows, 2 * hidden_width), BF16),
             pltpu.VMEM((chips, part_rows, 2 * hidden_width), BF16),
@@ -361,29 +347,23 @@
         cost_estimate=cost(MIB, 6 * MIB),
         name="chip_sums",
     )(chip.reshape(1), keep, got)
-    to_right = [(i, (i + 1) % chips) for i in range(chips)]
-    to_left = [(i, (i - 1) % chips) for i in range(chips)]
-    right, left = pl.pallas_call(
-        relay_kernel,
-        out_shape=(share_shape,) * 2,
-        in_specs=whole(4),
-        out_specs=tuple(whole(2)),
-        compiler_params=params(8),
-        cost_estimate=cost(MIB, 2 * MIB),
-        name="relay_sums",
-    )(right, left, lax.ppermute(far_low, "x", to_right), lax.ppermute(far_high, "x", to_left))
-    parts = [own, lax.ppermute(right, "x", to_right), lax.ppermute(left, "x", to_left)]
-
-    back, _ = lax.optimization_barrier((back, right))
+    parts = [
+        lax.ppermute(chip_sums[s], "x", [(i, (i + s) % chips) for i in range(chips)]) for s in range(1, chips)
+    ] + [chip_sums[0]]
+
+    back, _ = lax.optimization_barrier((back, chip_sums[0]))
     sums = pl.pallas_call(
         combine_kernel,
-        out_shape=shape(tokens, width + LANES),
-        in_specs=[scalar] + whole(3),
-        out_specs=whole(1)[0],
+        out_shape=(shape(block, width + LANES),) * FAR,
+        in_specs=[scalar] * 2 + whole(3),
+        out_specs=tuple(whole(FAR)),
+        scratch_shapes=[pltpu.VMEM((FAR, block, width + LANES), BF16)],
         compiler_params=params(24),
         name="combine_rows",
-    )(base, back, pick, near_tokens[:, 2 * width :])
-    sums = exchange(sums.reshape(FAR, block, width + LANES), "far")
+    )(base, far.reshape(1), back, pick, near_tokens[:, 2 * width :])
+    sums = [sums[0]] + [
+        lax.ppermute(sums[s], "far", [(i, (i + s) % FAR) for i in range(FAR)]) for s in range(1, FAR)
+    ]
 
     grad_in, grad_probs, grad_gate, grad_up, grad_down = pl.pallas_call(
         finish_kernel,
@@ -394,11 +374,11 @@
             jax.ShapeDtypeStruct((share, hidden_width), F32),
             jax.ShapeDtypeStruct((down_share, width), F32),
         ),
-        in_specs=whole(1 + len(parts)),
+        in_specs=whole(FAR + len(parts)),
         out_specs=tuple(whole(5)),
         compiler_params=params(24),
         name="finish",
-    )(sums, *parts)
+    )(*sums, *parts)
     return grad_in, grad_probs.T, grad_gate[None], grad_up[None], grad_down[None]
 
 

time: 170 us -> 173 us (1.018)
  the two profiles are of different devices: /device:TPU:39 before, /device:TPU:1 now
where the time goes in v7:
time: 173 us; the launch traced here: 172 us
  blocking collectives  92.7 us (54%)
  starting transfers between devices  35.9 us (21%)
  waiting for transfers between devices  22.5 us (13%)
  Pallas kernels  20.1 us (12%)
    all_to_all x1, blocking collectives, per_device(): near_exchange(send.reshape(NEAR, FAR * CAP, 2 * width))  49.6 us
    all_gather x1, blocking collectives, per_device(): near_tokens = lax.all_gather(packed, 'far', tiled=True)  43.1 us
    ppermute x3, waiting for transfers between devices, per_device(): lax.ppermute(sums[s], 'far', [(i, (i + s) % FAR) for i in range(FAR)])  18.5 us
    ppermute x3, starting transfers between devices, per_device(): lax.ppermute(sums[s], 'far', [(i, (i + s) % FAR) for i in range(FAR)])  16 us
    ppermute x3, starting transfers between devices, per_device(): lax.ppermute(chip_sums[s], 'x', [(i, (i + s) % chips) for i in range(chip...  10.5 us
    all_to_all x1, starting transfers between devices, per_device(): near_exchange(back.reshape(NEAR, FAR * CAP, width + LANES))  7.48 us
    pallas_call x1, Pallas kernels, per_device(): pl.pallas_call(part_kernel, out_shape=(shape(chips, part_rows, 2 * hidden...  5.76 us
    pallas_call x1, Pallas kernels, per_device(): pl.pallas_call(expert_kernel, out_shape=(shape(slots, width + LANES), sha...  4.47 us
  transfers between devices with their start and end apart: 8, of which 3 were waited for; matrix products, arithmetic and copies ran while one was open for 0% of the time, Pallas kernels for 6%

profile of v7, /device:TPU:1, one launch (start us, length us, event | category | flops | bytes accessed | tf_op | source)
XLA Modules:
  0.0 172.2 jit_solution(4198558206341778054)
XLA Ops:
  0.6 2.3 %pack_tokens.1 = bf16[32,3200]{1,0:T(8,128)(2,1)} custom-call(bf16[32,1536]{1,0:T(8,128)(2,1)} %layer_ref.1, bf16[32,1536]{1,0:T(8,128)(2,1)} %grad_ref.1, s32[8,32]{1,0:T(8,128)} %bitcast.24, bf16[8,32]{1,0:T(8,128)(2,1)} %bitcast.25), custom_call_target="tpu_custom_call" | custom-call | tf_op jit(solution)/shard_map/pack_tokens/pallas_call | solution.py:279
  3.0 43.1 %all_gather.3.tok_ref = bf16[128,3200]{1,0:T(8,128)(2,1)S(1)} all-gather(bf16[32,3200]{1,0:T(8,128)(2,1)} %pack_tokens.1), channel_id=1, replica_groups=mesh['x'=4,'core'=2,'far'=4,'near'=4,'y'=4] {'far'}, dimensions={0}, use_global_device_ids=true | all-gather | bytes 1024000 | tf_op jit(solution)/shard_map/all_gather | solution.py:288
  46.1 1.5 select_rows.1
  47.6 0.0 copy-start.1
  47.6 0.0 copy-start.2
  47.6 0.0 copy-start.3
  47.6 49.6 %all_to_all.10 = bf16[16,24,3072]{2,1,0:T(8,128)(2,1)S(1)} all-to-all(bf16[16,24,3072]{2,1,0:T(8,128)(2,1)S(1)} %bitcast.20), channel_id=1, replica_groups={{0,1,2,3,4,5,6,7,8,9,10,11,12,13,14,15},{16,17,18,19,20,21,22,23,24,25,..., dimensions={0} | all-to-all | bytes 4718592 | tf_op jit(solution)/shard_map/all_to_all | solution.py:305
  97.2 0.0 copy-start
  97.2 0.0 copy-done.1
  97.2 0.0 copy-done.2
  97.2 0.0 copy-done.3
  97.2 4.5 %expert_rows.1 = (bf16[384,1664]{1,0:T(8,128)(2,1)}, bf16[384,768]{1,0:T(8,128)(2,1)S(1)}, bf16[384,384]{1,0:T(8,128)(2,1)S(1)}) custom-call(bf16[384,3072]{1,0:T(8,128)(2,1)S(1)} %bitcast.18, bf16[1536,384]{1,0:T(8,128)(2,1)S(1)} %bitcast.21, bf16[1536,384]{1,0:T(8,128)(2,1)S(1)} %bitcast.22, bf16[384,1536]{1,0:T(8,128)(2,1)S(1)} %bitcast.23), custom_call_target="tpu_custom_call" | custom-call | flops 2264924160 | bytes 8388608 | tf_op jit(solution)/shard_map/expert_rows/pallas_call | solution.py:308
  101.7 0.0 copy-done
  101.7 7.5 %all-to-all-start.1 = ((bf16[16,24,1664]{2,1,0:T(8,128)(2,1)}), bf16[16,24,1664]{2,1,0:T(8,128)(2,1)S(1)}, u32[]{:S(2)}, u32[]{:S(2)}) async-start(bf16[16,24,1664]{2,1,0:T(8,128)(2,1)} %bitcast.9), calls=%async_computation.1 | async-start | bytes 2555904 | tf_op jit(solution)/shard_map/all_to_all | solution.py:317
  109.2 5.8 %weight_parts.1 = (bf16[4,288,768]{2,1,0:T(8,128)(2,1)}, bf16[4,288,768]{2,1,0:T(8,128)(2,1)}) custom-call(s32[1]{0:T(128)} %bitcast.12.core_ref, bf16[384,3072]{1,0:T(8,128)(2,1)} %bitcast.19, bf16[384,768]{1,0:T(8,128)(2,1)S(1)} %get-tuple-element.28.both_ref, bf16[384,384]{1,0:T(8,128)(2,1)S(1)} %get-tuple-element.29.hidden_ref), custom_call_target="tpu_custom_call" | custom-call | flops 1358954496 | bytes 8388608 | tf_op jit(solution)/shard_map/weight_parts/pallas_call | solution.py:319
  115.0 1.9 %collective-permute-start = (bf16[4,288,768]{2,1,0:T(8,128)(2,1)}, bf16[4,288,768]{2,1,0:T(8,128)(2,1)}, u32[]{:S(2)}, u32[]{:S(2)}) collective-permute-start(bf16[4,288,768]{2,1,0:T(8,128)(2,1)} %get-tuple-element.31), channel_id=1, source_target_pairs={{0,64},{64,0},{1,65},{65,1},{2,66},{66,2},{3,67},{67,3},{4,68},{68... | collective-permute-start | bytes 5308424 | tf_op jit(solution)/shard_map/ppermute | solution.py:335
  116.9 4.0 %collective-permute-done.got_hbm = bf16[4,288,768]{2,1,0:T(8,128)(2,1)} collective-permute-done((bf16[4,288,768]{2,1,0:T(8,128)(2,1)}, bf16[4,288,768]{2,1,0:T(8,128)(2,1)}, u32[]{:S(2)}, u32[]{:S(2)}) %collective-permute-start) | collective-permute-done | bytes 1769504 | tf_op jit(solution)/shard_map/ppermute | solution.py:335
  120.9 3.1 %chip_sums.1 = (bf16[288,768]{1,0:T(8,128)(2,1)S(1)}, bf16[288,768]{1,0:T(8,128)(2,1)}, bf16[288,768]{1,0:T(8,128)(2,1)}, bf16[288,768]{1,0:T(8,128)(2,1)}) custom-call(s32[1]{0:T(128)} %bitcast.11.chip_ref, bf16[4,288,768]{2,1,0:T(8,128)(2,1)} %get-tuple-element.30.keep_hbm, bf16[4,288,768]{2,1,0:T(8,128)(2,1)} %collective-permute-done.got_hbm), custom_call_target="tpu_custom_call" | custom-call | flops 1048576 | bytes 6291456 | tf_op jit(solution)/shard_map/chip_sums/pallas_call | solution.py:336
  124.0 3.1 %collective-permute-start.4 = (bf16[288,768]{1,0:T(8,128)(2,1)}, bf16[288,768]{1,0:T(8,128)(2,1)S(1)}, u32[]{:S(2)}, u32[]{:S(2)}) collective-permute-start(bf16[288,768]{1,0:T(8,128)(2,1)} %get-tuple-element.39), channel_id=1, source_target_pairs={{0,128},{128,256},{256,384},{384,0},{1,129},{129,257},{257,385},{3... | collective-permute-start | bytes 1327112 | tf_op jit(solution)/shard_map/ppermute | solution.py:351
  127.1 4.4 %collective-permute-start.5 = (bf16[288,768]{1,0:T(8,128)(2,1)}, bf16[288,768]{1,0:T(8,128)(2,1)S(1)}, u32[]{:S(2)}, u32[]{:S(2)}) collective-permute-start(bf16[288,768]{1,0:T(8,128)(2,1)} %get-tuple-element.40), channel_id=1, source_target_pairs={{0,256},{128,384},{256,0},{384,128},{1,257},{129,385},{257,1},{385... | collective-permute-start | bytes 1327112 | tf_op jit(solution)/shard_map/ppermute | solution.py:351
  131.5 3.1 %collective-permute-start.6 = (bf16[288,768]{1,0:T(8,128)(2,1)}, bf16[288,768]{1,0:T(8,128)(2,1)}, u32[]{:S(2)}, u32[]{:S(2)}) collective-permute-start(bf16[288,768]{1,0:T(8,128)(2,1)} %get-tuple-element.41), channel_id=1, source_target_pairs={{0,384},{128,0},{256,128},{384,256},{1,385},{129,1},{257,129},{385... | collective-permute-start | bytes 1327112 | tf_op jit(solution)/shard_map/ppermute | solution.py:351
  134.6 0.0 all-to-all-done.1
  134.6 0.9 combine_rows.1
  135.5 4.4 %collective-permute-start.1 = (bf16[32,1664]{1,0:T(8,128)(2,1)S(1)}, bf16[32,1664]{1,0:T(8,128)(2,1)S(1)}, u32[]{:S(2)}, u32[]{:S(2)}) collective-permute-start(bf16[32,1664]{1,0:T(8,128)(2,1)S(1)} %get-tuple-element.36), channel_id=1, source_target_pairs={{0,16},{16,32},{32,48},{48,0},{1,17},{17,33},{33,49},{49,1},{2,18}... | collective-permute-start | bytes 319496 | tf_op jit(solution)/shard_map/ppermute | solution.py:365
  139.8 7.6 %collective-permute-start.2 = (bf16[32,1664]{1,0:T(8,128)(2,1)S(1)}, bf16[32,1664]{1,0:T(8,128)(2,1)S(1)}, u32[]{:S(2)}, u32[]{:S(2)}) collective-permute-start(bf16[32,1664]{1,0:T(8,128)(2,1)S(1)} %get-tuple-element.37), channel_id=1, source_target_pairs={{0,32},{16,48},{32,0},{48,16},{1,33},{17,49},{33,1},{49,17},{2,34}... | collective-permute-start | bytes 319496 | tf_op jit(solution)/shard_map/ppermute | solution.py:365
  147.5 0.0 collective-permute-done.4.refs_4_
  147.5 4.0 %collective-permute-start.3 = (bf16[32,1664]{1,0:T(8,128)(2,1)S(1)}, bf16[32,1664]{1,0:T(8,128)(2,1)S(1)}, u32[]{:S(2)}, u32[]{:S(2)}) collective-permute-start(bf16[32,1664]{1,0:T(8,128)(2,1)S(1)} %get-tuple-element.38), channel_id=1, source_target_pairs={{0,48},{16,0},{32,16},{48,32},{1,49},{17,1},{33,17},{49,33},{2,50}... | collective-permute-start | bytes 319496 | tf_op jit(solution)/shard_map/ppermute | solution.py:365
  151.5 0.0 collective-permute-done.5.refs_5_
  151.5 0.0 collective-permute-done.6.refs_6_
  151.5 0.0 collective-permute-done.1.refs_1_
  151.5 3.3 %collective-permute-done.2.refs_2_ = bf16[32,1664]{1,0:T(8,128)(2,1)S(1)} collective-permute-done((bf16[32,1664]{1,0:T(8,128)(2,1)S(1)}, bf16[32,1664]{1,0:T(8,128)(2,1)S(1)}, u32[]{:S(2)}, u32[]{:S(2)}) %collective-permute-start.2) | collective-permute-done | bytes 106528 | tf_op jit(solution)/shard_map/ppermute | solution.py:365
  154.9 15.2 %collective-permute-done.3.refs_3_ = bf16[32,1664]{1,0:T(8,128)(2,1)S(1)} collective-permute-done((bf16[32,1664]{1,0:T(8,128)(2,1)S(1)}, bf16[32,1664]{1,0:T(8,128)(2,1)S(1)}, u32[]{:S(2)}, u32[]{:S(2)}) %collective-permute-start.3) | collective-permute-done | bytes 106528 | tf_op jit(solution)/shard_map/ppermute | solution.py:365
  170.1 2.1 %finish.1 = (bf16[32,1536]{1,0:T(8,128)(2,1)}, bf16[8,32]{1,0:T(8,128)(2,1)}, f32[192,384]{1,0:T(8,128)}, f32[192,384]{1,0:T(8,128)}, f32[48,1536]{1,0:T(8,128)}) custom-call(bf16[32,1664]{1,0:T(8,128)(2,1)S(1)} %get-tuple-element.35.refs_0_, bf16[32,1664]{1,0:T(8,128)(2,1)S(1)} %collective-permute-done.1.refs_1_, ...), custom_call_target="tpu_custom_call" | custom-call | tf_op jit(solution)/shard_map/finish/pallas_call | solution.py:368
  (1 shorter events, 0.0 us)
Async XLA Ops:
  47.6 49.7 %copy-start.1 = (bf16[1,1536,384]{2,1,0:T(8,128)(2,1)S(1)}, bf16[1,1536,384]{2,1,0:T(8,128)(2,1)}, u32[]{:S(2)}) copy-start(bf16[1,1536,384]{2,1,0:T(8,128)(2,1)} %param.11) | copy-start | bytes 3538948
  47.6 49.6 %copy-start.2 = (bf16[1,1536,384]{2,1,0:T(8,128)(2,1)S(1)}, bf16[1,1536,384]{2,1,0:T(8,128)(2,1)}, u32[]{:S(2)}) copy-start(bf16[1,1536,384]{2,1,0:T(8,128)(2,1)} %param.12) | copy-start | bytes 3538948
  47.6 49.6 %copy-start.3 = (bf16[1,384,1536]{2,1,0:T(8,128)(2,1)S(1)}, bf16[1,384,1536]{2,1,0:T(8,128)(2,1)}, u32[]{:S(2)}) copy-start(bf16[1,384,1536]{2,1,0:T(8,128)(2,1)} %param.13) | copy-start | bytes 3538948
  97.2 4.5 %copy-start = (bf16[16,24,3072]{2,1,0:T(8,128)(2,1)}, bf16[16,24,3072]{2,1,0:T(8,128)(2,1)S(1)}, u32[]{:S(2)}) copy-start(bf16[16,24,3072]{2,1,0:T(8,128)(2,1)S(1)} %all_to_all.10) | copy-start | bytes 7077892
  101.7 32.9 %all-to-all-start.1 = ((bf16[16,24,1664]{2,1,0:T(8,128)(2,1)}), bf16[16,24,1664]{2,1,0:T(8,128)(2,1)S(1)}, u32[]{:S(2)}, u32[]{:S(2)}) async-start(bf16[16,24,1664]{2,1,0:T(8,128)(2,1)} %bitcast.9), calls=%async_computation.1 | async-start | bytes 2555904 | tf_op jit(solution)/shard_map/all_to_all | solution.py:317
  115.0 5.9 %collective-permute-start = (bf16[4,288,768]{2,1,0:T(8,128)(2,1)}, bf16[4,288,768]{2,1,0:T(8,128)(2,1)}, u32[]{:S(2)}, u32[]{:S(2)}) collective-permute-start(bf16[4,288,768]{2,1,0:T(8,128)(2,1)} %get-tuple-element.31), channel_id=1, source_target_pairs={{0,64},{64,0},{1,65},{65,1},{2,66},{66,2},{3,67},{67,3},{4,68},{68... | collective-permute-start | bytes 5308424 | tf_op jit(solution)/shard_map/ppermute | solution.py:335
  124.0 23.5 %collective-permute-start.4 = (bf16[288,768]{1,0:T(8,128)(2,1)}, bf16[288,768]{1,0:T(8,128)(2,1)S(1)}, u32[]{:S(2)}, u32[]{:S(2)}) collective-permute-start(bf16[288,768]{1,0:T(8,128)(2,1)} %get-tuple-element.39), channel_id=1, source_target_pairs={{0,128},{128,256},{256,384},{384,0},{1,129},{129,257},{257,385},{3... | collective-permute-start | bytes 1327112 | tf_op jit(solution)/shard_map/ppermute | solution.py:351
  127.1 24.4 %collective-permute-start.5 = (bf16[288,768]{1,0:T(8,128)(2,1)}, bf16[288,768]{1,0:T(8,128)(2,1)S(1)}, u32[]{:S(2)}, u32[]{:S(2)}) collective-permute-start(bf16[288,768]{1,0:T(8,128)(2,1)} %get-tuple-element.40), channel_id=1, source_target_pairs={{0,256},{128,384},{256,0},{384,128},{1,257},{129,385},{257,1},{385... | collective-permute-start | bytes 1327112 | tf_op jit(solution)/shard_map/ppermute | solution.py:351
  131.5 20.0 %collective-permute-start.6 = (bf16[288,768]{1,0:T(8,128)(2,1)}, bf16[288,768]{1,0:T(8,128)(2,1)}, u32[]{:S(2)}, u32[]{:S(2)}) collective-permute-start(bf16[288,768]{1,0:T(8,128)(2,1)} %get-tuple-element.41), channel_id=1, source_target_pairs={{0,384},{128,0},{256,128},{384,256},{1,385},{129,1},{257,129},{385... | collective-permute-start | bytes 1327112 | tf_op jit(solution)/shard_map/ppermute | solution.py:351
  135.5 16.1 %collective-permute-start.1 = (bf16[32,1664]{1,0:T(8,128)(2,1)S(1)}, bf16[32,1664]{1,0:T(8,128)(2,1)S(1)}, u32[]{:S(2)}, u32[]{:S(2)}) collective-permute-start(bf16[32,1664]{1,0:T(8,128)(2,1)S(1)} %get-tuple-element.36), channel_id=1, source_target_pairs={{0,16},{16,32},{32,48},{48,0},{1,17},{17,33},{33,49},{49,1},{2,18}... | collective-permute-start | bytes 319496 | tf_op jit(solution)/shard_map/ppermute | solution.py:365
  139.8 15.0 %collective-permute-start.2 = (bf16[32,1664]{1,0:T(8,128)(2,1)S(1)}, bf16[32,1664]{1,0:T(8,128)(2,1)S(1)}, u32[]{:S(2)}, u32[]{:S(2)}) collective-permute-start(bf16[32,1664]{1,0:T(8,128)(2,1)S(1)} %get-tuple-element.37), channel_id=1, source_target_pairs={{0,32},{16,48},{32,0},{48,16},{1,33},{17,49},{33,1},{49,17},{2,34}... | collective-permute-start | bytes 319496 | tf_op jit(solution)/shard_map/ppermute | solution.py:365
  147.5 22.6 %collective-permute-start.3 = (bf16[32,1664]{1,0:T(8,128)(2,1)S(1)}, bf16[32,1664]{1,0:T(8,128)(2,1)S(1)}, u32[]{:S(2)}, u32[]{:S(2)}) collective-permute-start(bf16[32,1664]{1,0:T(8,128)(2,1)S(1)} %get-tuple-element.38), channel_id=1, source_target_pairs={{0,48},{16,0},{32,16},{48,32},{1,49},{17,1},{33,17},{49,33},{2,50}... | collective-permute-start | bytes 319496 | tf_op jit(solution)/shard_map/ppermute | solution.py:365

commit v8 on v6

--- a/solution.py
+++ b/solution.py
@@ -49,24 +49,24 @@
     return lists
 
 
-def pack_kernel(layer_ref, grad_ref, ids_ref, probs_ref, out_ref, ids_vmem, sems):
-    width = layer_ref.shape[1]
+def pack_kernel(layer_hbm, grad_hbm, ids_ref, probs_ref, out_hbm, extras, sems):
+    width = layer_hbm.shape[1]
     copies = [
-        pltpu.make_async_copy(ids_ref, ids_vmem, sems.at[0]),
-        pltpu.make_async_copy(layer_ref, out_ref.at[:, :width], sems.at[1]),
-        pltpu.make_async_copy(grad_ref, out_ref.at[:, width : 2 * width], sems.at[2]),
+        pltpu.make_async_copy(layer_hbm, out_hbm.at[:, :width], sems.at[0]),
+        pltpu.make_async_copy(grad_hbm, out_hbm.at[:, width : 2 * width], sems.at[1]),
+        pltpu.make_async_copy(extras, out_hbm.at[:, 2 * width :], sems.at[2]),
     ]
-    for copy in copies:
-        copy.start()
+    copies[0].start()
+    copies[1].start()
     choice, lane = iota((TOP, LANES), 0), iota((TOP, LANES), 1)
     ids_lane = jnp.where(lane == choice, 1.0, 0.0).astype(BF16)
     probs_lane = jnp.where(lane == choice + TOP, 1.0, 0.0).astype(BF16)
-    copies[0].wait()
-    ids = ids_vmem[...].astype(F32).astype(BF16)
-    extras = dot(ids, ids_lane, ((0,), (0,))) + dot(probs_ref[...], probs_lane, ((0,), (0,)))
-    out_ref[:, 2 * width :] = extras.astype(BF16)
-    copies[1].wait()
-    copies[2].wait()
+    ids = ids_ref[...].astype(F32).astype(BF16)
+    both = dot(ids, ids_lane, ((0,), (0,))) + dot(probs_ref[...], probs_lane, ((0,), (0,)))
+    extras[...] = both.astype(BF16)
+    copies[2].start()
+    for copy in copies:
+        copy.wait()
 
 
 def select_kernel(base_ref, tok_ref, send_ref, pick_ref):
@@ -292,9 +292,9 @@
     packed = pl.pallas_call(
         pack_kernel,
         out_shape=shape(block, 2 * width + LANES),
-        in_specs=[hbm] * 3 + whole(1),
-        out_specs=whole(1)[0],
-        scratch_shapes=[pltpu.VMEM((TOP, block), jnp.int32), pltpu.SemaphoreType.DMA((3,))],
+        in_specs=[hbm] * 2 + whole(2),
+        out_specs=hbm,
+        scratch_shapes=[pltpu.VMEM((block, LANES), BF16), pltpu.SemaphoreType.DMA((3,))],
         compiler_params=params(60),
         name="pack_tokens",
     )(layer_in, grad_out, expert_ids.T, gate_probs.T)
@@ -363,6 +363,17 @@
     )(chip.reshape(1), keep, got)
     to_right = [(i, (i + 1) % chips) for i in range(chips)]
     to_left = [(i, (i - 1) % chips) for i in range(chips)]
+    got_low = lax.ppermute(far_low, "x", to_right)
+    got_high = lax.ppermute(far_high, "x", to_left)
+    sums = pl.pallas_call(
+        combine_kernel,
+        out_shape=shape(tokens, width + LANES),
+        in_specs=[scalar] + whole(3),
+        out_specs=whole(1)[0],
+        compiler_params=params(24),
+        name="combine_rows",
+    )(base, back, pick, near_tokens[:, 2 * width :])
+    right, left, sums = lax.optimization_barrier((right, left, sums))
     right, left = pl.pallas_call(
         relay_kernel,
         out_shape=(share_shape,) * 2,
@@ -371,18 +382,10 @@
         compiler_params=params(8),
         cost_estimate=cost(MIB, 2 * MIB),
         name="relay_sums",
-    )(right, left, lax.ppermute(far_low, "x", to_right), lax.ppermute(far_high, "x", to_left))
+    )(right, left, got_low, got_high)
     parts = [own, lax.ppermute(right, "x", to_right), lax.ppermute(left, "x", to_left)]
 
-    back, _ = lax.optimization_barrier((back, right))
-    sums = pl.pallas_call(
-        combine_kernel,
-        out_shape=shape(tokens, width + LANES),
-        in_specs=[scalar] + whole(3),
-        out_specs=whole(1)[0],
-        compiler_params=params(24),
-        name="combine_rows",
-    )(base, back, pick, near_tokens[:, 2 * width :])
+    sums, _ = lax.optimization_barrier((sums, right))
     sums = exchange(sums.reshape(FAR, block, width + LANES), "far")
 
     grad_in, grad_probs, grad_gate, grad_up, grad_down = pl.pallas_call(

time: 170 us -> 176 us (1.035)
  Pallas kernels: 19 us -> 26.8 us
    pallas_call x1, Pallas kernels: 2.34 us -> 7.78 us  [per_device(): pl.pallas_call(pack_kernel, out_shape=shape(block, 2 * width + LANES), in...]
    ppermute x2, waiting for transfers between devices: 6.48 us -> 4.25 us  [the longest x1 3.01 us: per_device(): got_high = lax.ppermute(far_high, 'x', to_left)]
  transfers between devices with their start and end apart: 7 -> 7, of which waited for: 6 -> 7; matrix products, arithmetic and copies ran while one was open for 0% -> 0% of each run, Pallas kernels for 5% -> 6%
where the time goes in v8:
time: 176 us
  blocking collectives  89.3 us (51%)
  starting transfers between devices  29.5 us (17%)
  waiting for transfers between devices  29.5 us (17%)
  Pallas kernels  26.8 us (15%)
    all_to_all x1, blocking collectives, per_device(): near_exchange(send.reshape(NEAR, FAR * CAP, 2 * width))  53.8 us
    all_gather x1, blocking collectives, per_device(): near_tokens = lax.all_gather(packed, 'far', tiled=True)  35.4 us
    all_to_all x1, waiting for transfers between devices, per_device(): sums = exchange(sums.reshape(FAR, block, width + LANES), 'far')  12.7 us
    all_to_all x1, starting transfers between devices, per_device(): near_exchange(back.reshape(NEAR, FAR * CAP, width + LANES))  9.66 us
    pallas_call x1, Pallas kernels, per_device(): pl.pallas_call(pack_kernel, out_shape=shape(block, 2 * width + LANES), in...  7.78 us
    ppermute x1, waiting for transfers between devices, per_device(): lax.ppermute(left, 'x', to_left)  6.92 us
    all_to_all x1, starting transfers between devices, per_device(): sums = exchange(sums.reshape(FAR, block, width + LANES), 'far')  6.17 us
    pallas_call x1, Pallas kernels, per_device(): pl.pallas_call(part_kernel, out_shape=(shape(chips, part_rows, 2 * hidden...  5.75 us
  transfers between devices with their start and end apart: 7, of which 7 were waited for; matrix products, arithmetic and copies ran while one was open for 0% of the time, Pallas kernels for 6%

profile of v8, /device:TPU:39, one launch (start us, length us, event | category | flops | bytes accessed | tf_op | source)
XLA Modules:
  0.0 175.9 jit_solution(11664784395298567501)
XLA Ops:
  0.6 7.8 %pack_tokens.1 = bf16[32,3200]{1,0:T(8,128)(2,1)} custom-call(bf16[32,1536]{1,0:T(8,128)(2,1)} %layer_hbm.1, bf16[32,1536]{1,0:T(8,128)(2,1)} %grad_hbm.1, s32[8,32]{1,0:T(8,128)} %bitcast.24, bf16[8,32]{1,0:T(8,128)(2,1)} %bitcast.25), custom_call_target="tpu_custom_call" | custom-call | tf_op jit(solution)/shard_map/pack_tokens/pallas_call | solution.py:292
  8.4 35.4 %all_gather.3.tok_ref = bf16[128,3200]{1,0:T(8,128)(2,1)S(1)} all-gather(bf16[32,3200]{1,0:T(8,128)(2,1)} %pack_tokens.1), channel_id=1, replica_groups=mesh['x'=4,'core'=2,'far'=4,'near'=4,'y'=4] {'far'}, dimensions={0}, use_global_device_ids=true | all-gather | bytes 1024000 | tf_op jit(solution)/shard_map/all_gather | solution.py:301
  43.9 1.5 select_rows.1
  45.3 0.0 copy-start.1
  45.4 0.0 copy-start.2
  45.4 0.0 copy-start.3
  45.4 53.8 %all_to_all.15 = bf16[16,24,3072]{2,1,0:T(8,128)(2,1)S(1)} all-to-all(bf16[16,24,3072]{2,1,0:T(8,128)(2,1)S(1)} %bitcast.20), channel_id=1, replica_groups={{0,1,2,3,4,5,6,7,8,9,10,11,12,13,14,15},{16,17,18,19,20,21,22,23,24,25,..., dimensions={0} | all-to-all | bytes 4718592 | tf_op jit(solution)/shard_map/all_to_all | solution.py:318
  99.2 0.0 copy-start
  99.2 0.0 copy-done.1
  99.2 0.0 copy-done.2
  99.2 0.0 copy-done.3
  99.2 4.5 %expert_rows.1 = (bf16[384,1664]{1,0:T(8,128)(2,1)}, bf16[384,768]{1,0:T(8,128)(2,1)S(1)}, bf16[384,384]{1,0:T(8,128)(2,1)S(1)}) custom-call(bf16[384,3072]{1,0:T(8,128)(2,1)S(1)} %bitcast.18, bf16[1536,384]{1,0:T(8,128)(2,1)S(1)} %bitcast.21, bf16[1536,384]{1,0:T(8,128)(2,1)S(1)} %bitcast.22, bf16[384,1536]{1,0:T(8,128)(2,1)S(1)} %bitcast.23), custom_call_target="tpu_custom_call" | custom-call | flops 2264924160 | bytes 8388608 | tf_op jit(solution)/shard_map/expert_rows/pallas_call | solution.py:321
  103.7 0.0 copy-done
  103.7 9.7 %all-to-all-start.1 = ((bf16[16,24,1664]{2,1,0:T(8,128)(2,1)}), bf16[16,24,1664]{2,1,0:T(8,128)(2,1)S(1)}, u32[]{:S(2)}, u32[]{:S(2)}) async-start(bf16[16,24,1664]{2,1,0:T(8,128)(2,1)} %bitcast.10), calls=%async_computation.1 | async-start | bytes 2555904 | tf_op jit(solution)/shard_map/all_to_all | solution.py:330
  113.4 5.8 %weight_parts.1 = (bf16[4,288,768]{2,1,0:T(8,128)(2,1)}, bf16[4,288,768]{2,1,0:T(8,128)(2,1)}) custom-call(s32[1]{0:T(128)} %bitcast.1.core_ref, bf16[384,3072]{1,0:T(8,128)(2,1)} %bitcast.19, bf16[384,768]{1,0:T(8,128)(2,1)S(1)} %get-tuple-element.29.both_ref, bf16[384,384]{1,0:T(8,128)(2,1)S(1)} %get-tuple-element.30.hidden_ref), custom_call_target="tpu_custom_call" | custom-call | flops 1358954496 | bytes 8388608 | tf_op jit(solution)/shard_map/weight_parts/pallas_call | solution.py:332
  119.1 1.9 %collective-permute-start = (bf16[4,288,768]{2,1,0:T(8,128)(2,1)}, bf16[4,288,768]{2,1,0:T(8,128)(2,1)}, u32[]{:S(2)}, u32[]{:S(2)}) collective-permute-start(bf16[4,288,768]{2,1,0:T(8,128)(2,1)} %get-tuple-element.32), channel_id=1, source_target_pairs={{0,64},{64,0},{1,65},{65,1},{2,66},{66,2},{3,67},{67,3},{4,68},{68... | collective-permute-start | bytes 5308424 | tf_op jit(solution)/shard_map/ppermute | solution.py:348
  121.1 4.0 %collective-permute-done.got_hbm = bf16[4,288,768]{2,1,0:T(8,128)(2,1)} collective-permute-done((bf16[4,288,768]{2,1,0:T(8,128)(2,1)}, bf16[4,288,768]{2,1,0:T(8,128)(2,1)}, u32[]{:S(2)}, u32[]{:S(2)}) %collective-permute-start) | collective-permute-done | bytes 1769504 | tf_op jit(solution)/shard_map/ppermute | solution.py:348
  125.1 2.8 %chip_sums.1 = (bf16[288,768]{1,0:T(8,128)(2,1)S(1)}, bf16[288,768]{1,0:T(8,128)(2,1)S(1)}, bf16[288,768]{1,0:T(8,128)(2,1)S(1)}, bf16[144,768]{1,0:T(8,128)(2,1)}, bf16[144,768]{1,0:T(8,128)(2,1)}) custom-call(s32[1]{0:T(128)} %bitcast.chip_ref, bf16[4,288,768]{2,1,0:T(8,128)(2,1)} %get-tuple-element.31.keep_hbm, ...), custom_call_target="tpu_custom_call" | custom-call | flops 1048576 | bytes 6291456 | tf_op jit(solution)/shard_map/chip_sums/pallas_call | solution.py:350
  127.8 2.1 %collective-permute-start.1 = (bf16[144,768]{1,0:T(8,128)(2,1)}, bf16[144,768]{1,0:T(8,128)(2,1)}, u32[]{:S(2)}, u32[]{:S(2)}) collective-permute-start(bf16[144,768]{1,0:T(8,128)(2,1)} %get-tuple-element.40), channel_id=1, source_target_pairs={{0,128},{128,256},{256,384},{384,0},{1,129},{129,257},{257,385},{3... | collective-permute-start | bytes 663560 | tf_op jit(solution)/shard_map/ppermute | solution.py:366
  130.0 3.2 %collective-permute-start.2 = (bf16[144,768]{1,0:T(8,128)(2,1)}, bf16[144,768]{1,0:T(8,128)(2,1)}, u32[]{:S(2)}, u32[]{:S(2)}) collective-permute-start(bf16[144,768]{1,0:T(8,128)(2,1)} %get-tuple-element.41), channel_id=1, source_target_pairs={{0,384},{128,0},{256,128},{384,256},{1,385},{129,1},{257,129},{385... | collective-permute-start | bytes 663560 | tf_op jit(solution)/shard_map/ppermute | solution.py:367
  133.2 0.9 all-to-all-done.1
  134.1 1.6 combine_rows.1
  135.7 1.2 collective-permute-done.1.low_ref
  136.9 3.0 %collective-permute-done.2.high_ref = bf16[144,768]{1,0:T(8,128)(2,1)} collective-permute-done((bf16[144,768]{1,0:T(8,128)(2,1)}, bf16[144,768]{1,0:T(8,128)(2,1)}, u32[]{:S(2)}, u32[]{:S(2)}) %collective-permute-start.2) | collective-permute-done | bytes 221216 | tf_op jit(solution)/shard_map/ppermute | solution.py:367
  140.0 1.9 %relay_sums.1 = (bf16[288,768]{1,0:T(8,128)(2,1)S(1)}, bf16[288,768]{1,0:T(8,128)(2,1)}) custom-call(bf16[288,768]{1,0:T(8,128)(2,1)S(1)} %get-tuple-element.38.right_ref, bf16[288,768]{1,0:T(8,128)(2,1)S(1)} %get-tuple-element.39.left_ref, bf16[144,768]{1,0:T(8,128)(2,1)} %collective-permute-done.1.low_ref, bf16[144,768]{1,0:T(8,128)(2,1)} %collective-permute-done.2.high_ref), custom_call_target="tpu_custom_call" | custom-call | flops 1048576 | bytes 2097152 | tf_op jit(solution)/shard_map/relay_sums/pallas_call | solution.py:377
  141.8 6.2 %all-to-all-start.2 = ((bf16[4,32,1664]{2,1,0:T(8,128)(2,1)}), bf16[4,32,1664]{2,1,0:T(8,128)(2,1)S(1)}, u32[]{:S(2)}, u32[]{:S(2)}) async-start(bf16[4,32,1664]{2,1,0:T(8,128)(2,1)} %bitcast.12), calls=%async_computation.2 | async-start | bytes 851968 | tf_op jit(solution)/shard_map/all_to_all | solution.py:389
  148.0 2.0 %collective-permute-start.4 = (bf16[288,768]{1,0:T(8,128)(2,1)}, bf16[288,768]{1,0:T(8,128)(2,1)S(1)}, u32[]{:S(2)}, u32[]{:S(2)}) collective-permute-start(bf16[288,768]{1,0:T(8,128)(2,1)} %get-tuple-element.45), channel_id=1, source_target_pairs={{0,384},{128,0},{256,128},{384,256},{1,385},{129,1},{257,129},{385... | collective-permute-start | bytes 1327112 | tf_op jit(solution)/shard_map/ppermute | solution.py:386
  150.0 4.5 %collective-permute-start.3 = (bf16[288,768]{1,0:T(8,128)(2,1)S(1)}, bf16[288,768]{1,0:T(8,128)(2,1)S(1)}, u32[]{:S(2)}, u32[]{:S(2)}) collective-permute-start(bf16[288,768]{1,0:T(8,128)(2,1)S(1)} %get-tuple-element.42), channel_id=1, source_target_pairs={{0,128},{128,256},{256,384},{384,0},{1,129},{129,257},{257,385},{3... | collective-permute-start | bytes 1327112 | tf_op jit(solution)/shard_map/ppermute | solution.py:386
  154.5 6.9 %collective-permute-done.4.refs_3_ = bf16[288,768]{1,0:T(8,128)(2,1)S(1)} collective-permute-done((bf16[288,768]{1,0:T(8,128)(2,1)}, bf16[288,768]{1,0:T(8,128)(2,1)S(1)}, u32[]{:S(2)}, u32[]{:S(2)}) %collective-permute-start.4) | collective-permute-done | bytes 442400 | tf_op jit(solution)/shard_map/ppermute | solution.py:386
  161.4 0.7 collective-permute-done.3.refs_2_
  162.1 12.7 %all-to-all-done.2.refs_0_ = bf16[4,32,1664]{2,1,0:T(8,128)(2,1)S(1)} async-done(((bf16[4,32,1664]{2,1,0:T(8,128)(2,1)}), bf16[4,32,1664]{2,1,0:T(8,128)(2,1)S(1)}, u32[]{:S(2)}, u32[]{:S(2)}) %all-to-all-start.2) | async-done | bytes 426016 | tf_op jit(solution)/shard_map/all_to_all | solution.py:389
  174.8 1.1 finish.1
  (1 shorter events, 0.0 us)
Async XLA Ops:
  45.3 53.9 %copy-start.1 = (bf16[1,1536,384]{2,1,0:T(8,128)(2,1)S(1)}, bf16[1,1536,384]{2,1,0:T(8,128)(2,1)}, u32[]{:S(2)}) copy-start(bf16[1,1536,384]{2,1,0:T(8,128)(2,1)} %param.11) | copy-start | bytes 3538948
  45.4 53.9 %copy-start.2 = (bf16[1,1536,384]{2,1,0:T(8,128)(2,1)S(1)}, bf16[1,1536,384]{2,1,0:T(8,128)(2,1)}, u32[]{:S(2)}) copy-start(bf16[1,1536,384]{2,1,0:T(8,128)(2,1)} %param.12) | copy-start | bytes 3538948
  45.4 53.9 %copy-start.3 = (bf16[1,384,1536]{2,1,0:T(8,128)(2,1)S(1)}, bf16[1,384,1536]{2,1,0:T(8,128)(2,1)}, u32[]{:S(2)}) copy-start(bf16[1,384,1536]{2,1,0:T(8,128)(2,1)} %param.13) | copy-start | bytes 3538948
  99.2 4.5 %copy-start = (bf16[16,24,3072]{2,1,0:T(8,128)(2,1)}, bf16[16,24,3072]{2,1,0:T(8,128)(2,1)S(1)}, u32[]{:S(2)}) copy-start(bf16[16,24,3072]{2,1,0:T(8,128)(2,1)S(1)} %all_to_all.15) | copy-start | bytes 7077892
  103.7 30.4 %all-to-all-start.1 = ((bf16[16,24,1664]{2,1,0:T(8,128)(2,1)}), bf16[16,24,1664]{2,1,0:T(8,128)(2,1)S(1)}, u32[]{:S(2)}, u32[]{:S(2)}) async-start(bf16[16,24,1664]{2,1,0:T(8,128)(2,1)} %bitcast.10), calls=%async_computation.1 | async-start | bytes 2555904 | tf_op jit(solution)/shard_map/all_to_all | solution.py:330
  119.1 5.9 %collective-permute-start = (bf16[4,288,768]{2,1,0:T(8,128)(2,1)}, bf16[4,288,768]{2,1,0:T(8,128)(2,1)}, u32[]{:S(2)}, u32[]{:S(2)}) collective-permute-start(bf16[4,288,768]{2,1,0:T(8,128)(2,1)} %get-tuple-element.32), channel_id=1, source_target_pairs={{0,64},{64,0},{1,65},{65,1},{2,66},{66,2},{3,67},{67,3},{4,68},{68... | collective-permute-start | bytes 5308424 | tf_op jit(solution)/shard_map/ppermute | solution.py:348
  127.8 9.1 %collective-permute-start.1 = (bf16[144,768]{1,0:T(8,128)(2,1)}, bf16[144,768]{1,0:T(8,128)(2,1)}, u32[]{:S(2)}, u32[]{:S(2)}) collective-permute-start(bf16[144,768]{1,0:T(8,128)(2,1)} %get-tuple-element.40), channel_id=1, source_target_pairs={{0,128},{128,256},{256,384},{384,0},{1,129},{129,257},{257,385},{3... | collective-permute-start | bytes 663560 | tf_op jit(solution)/shard_map/ppermute | solution.py:366
  130.0 10.0 %collective-permute-start.2 = (bf16[144,768]{1,0:T(8,128)(2,1)}, bf16[144,768]{1,0:T(8,128)(2,1)}, u32[]{:S(2)}, u32[]{:S(2)}) collective-permute-start(bf16[144,768]{1,0:T(8,128)(2,1)} %get-tuple-element.41), channel_id=1, source_target_pairs={{0,384},{128,0},{256,128},{384,256},{1,385},{129,1},{257,129},{385... | collective-permute-start | bytes 663560 | tf_op jit(solution)/shard_map/ppermute | solution.py:367
  141.8 33.0 %all-to-all-start.2 = ((bf16[4,32,1664]{2,1,0:T(8,128)(2,1)}), bf16[4,32,1664]{2,1,0:T(8,128)(2,1)S(1)}, u32[]{:S(2)}, u32[]{:S(2)}) async-start(bf16[4,32,1664]{2,1,0:T(8,128)(2,1)} %bitcast.12), calls=%async_computation.2 | async-start | bytes 851968 | tf_op jit(solution)/shard_map/all_to_all | solution.py:389
  148.0 13.4 %collective-permute-start.4 = (bf16[288,768]{1,0:T(8,128)(2,1)}, bf16[288,768]{1,0:T(8,128)(2,1)S(1)}, u32[]{:S(2)}, u32[]{:S(2)}) collective-permute-start(bf16[288,768]{1,0:T(8,128)(2,1)} %get-tuple-element.45), channel_id=1, source_target_pairs={{0,384},{128,0},{256,128},{384,256},{1,385},{129,1},{257,129},{385... | collective-permute-start | bytes 1327112 | tf_op jit(solution)/shard_map/ppermute | solution.py:386
  150.0 12.1 %collective-permute-start.3 = (bf16[288,768]{1,0:T(8,128)(2,1)S(1)}, bf16[288,768]{1,0:T(8,128)(2,1)S(1)}, u32[]{:S(2)}, u32[]{:S(2)}) collective-permute-start(bf16[288,768]{1,0:T(8,128)(2,1)S(1)} %get-tuple-element.42), channel_id=1, source_target_pairs={{0,128},{128,256},{256,384},{384,0},{1,129},{129,257},{257,385},{3... | collective-permute-start | bytes 1327112 | tf_op jit(solution)/shard_map/ppermute | solution.py:386

commit v9 on v7

--- a/solution.py
+++ b/solution.py
@@ -193,14 +193,12 @@
         out_refs[s][...] = (keep[s].astype(F32) + got[s].astype(F32)).astype(BF16)
 
 
-def combine_kernel(base_ref, far_ref, back_ref, pick_ref, extra_ref, *refs):
-    out_refs, sum_ref = refs[:-1], refs[-1]
+def combine_kernel(base_ref, back_ref, pick_ref, extra_ref, sum_ref):
     slots = back_ref.shape[0]
     width = back_ref.shape[1] - LANES
-    tokens = pick_ref.shape[0]
-    block = tokens // FAR
+    tokens = sum_ref.shape[0]
     pick = pick_ref[...]
-    sum_ref[:, :, :width] = dot(pick, back_ref[:, :width]).astype(BF16).reshape(FAR, block, width)
+    sum_ref[:, :width] = dot(pick, back_ref[:, :width]).astype(BF16)
     expert, _, _ = slot_parts(iota((slots, LANES), 0))
     own = iota((slots, LANES), 1) == expert
     spread = jnp.where(own, back_ref[:, width:].astype(F32), 0.0).astype(BF16)
@@ -214,18 +212,16 @@
         value = jnp.sum(jnp.where(hit, by_expert, 0.0), axis=1, keepdims=True)
         value = value / extras[:, TOP + k : TOP + k + 1]
         result = jnp.where(lane == k, value, result)
-    sum_ref[:, :, width:] = result.astype(BF16).reshape(FAR, block, LANES)
-    for s, out_ref in enumerate(out_refs):
-        out_ref[...] = sum_ref[(far_ref[0] + s) & (FAR - 1)]
+    sum_ref[:, width:] = result.astype(BF16)
 
 
 def finish_kernel(*refs):
-    sum_refs, part_refs = refs[:FAR], refs[FAR:-5]
+    sums_ref, part_refs = refs[0], refs[1:-5]
     in_ref, prob_ref, gate_ref, up_ref, down_ref = refs[-5:]
     width = in_ref.shape[1]
-    total = sum_refs[0][...].astype(F32)
-    for ref in sum_refs[1:]:
-        total = total + ref[...].astype(F32)
+    total = sums_ref[0].astype(F32)
+    for s in range(1, FAR):
+        total = total + sums_ref[s].astype(F32)
     in_ref[...] = total[:, :width].astype(BF16)
     pick = jnp.where(iota((TOP, LANES), 0) == iota((TOP, LANES), 1), 1.0, 0.0).astype(BF16)
     prob_ref[...] = dot(pick, total[:, width:].astype(BF16), ((1,), (1,))).astype(BF16)
@@ -266,7 +262,6 @@
     part_rows = share + 2 * down_share
     core = lax.axis_index("core").astype(jnp.int32)
     chip = lax.axis_index("x").astype(jnp.int32)
-    far = lax.axis_index("far").astype(jnp.int32)
     moved = core * (NEAR // 2)
     place = lax.axis_index(("far", "near", "y")) - moved + EXPERTS
     base = ((place & -NEAR) + moved).astype(jnp.int32).reshape(1)
@@ -348,22 +343,19 @@
         name="chip_sums",
     )(chip.reshape(1), keep, got)
     parts = [
-        lax.ppermute(chip_sums[s], "x", [(i, (i + s) % chips) for i in range(chips)]) for s in range(1, chips)
+        lax.ppermute(chip_sums[s], "x", [(i, (i + s) % chips) for i in range(chips)]) for s in (2, 1, 3)
     ] + [chip_sums[0]]
 
     back, _ = lax.optimization_barrier((back, chip_sums[0]))
     sums = pl.pallas_call(
         combine_kernel,
-        out_shape=(shape(block, width + LANES),) * FAR,
-        in_specs=[scalar] * 2 + whole(3),
-        out_specs=tuple(whole(FAR)),
-        scratch_shapes=[pltpu.VMEM((FAR, block, width + LANES), BF16)],
+        out_shape=shape(tokens, width + LANES),
+        in_specs=[scalar] + whole(3),
+        out_specs=whole(1)[0],
         compiler_params=params(24),
         name="combine_rows",
-    )(base, far.reshape(1), back, pick, near_tokens[:, 2 * width :])
-    sums = [sums[0]] + [
-        lax.ppermute(sums[s], "far", [(i, (i + s) % FAR) for i in range(FAR)]) for s in range(1, FAR)
-    ]
+    )(base, back, pick, near_tokens[:, 2 * width :])
+    sums = exchange(sums.reshape(FAR, block, width + LANES), "far")
 
     grad_in, grad_probs, grad_gate, grad_up, grad_down = pl.pallas_call(
         finish_kernel,
@@ -374,11 +366,11 @@
             jax.ShapeDtypeStruct((share, hidden_width), F32),
             jax.ShapeDtypeStruct((down_share, width), F32),
         ),
-        in_specs=whole(FAR + len(parts)),
+        in_specs=whole(1 + len(parts)),
         out_specs=tuple(whole(5)),
         compiler_params=params(24),
         name="finish",
-    )(*sums, *parts)
+    )(sums, *parts)
     return grad_in, grad_probs.T, grad_gate[None], grad_up[None], grad_down[None]
 
 

time: 173 us -> 167 us (0.965)
  the two profiles are of different devices: /device:TPU:1 before, /device:TPU:6 now
where the time goes in v9:
time: 167 us; the launch traced here: 164 us
  blocking collectives  90.8 us (54%)
  starting transfers between devices  26.7 us (16%)
  waiting for transfers between devices  26.6 us (16%)
  Pallas kernels  19.5 us (12%)
    all_to_all x1, blocking collectives, per_device(): near_exchange(send.reshape(NEAR, FAR * CAP, 2 * width))  46.3 us
    all_gather x1, blocking collectives, per_device(): near_tokens = lax.all_gather(packed, 'far', tiled=True)  44.5 us
    ppermute x3, waiting for transfers between devices, per_device(): lax.ppermute(chip_sums[s], 'x', [(i, (i + s) % chips) for i in range(chip...  13.2 us
    all_to_all x1, waiting for transfers between devices, per_device(): near_exchange(back.reshape(NEAR, FAR * CAP, width + LANES))  9.76 us
    ppermute x3, starting transfers between devices, per_device(): lax.ppermute(chip_sums[s], 'x', [(i, (i + s) % chips) for i in range(chip...  9.23 us
    all_to_all x1, starting transfers between devices, per_device(): sums = exchange(sums.reshape(FAR, block, width + LANES), 'far')  7.15 us
    all_to_all x1, starting transfers between devices, per_device(): near_exchange(back.reshape(NEAR, FAR * CAP, width + LANES))  6.02 us
    pallas_call x1, Pallas kernels, per_device(): pl.pallas_call(part_kernel, out_shape=(shape(chips, part_rows, 2 * hidden...  5.73 us
  transfers between devices with their start and end apart: 6, of which 5 were waited for; matrix products, arithmetic and copies ran while one was open for 0% of the time, Pallas kernels for 5%

profile of v9, /device:TPU:6, one launch (start us, length us, event | category | flops | bytes accessed | tf_op | source)
XLA Modules:
  0.0 164.4 jit_solution(12503316372864333928)
XLA Ops:
  0.6 2.3 %pack_tokens.1 = bf16[32,3200]{1,0:T(8,128)(2,1)} custom-call(bf16[32,1536]{1,0:T(8,128)(2,1)} %layer_ref.1, bf16[32,1536]{1,0:T(8,128)(2,1)} %grad_ref.1, s32[8,32]{1,0:T(8,128)} %bitcast.24, bf16[8,32]{1,0:T(8,128)(2,1)} %bitcast.25), custom_call_target="tpu_custom_call" | custom-call | tf_op jit(solution)/shard_map/pack_tokens/pallas_call | solution.py:274
  3.0 44.5 %all_gather.3.tok_ref = bf16[128,3200]{1,0:T(8,128)(2,1)S(1)} all-gather(bf16[32,3200]{1,0:T(8,128)(2,1)} %pack_tokens.1), channel_id=1, replica_groups=mesh['x'=4,'core'=2,'far'=4,'near'=4,'y'=4] {'far'}, dimensions={0}, use_global_device_ids=true | all-gather | bytes 1024000 | tf_op jit(solution)/shard_map/all_gather | solution.py:283
  47.5 1.5 select_rows.1
  48.9 0.0 copy-start.1
  48.9 0.0 copy-start.2
  49.0 0.0 copy-start.3
  49.0 46.3 %all_to_all.15 = bf16[16,24,3072]{2,1,0:T(8,128)(2,1)S(1)} all-to-all(bf16[16,24,3072]{2,1,0:T(8,128)(2,1)S(1)} %bitcast.20), channel_id=1, replica_groups={{0,1,2,3,4,5,6,7,8,9,10,11,12,13,14,15},{16,17,18,19,20,21,22,23,24,25,..., dimensions={0} | all-to-all | bytes 4718592 | tf_op jit(solution)/shard_map/all_to_all | solution.py:300
  95.3 0.0 copy-start
  95.3 0.0 copy-done.1
  95.3 0.0 copy-done.2
  95.3 0.0 copy-done.3
  95.3 4.5 %expert_rows.1 = (bf16[384,1664]{1,0:T(8,128)(2,1)}, bf16[384,768]{1,0:T(8,128)(2,1)S(1)}, bf16[384,384]{1,0:T(8,128)(2,1)S(1)}) custom-call(bf16[384,3072]{1,0:T(8,128)(2,1)S(1)} %bitcast.18, bf16[1536,384]{1,0:T(8,128)(2,1)S(1)} %bitcast.21, bf16[1536,384]{1,0:T(8,128)(2,1)S(1)} %bitcast.22, bf16[384,1536]{1,0:T(8,128)(2,1)S(1)} %bitcast.23), custom_call_target="tpu_custom_call" | custom-call | flops 2264924160 | bytes 8388608 | tf_op jit(solution)/shard_map/expert_rows/pallas_call | solution.py:303
  99.8 0.0 copy-done
  99.8 6.0 %all-to-all-start.1 = ((bf16[16,24,1664]{2,1,0:T(8,128)(2,1)}), bf16[16,24,1664]{2,1,0:T(8,128)(2,1)S(1)}, u32[]{:S(2)}, u32[]{:S(2)}) async-start(bf16[16,24,1664]{2,1,0:T(8,128)(2,1)} %bitcast.8), calls=%async_computation.1 | async-start | bytes 2555904 | tf_op jit(solution)/shard_map/all_to_all | solution.py:312
  105.8 5.7 %weight_parts.1 = (bf16[4,288,768]{2,1,0:T(8,128)(2,1)}, bf16[4,288,768]{2,1,0:T(8,128)(2,1)}) custom-call(s32[1]{0:T(128)} %bitcast.11.core_ref, bf16[384,3072]{1,0:T(8,128)(2,1)} %bitcast.19, bf16[384,768]{1,0:T(8,128)(2,1)S(1)} %get-tuple-element.24.both_ref, bf16[384,384]{1,0:T(8,128)(2,1)S(1)} %get-tuple-element.25.hidden_ref), custom_call_target="tpu_custom_call" | custom-call | flops 1358954496 | bytes 8388608 | tf_op jit(solution)/shard_map/weight_parts/pallas_call | solution.py:314
  111.5 4.3 %collective-permute-start = (bf16[4,288,768]{2,1,0:T(8,128)(2,1)}, bf16[4,288,768]{2,1,0:T(8,128)(2,1)}, u32[]{:S(2)}, u32[]{:S(2)}) collective-permute-start(bf16[4,288,768]{2,1,0:T(8,128)(2,1)} %get-tuple-element.27), channel_id=1, source_target_pairs={{0,64},{64,0},{1,65},{65,1},{2,66},{66,2},{3,67},{67,3},{4,68},{68... | collective-permute-start | bytes 5308424 | tf_op jit(solution)/shard_map/ppermute | solution.py:330
  115.9 3.6 %collective-permute-done.got_hbm = bf16[4,288,768]{2,1,0:T(8,128)(2,1)} collective-permute-done((bf16[4,288,768]{2,1,0:T(8,128)(2,1)}, bf16[4,288,768]{2,1,0:T(8,128)(2,1)}, u32[]{:S(2)}, u32[]{:S(2)}) %collective-permute-start) | collective-permute-done | bytes 1769504 | tf_op jit(solution)/shard_map/ppermute | solution.py:330
  119.5 2.8 %chip_sums.1 = (bf16[288,768]{1,0:T(8,128)(2,1)S(1)}, bf16[288,768]{1,0:T(8,128)(2,1)S(1)}, bf16[288,768]{1,0:T(8,128)(2,1)}, bf16[288,768]{1,0:T(8,128)(2,1)S(1)}) custom-call(s32[1]{0:T(128)} %bitcast.10.chip_ref, bf16[4,288,768]{2,1,0:T(8,128)(2,1)} %get-tuple-element.26.keep_hbm, bf16[4,288,768]{2,1,0:T(8,128)(2,1)} %collective-permute-done.got_hbm), custom_call_target="tpu_custom_call" | custom-call | flops 1048576 | bytes 6291456 | tf_op jit(solution)/shard_map/chip_sums/pallas_call | solution.py:331
  122.3 9.8 %all-to-all-done.1 = bf16[16,24,1664]{2,1,0:T(8,128)(2,1)S(1)} async-done(((bf16[16,24,1664]{2,1,0:T(8,128)(2,1)}), bf16[16,24,1664]{2,1,0:T(8,128)(2,1)S(1)}, u32[]{:S(2)}, u32[]{:S(2)}) %all-to-all-start.1) | async-done | bytes 1277984 | tf_op jit(solution)/shard_map/all_to_all | solution.py:312
  132.1 1.6 combine_rows.1
  133.7 7.1 %all-to-all-start.2 = ((bf16[4,32,1664]{2,1,0:T(8,128)(2,1)}), bf16[4,32,1664]{2,1,0:T(8,128)(2,1)S(1)}, u32[]{:S(2)}, u32[]{:S(2)}) async-start(bf16[4,32,1664]{2,1,0:T(8,128)(2,1)} %bitcast.12), calls=%async_computation.2 | async-start | bytes 851968 | tf_op jit(solution)/shard_map/all_to_all | solution.py:358
  140.8 3.3 %collective-permute-start.1 = (bf16[288,768]{1,0:T(8,128)(2,1)}, bf16[288,768]{1,0:T(8,128)(2,1)S(1)}, u32[]{:S(2)}, u32[]{:S(2)}) collective-permute-start(bf16[288,768]{1,0:T(8,128)(2,1)} %get-tuple-element.31), channel_id=1, source_target_pairs={{0,256},{128,384},{256,0},{384,128},{1,257},{129,385},{257,1},{385... | collective-permute-start | bytes 1327112 | tf_op jit(solution)/shard_map/ppermute | solution.py:346
  144.1 4.0 %collective-permute-start.2 = (bf16[288,768]{1,0:T(8,128)(2,1)S(1)}, bf16[288,768]{1,0:T(8,128)(2,1)S(1)}, u32[]{:S(2)}, u32[]{:S(2)}) collective-permute-start(bf16[288,768]{1,0:T(8,128)(2,1)S(1)} %get-tuple-element.32), channel_id=1, source_target_pairs={{0,128},{128,256},{256,384},{384,0},{1,129},{129,257},{257,385},{3... | collective-permute-start | bytes 1327112 | tf_op jit(solution)/shard_map/ppermute | solution.py:346
  148.2 1.9 %collective-permute-start.3 = (bf16[288,768]{1,0:T(8,128)(2,1)S(1)}, bf16[288,768]{1,0:T(8,128)(2,1)S(1)}, u32[]{:S(2)}, u32[]{:S(2)}) collective-permute-start(bf16[288,768]{1,0:T(8,128)(2,1)S(1)} %get-tuple-element.33), channel_id=1, source_target_pairs={{0,384},{128,0},{256,128},{384,256},{1,385},{129,1},{257,129},{385... | collective-permute-start | bytes 1327112 | tf_op jit(solution)/shard_map/ppermute | solution.py:346
  150.1 7.5 %collective-permute-done.1.refs_1_ = bf16[288,768]{1,0:T(8,128)(2,1)S(1)} collective-permute-done((bf16[288,768]{1,0:T(8,128)(2,1)}, bf16[288,768]{1,0:T(8,128)(2,1)S(1)}, u32[]{:S(2)}, u32[]{:S(2)}) %collective-permute-start.1) | collective-permute-done | bytes 442400 | tf_op jit(solution)/shard_map/ppermute | solution.py:346
  157.5 3.0 %collective-permute-done.2.refs_2_ = bf16[288,768]{1,0:T(8,128)(2,1)S(1)} collective-permute-done((bf16[288,768]{1,0:T(8,128)(2,1)S(1)}, bf16[288,768]{1,0:T(8,128)(2,1)S(1)}, u32[]{:S(2)}, u32[]{:S(2)}) %collective-permute-start.2) | collective-permute-done | bytes 442400 | tf_op jit(solution)/shard_map/ppermute | solution.py:346
  160.5 2.7 %collective-permute-done.3.refs_3_ = bf16[288,768]{1,0:T(8,128)(2,1)S(1)} collective-permute-done((bf16[288,768]{1,0:T(8,128)(2,1)S(1)}, bf16[288,768]{1,0:T(8,128)(2,1)S(1)}, u32[]{:S(2)}, u32[]{:S(2)}) %collective-permute-start.3) | collective-permute-done | bytes 442400 | tf_op jit(solution)/shard_map/ppermute | solution.py:346
  163.3 0.0 all-to-all-done.2.refs_0_
  163.3 1.1 finish.1
  (1 shorter events, 0.0 us)
Async XLA Ops:
  48.9 46.3 %copy-start.1 = (bf16[1,1536,384]{2,1,0:T(8,128)(2,1)S(1)}, bf16[1,1536,384]{2,1,0:T(8,128)(2,1)}, u32[]{:S(2)}) copy-start(bf16[1,1536,384]{2,1,0:T(8,128)(2,1)} %param.11) | copy-start | bytes 3538948
  48.9 46.3 %copy-start.2 = (bf16[1,1536,384]{2,1,0:T(8,128)(2,1)S(1)}, bf16[1,1536,384]{2,1,0:T(8,128)(2,1)}, u32[]{:S(2)}) copy-start(bf16[1,1536,384]{2,1,0:T(8,128)(2,1)} %param.12) | copy-start | bytes 3538948
  49.0 46.3 %copy-start.3 = (bf16[1,384,1536]{2,1,0:T(8,128)(2,1)S(1)}, bf16[1,384,1536]{2,1,0:T(8,128)(2,1)}, u32[]{:S(2)}) copy-start(bf16[1,384,1536]{2,1,0:T(8,128)(2,1)} %param.13) | copy-start | bytes 3538948
  95.3 4.5 %copy-start = (bf16[16,24,3072]{2,1,0:T(8,128)(2,1)}, bf16[16,24,3072]{2,1,0:T(8,128)(2,1)S(1)}, u32[]{:S(2)}) copy-start(bf16[16,24,3072]{2,1,0:T(8,128)(2,1)S(1)} %all_to_all.15) | copy-start | bytes 7077892
  99.8 32.3 %all-to-all-start.1 = ((bf16[16,24,1664]{2,1,0:T(8,128)(2,1)}), bf16[16,24,1664]{2,1,0:T(8,128)(2,1)S(1)}, u32[]{:S(2)}, u32[]{:S(2)}) async-start(bf16[16,24,1664]{2,1,0:T(8,128)(2,1)} %bitcast.8), calls=%async_computation.1 | async-start | bytes 2555904 | tf_op jit(solution)/shard_map/all_to_all | solution.py:312
  111.5 8.0 %collective-permute-start = (bf16[4,288,768]{2,1,0:T(8,128)(2,1)}, bf16[4,288,768]{2,1,0:T(8,128)(2,1)}, u32[]{:S(2)}, u32[]{:S(2)}) collective-permute-start(bf16[4,288,768]{2,1,0:T(8,128)(2,1)} %get-tuple-element.27), channel_id=1, source_target_pairs={{0,64},{64,0},{1,65},{65,1},{2,66},{66,2},{3,67},{67,3},{4,68},{68... | collective-permute-start | bytes 5308424 | tf_op jit(solution)/shard_map/ppermute | solution.py:330
  133.7 29.6 %all-to-all-start.2 = ((bf16[4,32,1664]{2,1,0:T(8,128)(2,1)}), bf16[4,32,1664]{2,1,0:T(8,128)(2,1)S(1)}, u32[]{:S(2)}, u32[]{:S(2)}) async-start(bf16[4,32,1664]{2,1,0:T(8,128)(2,1)} %bitcast.12), calls=%async_computation.2 | async-start | bytes 851968 | tf_op jit(solution)/shard_map/all_to_all | solution.py:358
  140.8 16.7 %collective-permute-start.1 = (bf16[288,768]{1,0:T(8,128)(2,1)}, bf16[288,768]{1,0:T(8,128)(2,1)S(1)}, u32[]{:S(2)}, u32[]{:S(2)}) collective-permute-start(bf16[288,768]{1,0:T(8,128)(2,1)} %get-tuple-element.31), channel_id=1, source_target_pairs={{0,256},{128,384},{256,0},{384,128},{1,257},{129,385},{257,1},{385... | collective-permute-start | bytes 1327112 | tf_op jit(solution)/shard_map/ppermute | solution.py:346
  144.1 16.4 %collective-permute-start.2 = (bf16[288,768]{1,0:T(8,128)(2,1)S(1)}, bf16[288,768]{1,0:T(8,128)(2,1)S(1)}, u32[]{:S(2)}, u32[]{:S(2)}) collective-permute-start(bf16[288,768]{1,0:T(8,128)(2,1)S(1)} %get-tuple-element.32), channel_id=1, source_target_pairs={{0,128},{128,256},{256,384},{384,0},{1,129},{129,257},{257,385},{3... | collective-permute-start | bytes 1327112 | tf_op jit(solution)/shard_map/ppermute | solution.py:346
  148.2 15.1 %collective-permute-start.3 = (bf16[288,768]{1,0:T(8,128)(2,1)S(1)}, bf16[288,768]{1,0:T(8,128)(2,1)S(1)}, u32[]{:S(2)}, u32[]{:S(2)}) collective-permute-start(bf16[288,768]{1,0:T(8,128)(2,1)S(1)} %get-tuple-element.33), channel_id=1, source_target_pairs={{0,384},{128,0},{256,128},{384,256},{1,385},{129,1},{257,129},{385... | collective-permute-start | bytes 1327112 | tf_op jit(solution)/shard_map/ppermute | solution.py:346

commit v10 on v9

--- a/solution.py
+++ b/solution.py
@@ -215,9 +215,7 @@
     sum_ref[:, width:] = result.astype(BF16)
 
 
-def finish_kernel(*refs):
-    sums_ref, part_refs = refs[0], refs[1:-5]
-    in_ref, prob_ref, gate_ref, up_ref, down_ref = refs[-5:]
+def finish_kernel(sums_ref, in_ref, prob_ref):
     width = in_ref.shape[1]
     total = sums_ref[0].astype(F32)
     for s in range(1, FAR):
@@ -225,8 +223,12 @@
     in_ref[...] = total[:, :width].astype(BF16)
     pick = jnp.where(iota((TOP, LANES), 0) == iota((TOP, LANES), 1), 1.0, 0.0).astype(BF16)
     prob_ref[...] = dot(pick, total[:, width:].astype(BF16), ((1,), (1,))).astype(BF16)
+
+
+def weight_sum_kernel(*refs):
+    part_refs, (gate_ref, up_ref, down_ref) = refs[:-3], refs[-3:]
     share, hidden_width = gate_ref.shape
-    down_share = down_ref.shape[0]
+    down_share, width = down_ref.shape
     half = width // 2
 
     def part(low, size):
@@ -357,20 +359,27 @@
     )(base, back, pick, near_tokens[:, 2 * width :])
     sums = exchange(sums.reshape(FAR, block, width + LANES), "far")
 
-    grad_in, grad_probs, grad_gate, grad_up, grad_down = pl.pallas_call(
-        finish_kernel,
+    grad_gate, grad_up, grad_down = pl.pallas_call(
+        weight_sum_kernel,
         out_shape=(
-            shape(block, width),
-            shape(TOP, block),
             jax.ShapeDtypeStruct((share, hidden_width), F32),
             jax.ShapeDtypeStruct((share, hidden_width), F32),
             jax.ShapeDtypeStruct((down_share, width), F32),
         ),
-        in_specs=whole(1 + len(parts)),
-        out_specs=tuple(whole(5)),
+        in_specs=whole(chips),
+        out_specs=tuple(whole(3)),
+        compiler_params=params(24),
+        cost_estimate=cost(MIB, 3 * MIB),
+        name="weight_sums",
+    )(*parts)
+    grad_in, grad_probs = pl.pallas_call(
+        finish_kernel,
+        out_shape=(shape(block, width), shape(TOP, block)),
+        in_specs=whole(1),
+        out_specs=tuple(whole(2)),
         compiler_params=params(24),
         name="finish",
-    )(sums, *parts)
+    )(sums)
     return grad_in, grad_probs.T, grad_gate[None], grad_up[None], grad_down[None]
 
 

time: 167 us -> 167 us (level)
  no operation moved by 1% of the time
where the time goes in v10:
time: 167 us; the launch traced here: 165 us
  blocking collectives  90.8 us (54%)
  waiting for transfers between devices  27.1 us (16%)
  starting transfers between devices  26.7 us (16%)
  Pallas kernels  19.5 us (12%)
    all_to_all x1, blocking collectives, per_device(): near_exchange(send.reshape(NEAR, FAR * CAP, 2 * width))  46.3 us
    all_gather x1, blocking collectives, per_device(): near_tokens = lax.all_gather(packed, 'far', tiled=True)  44.5 us
    ppermute x3, waiting for transfers between devices, per_device(): lax.ppermute(chip_sums[s], 'x', [(i, (i + s) % chips) for i in range(chip...  13 us
    all_to_all x1, waiting for transfers between devices, per_device(): near_exchange(back.reshape(NEAR, FAR * CAP, width + LANES))  10.4 us
    ppermute x3, starting transfers between devices, per_device(): lax.ppermute(chip_sums[s], 'x', [(i, (i + s) % chips) for i in range(chip...  9.22 us
    all_to_all x1, starting transfers between devices, per_device(): sums = exchange(sums.reshape(FAR, block, width + LANES), 'far')  7.14 us
    all_to_all x1, starting transfers between devices, per_device(): near_exchange(back.reshape(NEAR, FAR * CAP, width + LANES))  6.02 us
    pallas_call x1, Pallas kernels, per_device(): pl.pallas_call(part_kernel, out_shape=(shape(chips, part_rows, 2 * hidden...  5.73 us
  transfers between devices with their start and end apart: 6, of which 5 were waited for; matrix products, arithmetic and copies ran while one was open for 0% of the time, Pallas kernels for 5%

profile of v10, /device:TPU:6, one launch (start us, length us, event | category | flops | bytes accessed | tf_op | source)
XLA Modules:
  0.0 164.8 jit_solution(8972434860630709426)
XLA Ops:
  0.6 2.3 %pack_tokens.1 = bf16[32,3200]{1,0:T(8,128)(2,1)} custom-call(bf16[32,1536]{1,0:T(8,128)(2,1)} %layer_ref.1, bf16[32,1536]{1,0:T(8,128)(2,1)} %grad_ref.1, s32[8,32]{1,0:T(8,128)} %bitcast.24, bf16[8,32]{1,0:T(8,128)(2,1)} %bitcast.25), custom_call_target="tpu_custom_call" | custom-call | tf_op jit(solution)/shard_map/pack_tokens/pallas_call | solution.py:276
  3.0 44.5 %all_gather.3.tok_ref = bf16[128,3200]{1,0:T(8,128)(2,1)S(1)} all-gather(bf16[32,3200]{1,0:T(8,128)(2,1)} %pack_tokens.1), channel_id=1, replica_groups=mesh['x'=4,'core'=2,'far'=4,'near'=4,'y'=4] {'far'}, dimensions={0}, use_global_device_ids=true | all-gather | bytes 1024000 | tf_op jit(solution)/shard_map/all_gather | solution.py:285
  47.5 1.5 select_rows.1
  48.9 0.0 copy-start.1
  48.9 0.0 copy-start.2
  49.0 0.0 copy-start.3
  49.0 46.3 %all_to_all.15 = bf16[16,24,3072]{2,1,0:T(8,128)(2,1)S(1)} all-to-all(bf16[16,24,3072]{2,1,0:T(8,128)(2,1)S(1)} %bitcast.20), channel_id=1, replica_groups={{0,1,2,3,4,5,6,7,8,9,10,11,12,13,14,15},{16,17,18,19,20,21,22,23,24,25,..., dimensions={0} | all-to-all | bytes 4718592 | tf_op jit(solution)/shard_map/all_to_all | solution.py:302
  95.3 0.0 copy-start
  95.3 0.0 copy-done.1
  95.3 0.0 copy-done.2
  95.3 0.0 copy-done.3
  95.3 4.5 %expert_rows.1 = (bf16[384,1664]{1,0:T(8,128)(2,1)}, bf16[384,768]{1,0:T(8,128)(2,1)S(1)}, bf16[384,384]{1,0:T(8,128)(2,1)S(1)}) custom-call(bf16[384,3072]{1,0:T(8,128)(2,1)S(1)} %bitcast.18, bf16[1536,384]{1,0:T(8,128)(2,1)S(1)} %bitcast.21, bf16[1536,384]{1,0:T(8,128)(2,1)S(1)} %bitcast.22, bf16[384,1536]{1,0:T(8,128)(2,1)S(1)} %bitcast.23), custom_call_target="tpu_custom_call" | custom-call | flops 2264924160 | bytes 8388608 | tf_op jit(solution)/shard_map/expert_rows/pallas_call | solution.py:305
  99.8 0.0 copy-done
  99.8 6.0 %all-to-all-start.1 = ((bf16[16,24,1664]{2,1,0:T(8,128)(2,1)}), bf16[16,24,1664]{2,1,0:T(8,128)(2,1)S(1)}, u32[]{:S(2)}, u32[]{:S(2)}) async-start(bf16[16,24,1664]{2,1,0:T(8,128)(2,1)} %bitcast.8), calls=%async_computation.1 | async-start | bytes 2555904 | tf_op jit(solution)/shard_map/all_to_all | solution.py:314
  105.8 5.7 %weight_parts.1 = (bf16[4,288,768]{2,1,0:T(8,128)(2,1)}, bf16[4,288,768]{2,1,0:T(8,128)(2,1)}) custom-call(s32[1]{0:T(128)} %bitcast.11.core_ref, bf16[384,3072]{1,0:T(8,128)(2,1)} %bitcast.19, bf16[384,768]{1,0:T(8,128)(2,1)S(1)} %get-tuple-element.24.both_ref, bf16[384,384]{1,0:T(8,128)(2,1)S(1)} %get-tuple-element.25.hidden_ref), custom_call_target="tpu_custom_call" | custom-call | flops 1358954496 | bytes 8388608 | tf_op jit(solution)/shard_map/weight_parts/pallas_call | solution.py:316
  111.5 4.3 %collective-permute-start = (bf16[4,288,768]{2,1,0:T(8,128)(2,1)}, bf16[4,288,768]{2,1,0:T(8,128)(2,1)}, u32[]{:S(2)}, u32[]{:S(2)}) collective-permute-start(bf16[4,288,768]{2,1,0:T(8,128)(2,1)} %get-tuple-element.27), channel_id=1, source_target_pairs={{0,64},{64,0},{1,65},{65,1},{2,66},{66,2},{3,67},{67,3},{4,68},{68... | collective-permute-start | bytes 5308424 | tf_op jit(solution)/shard_map/ppermute | solution.py:332
  115.9 3.6 %collective-permute-done.got_hbm = bf16[4,288,768]{2,1,0:T(8,128)(2,1)} collective-permute-done((bf16[4,288,768]{2,1,0:T(8,128)(2,1)}, bf16[4,288,768]{2,1,0:T(8,128)(2,1)}, u32[]{:S(2)}, u32[]{:S(2)}) %collective-permute-start) | collective-permute-done | bytes 1769504 | tf_op jit(solution)/shard_map/ppermute | solution.py:332
  119.5 2.1 %chip_sums.1 = (bf16[288,768]{1,0:T(8,128)(2,1)S(1)}, bf16[288,768]{1,0:T(8,128)(2,1)S(1)}, bf16[288,768]{1,0:T(8,128)(2,1)S(1)}, bf16[288,768]{1,0:T(8,128)(2,1)S(1)}) custom-call(s32[1]{0:T(128)} %bitcast.10.chip_ref, bf16[4,288,768]{2,1,0:T(8,128)(2,1)} %get-tuple-element.26.keep_hbm, bf16[4,288,768]{2,1,0:T(8,128)(2,1)} %collective-permute-done.got_hbm), custom_call_target="tpu_custom_call" | custom-call | flops 1048576 | bytes 6291456 | tf_op jit(solution)/shard_map/chip_sums/pallas_call | solution.py:333
  121.6 10.4 %all-to-all-done.1 = bf16[16,24,1664]{2,1,0:T(8,128)(2,1)S(1)} async-done(((bf16[16,24,1664]{2,1,0:T(8,128)(2,1)}), bf16[16,24,1664]{2,1,0:T(8,128)(2,1)S(1)}, u32[]{:S(2)}, u32[]{:S(2)}) %all-to-all-start.1) | async-done | bytes 1277984 | tf_op jit(solution)/shard_map/all_to_all | solution.py:314
  132.1 1.6 combine_rows.1
  133.7 7.1 %all-to-all-start.2 = ((bf16[4,32,1664]{2,1,0:T(8,128)(2,1)}), bf16[4,32,1664]{2,1,0:T(8,128)(2,1)S(1)}, u32[]{:S(2)}, u32[]{:S(2)}) async-start(bf16[4,32,1664]{2,1,0:T(8,128)(2,1)} %bitcast.12), calls=%async_computation.2 | async-start | bytes 851968 | tf_op jit(solution)/shard_map/all_to_all | solution.py:360
  140.8 3.3 %collective-permute-start.1 = (bf16[288,768]{1,0:T(8,128)(2,1)S(1)}, bf16[288,768]{1,0:T(8,128)(2,1)S(1)}, u32[]{:S(2)}, u32[]{:S(2)}) collective-permute-start(bf16[288,768]{1,0:T(8,128)(2,1)S(1)} %get-tuple-element.33), channel_id=1, source_target_pairs={{0,256},{128,384},{256,0},{384,128},{1,257},{129,385},{257,1},{385... | collective-permute-start | bytes 1327112 | tf_op jit(solution)/shard_map/ppermute | solution.py:348
  144.1 4.0 %collective-permute-start.2 = (bf16[288,768]{1,0:T(8,128)(2,1)S(1)}, bf16[288,768]{1,0:T(8,128)(2,1)S(1)}, u32[]{:S(2)}, u32[]{:S(2)}) collective-permute-start(bf16[288,768]{1,0:T(8,128)(2,1)S(1)} %get-tuple-element.34), channel_id=1, source_target_pairs={{0,128},{128,256},{256,384},{384,0},{1,129},{129,257},{257,385},{3... | collective-permute-start | bytes 1327112 | tf_op jit(solution)/shard_map/ppermute | solution.py:348
  148.1 1.9 %collective-permute-start.3 = (bf16[288,768]{1,0:T(8,128)(2,1)S(1)}, bf16[288,768]{1,0:T(8,128)(2,1)S(1)}, u32[]{:S(2)}, u32[]{:S(2)}) collective-permute-start(bf16[288,768]{1,0:T(8,128)(2,1)S(1)} %get-tuple-element.35), channel_id=1, source_target_pairs={{0,384},{128,0},{256,128},{384,256},{1,385},{129,1},{257,129},{385... | collective-permute-start | bytes 1327112 | tf_op jit(solution)/shard_map/ppermute | solution.py:348
  150.1 7.1 %collective-permute-done.1.refs_0_ = bf16[288,768]{1,0:T(8,128)(2,1)S(1)} collective-permute-done((bf16[288,768]{1,0:T(8,128)(2,1)S(1)}, bf16[288,768]{1,0:T(8,128)(2,1)S(1)}, u32[]{:S(2)}, u32[]{:S(2)}) %collective-permute-start.1) | collective-permute-done | bytes 442400 | tf_op jit(solution)/shard_map/ppermute | solution.py:348
  157.2 3.1 %collective-permute-done.2.refs_1_ = bf16[288,768]{1,0:T(8,128)(2,1)S(1)} collective-permute-done((bf16[288,768]{1,0:T(8,128)(2,1)S(1)}, bf16[288,768]{1,0:T(8,128)(2,1)S(1)}, u32[]{:S(2)}, u32[]{:S(2)}) %collective-permute-start.2) | collective-permute-done | bytes 442400 | tf_op jit(solution)/shard_map/ppermute | solution.py:348
  160.3 2.8 %collective-permute-done.3.refs_2_ = bf16[288,768]{1,0:T(8,128)(2,1)S(1)} collective-permute-done((bf16[288,768]{1,0:T(8,128)(2,1)S(1)}, bf16[288,768]{1,0:T(8,128)(2,1)S(1)}, u32[]{:S(2)}, u32[]{:S(2)}) %collective-permute-start.3) | collective-permute-done | bytes 442400 | tf_op jit(solution)/shard_map/ppermute | solution.py:348
  163.1 1.0 weight_sums.1
  164.1 0.0 all-to-all-done.2.sums_ref
  164.1 0.7 finish.1
  (1 shorter events, 0.0 us)
Async XLA Ops:
  48.9 46.3 %copy-start.1 = (bf16[1,1536,384]{2,1,0:T(8,128)(2,1)S(1)}, bf16[1,1536,384]{2,1,0:T(8,128)(2,1)}, u32[]{:S(2)}) copy-start(bf16[1,1536,384]{2,1,0:T(8,128)(2,1)} %param.11) | copy-start | bytes 3538948
  48.9 46.3 %copy-start.2 = (bf16[1,1536,384]{2,1,0:T(8,128)(2,1)S(1)}, bf16[1,1536,384]{2,1,0:T(8,128)(2,1)}, u32[]{:S(2)}) copy-start(bf16[1,1536,384]{2,1,0:T(8,128)(2,1)} %param.12) | copy-start | bytes 3538948
  49.0 46.3 %copy-start.3 = (bf16[1,384,1536]{2,1,0:T(8,128)(2,1)S(1)}, bf16[1,384,1536]{2,1,0:T(8,128)(2,1)}, u32[]{:S(2)}) copy-start(bf16[1,384,1536]{2,1,0:T(8,128)(2,1)} %param.13) | copy-start | bytes 3538948
  95.3 4.5 %copy-start = (bf16[16,24,3072]{2,1,0:T(8,128)(2,1)}, bf16[16,24,3072]{2,1,0:T(8,128)(2,1)S(1)}, u32[]{:S(2)}) copy-start(bf16[16,24,3072]{2,1,0:T(8,128)(2,1)S(1)} %all_to_all.15) | copy-start | bytes 7077892
  99.8 32.3 %all-to-all-start.1 = ((bf16[16,24,1664]{2,1,0:T(8,128)(2,1)}), bf16[16,24,1664]{2,1,0:T(8,128)(2,1)S(1)}, u32[]{:S(2)}, u32[]{:S(2)}) async-start(bf16[16,24,1664]{2,1,0:T(8,128)(2,1)} %bitcast.8), calls=%async_computation.1 | async-start | bytes 2555904 | tf_op jit(solution)/shard_map/all_to_all | solution.py:314
  111.5 8.0 %collective-permute-start = (bf16[4,288,768]{2,1,0:T(8,128)(2,1)}, bf16[4,288,768]{2,1,0:T(8,128)(2,1)}, u32[]{:S(2)}, u32[]{:S(2)}) collective-permute-start(bf16[4,288,768]{2,1,0:T(8,128)(2,1)} %get-tuple-element.27), channel_id=1, source_target_pairs={{0,64},{64,0},{1,65},{65,1},{2,66},{66,2},{3,67},{67,3},{4,68},{68... | collective-permute-start | bytes 5308424 | tf_op jit(solution)/shard_map/ppermute | solution.py:332
  133.7 30.4 %all-to-all-start.2 = ((bf16[4,32,1664]{2,1,0:T(8,128)(2,1)}), bf16[4,32,1664]{2,1,0:T(8,128)(2,1)S(1)}, u32[]{:S(2)}, u32[]{:S(2)}) async-start(bf16[4,32,1664]{2,1,0:T(8,128)(2,1)} %bitcast.12), calls=%async_computation.2 | async-start | bytes 851968 | tf_op jit(solution)/shard_map/all_to_all | solution.py:360
  140.8 16.4 %collective-permute-start.1 = (bf16[288,768]{1,0:T(8,128)(2,1)S(1)}, bf16[288,768]{1,0:T(8,128)(2,1)S(1)}, u32[]{:S(2)}, u32[]{:S(2)}) collective-permute-start(bf16[288,768]{1,0:T(8,128)(2,1)S(1)} %get-tuple-element.33), channel_id=1, source_target_pairs={{0,256},{128,384},{256,0},{384,128},{1,257},{129,385},{257,1},{385... | collective-permute-start | bytes 1327112 | tf_op jit(solution)/shard_map/ppermute | solution.py:348
  144.1 16.2 %collective-permute-start.2 = (bf16[288,768]{1,0:T(8,128)(2,1)S(1)}, bf16[288,768]{1,0:T(8,128)(2,1)S(1)}, u32[]{:S(2)}, u32[]{:S(2)}) collective-permute-start(bf16[288,768]{1,0:T(8,128)(2,1)S(1)} %get-tuple-element.34), channel_id=1, source_target_pairs={{0,128},{128,256},{256,384},{384,0},{1,129},{129,257},{257,385},{3... | collective-permute-start | bytes 1327112 | tf_op jit(solution)/shard_map/ppermute | solution.py:348
  148.1 14.9 %collective-permute-start.3 = (bf16[288,768]{1,0:T(8,128)(2,1)S(1)}, bf16[288,768]{1,0:T(8,128)(2,1)S(1)}, u32[]{:S(2)}, u32[]{:S(2)}) collective-permute-start(bf16[288,768]{1,0:T(8,128)(2,1)S(1)} %get-tuple-element.35), channel_id=1, source_target_pairs={{0,384},{128,0},{256,128},{384,256},{1,385},{129,1},{257,129},{385... | collective-permute-start | bytes 1327112 | tf_op jit(solution)/shard_map/ppermute | solution.py:348

commit v11 on v10

--- a/solution.py
+++ b/solution.py
@@ -16,6 +16,7 @@
 TOP = 8
 EXPERTS = 64
 MIB = 1 << 20
+PLACING_FLOPS = 10**11
 
 
 def iota(shape, dim):
@@ -369,7 +370,7 @@
         in_specs=whole(chips),
         out_specs=tuple(whole(3)),
         compiler_params=params(24),
-        cost_estimate=cost(MIB, 3 * MIB),
+        cost_estimate=cost(PLACING_FLOPS, 3 * MIB),
         name="weight_sums",
     )(*parts)
     grad_in, grad_probs = pl.pallas_call(

time: 167 us -> 170 us (1.018)
  the two profiles are of different devices: /device:TPU:6 before, /device:TPU:33 now
where the time goes in v11:
time: 170 us; the launch traced here: 169 us
  blocking collectives  89.3 us (53%)
  waiting for transfers between devices  29 us (17%)
  starting transfers between devices  28.9 us (17%)
  Pallas kernels  21.4 us (13%)
    all_to_all x1, blocking collectives, per_device(): near_exchange(send.reshape(NEAR, FAR * CAP, 2 * width))  53.8 us
    all_gather x1, blocking collectives, per_device(): near_tokens = lax.all_gather(packed, 'far', tiled=True)  35.4 us
    all_to_all x1, waiting for transfers between devices, per_device(): sums = exchange(sums.reshape(FAR, block, width + LANES), 'far')  18.7 us
    ppermute x3, starting transfers between devices, per_device(): lax.ppermute(chip_sums[s], 'x', [(i, (i + s) % chips) for i in range(chip...  11.2 us
    all_to_all x1, starting transfers between devices, per_device(): near_exchange(back.reshape(NEAR, FAR * CAP, width + LANES))  9.66 us
    ppermute x3, waiting for transfers between devices, per_device(): lax.ppermute(chip_sums[s], 'x', [(i, (i + s) % chips) for i in range(chip...  6.31 us
    all_to_all x1, starting transfers between devices, per_device(): sums = exchange(sums.reshape(FAR, block, width + LANES), 'far')  6.17 us
    pallas_call x1, Pallas kernels, per_device(): pl.pallas_call(part_kernel, out_shape=(shape(chips, part_rows, 2 * hidden...  5.72 us
  transfers between devices with their start and end apart: 6, of which 3 were waited for; matrix products, arithmetic and copies ran while one was open for 0% of the time, Pallas kernels for 7%

profile of v11, /device:TPU:33, one launch (start us, length us, event | category | flops | bytes accessed | tf_op | source)
XLA Modules:
  0.0 169.4 jit_solution(14035713762809541973)
XLA Ops:
  0.6 2.3 %pack_tokens.1 = bf16[32,3200]{1,0:T(8,128)(2,1)} custom-call(bf16[32,1536]{1,0:T(8,128)(2,1)} %layer_ref.1, bf16[32,1536]{1,0:T(8,128)(2,1)} %grad_ref.1, s32[8,32]{1,0:T(8,128)} %bitcast.24, bf16[8,32]{1,0:T(8,128)(2,1)} %bitcast.25), custom_call_target="tpu_custom_call" | custom-call | tf_op jit(solution)/shard_map/pack_tokens/pallas_call | solution.py:277
  3.0 35.4 %all_gather.3.tok_ref = bf16[128,3200]{1,0:T(8,128)(2,1)S(1)} all-gather(bf16[32,3200]{1,0:T(8,128)(2,1)} %pack_tokens.1), channel_id=1, replica_groups=mesh['x'=4,'core'=2,'far'=4,'near'=4,'y'=4] {'far'}, dimensions={0}, use_global_device_ids=true | all-gather | bytes 1024000 | tf_op jit(solution)/shard_map/all_gather | solution.py:286
  38.4 1.5 select_rows.1
  39.9 0.0 copy-start.1
  39.9 0.0 copy-start.2
  39.9 0.0 copy-start.3
  39.9 53.8 %all_to_all.15 = bf16[16,24,3072]{2,1,0:T(8,128)(2,1)S(1)} all-to-all(bf16[16,24,3072]{2,1,0:T(8,128)(2,1)S(1)} %bitcast.20), channel_id=1, replica_groups={{0,1,2,3,4,5,6,7,8,9,10,11,12,13,14,15},{16,17,18,19,20,21,22,23,24,25,..., dimensions={0} | all-to-all | bytes 4718592 | tf_op jit(solution)/shard_map/all_to_all | solution.py:303
  93.8 0.0 copy-start
  93.8 0.0 copy-done.1
  93.8 0.0 copy-done.2
  93.8 0.0 copy-done.3
  93.8 4.5 %expert_rows.1 = (bf16[384,1664]{1,0:T(8,128)(2,1)}, bf16[384,768]{1,0:T(8,128)(2,1)S(1)}, bf16[384,384]{1,0:T(8,128)(2,1)S(1)}) custom-call(bf16[384,3072]{1,0:T(8,128)(2,1)S(1)} %bitcast.18, bf16[1536,384]{1,0:T(8,128)(2,1)S(1)} %bitcast.21, bf16[1536,384]{1,0:T(8,128)(2,1)S(1)} %bitcast.22, bf16[384,1536]{1,0:T(8,128)(2,1)S(1)} %bitcast.23), custom_call_target="tpu_custom_call" | custom-call | flops 2264924160 | bytes 8388608 | tf_op jit(solution)/shard_map/expert_rows/pallas_call | solution.py:306
  98.3 0.0 copy-done
  98.3 9.7 %all-to-all-start.1 = ((bf16[16,24,1664]{2,1,0:T(8,128)(2,1)}), bf16[16,24,1664]{2,1,0:T(8,128)(2,1)S(1)}, u32[]{:S(2)}, u32[]{:S(2)}) async-start(bf16[16,24,1664]{2,1,0:T(8,128)(2,1)} %bitcast.8), calls=%async_computation.1 | async-start | bytes 2555904 | tf_op jit(solution)/shard_map/all_to_all | solution.py:315
  107.9 5.7 %weight_parts.1 = (bf16[4,288,768]{2,1,0:T(8,128)(2,1)}, bf16[4,288,768]{2,1,0:T(8,128)(2,1)}) custom-call(s32[1]{0:T(128)} %bitcast.11.core_ref, bf16[384,3072]{1,0:T(8,128)(2,1)} %bitcast.19, bf16[384,768]{1,0:T(8,128)(2,1)S(1)} %get-tuple-element.24.both_ref, bf16[384,384]{1,0:T(8,128)(2,1)S(1)} %get-tuple-element.25.hidden_ref), custom_call_target="tpu_custom_call" | custom-call | flops 1358954496 | bytes 8388608 | tf_op jit(solution)/shard_map/weight_parts/pallas_call | solution.py:317
  113.7 1.9 %collective-permute-start = (bf16[4,288,768]{2,1,0:T(8,128)(2,1)}, bf16[4,288,768]{2,1,0:T(8,128)(2,1)}, u32[]{:S(2)}, u32[]{:S(2)}) collective-permute-start(bf16[4,288,768]{2,1,0:T(8,128)(2,1)} %get-tuple-element.27), channel_id=1, source_target_pairs={{0,64},{64,0},{1,65},{65,1},{2,66},{66,2},{3,67},{67,3},{4,68},{68... | collective-permute-start | bytes 5308424 | tf_op jit(solution)/shard_map/ppermute | solution.py:333
  115.6 4.0 %collective-permute-done.got_hbm = bf16[4,288,768]{2,1,0:T(8,128)(2,1)} collective-permute-done((bf16[4,288,768]{2,1,0:T(8,128)(2,1)}, bf16[4,288,768]{2,1,0:T(8,128)(2,1)}, u32[]{:S(2)}, u32[]{:S(2)}) %collective-permute-start) | collective-permute-done | bytes 1769504 | tf_op jit(solution)/shard_map/ppermute | solution.py:333
  119.6 2.9 %chip_sums.1 = (bf16[288,768]{1,0:T(8,128)(2,1)S(1)}, bf16[288,768]{1,0:T(8,128)(2,1)}, bf16[288,768]{1,0:T(8,128)(2,1)}, bf16[288,768]{1,0:T(8,128)(2,1)S(1)}) custom-call(s32[1]{0:T(128)} %bitcast.10.chip_ref, bf16[4,288,768]{2,1,0:T(8,128)(2,1)} %get-tuple-element.26.keep_hbm, bf16[4,288,768]{2,1,0:T(8,128)(2,1)} %collective-permute-done.got_hbm), custom_call_target="tpu_custom_call" | custom-call | flops 1048576 | bytes 6291456 | tf_op jit(solution)/shard_map/chip_sums/pallas_call | solution.py:334
  122.5 4.7 %collective-permute-start.1 = (bf16[288,768]{1,0:T(8,128)(2,1)}, bf16[288,768]{1,0:T(8,128)(2,1)S(1)}, u32[]{:S(2)}, u32[]{:S(2)}) collective-permute-start(bf16[288,768]{1,0:T(8,128)(2,1)} %get-tuple-element.33), channel_id=1, source_target_pairs={{0,256},{128,384},{256,0},{384,128},{1,257},{129,385},{257,1},{385... | collective-permute-start | bytes 1327112 | tf_op jit(solution)/shard_map/ppermute | solution.py:349
  127.2 2.2 %collective-permute-start.2 = (bf16[288,768]{1,0:T(8,128)(2,1)}, bf16[288,768]{1,0:T(8,128)(2,1)}, u32[]{:S(2)}, u32[]{:S(2)}) collective-permute-start(bf16[288,768]{1,0:T(8,128)(2,1)} %get-tuple-element.34), channel_id=1, source_target_pairs={{0,128},{128,256},{256,384},{384,0},{1,129},{129,257},{257,385},{3... | collective-permute-start | bytes 1327112 | tf_op jit(solution)/shard_map/ppermute | solution.py:349
  129.4 4.3 %collective-permute-start.3 = (bf16[288,768]{1,0:T(8,128)(2,1)S(1)}, bf16[288,768]{1,0:T(8,128)(2,1)}, u32[]{:S(2)}, u32[]{:S(2)}) collective-permute-start(bf16[288,768]{1,0:T(8,128)(2,1)S(1)} %get-tuple-element.35), channel_id=1, source_target_pairs={{0,384},{128,0},{256,128},{384,256},{1,385},{129,1},{257,129},{385... | collective-permute-start | bytes 1327112 | tf_op jit(solution)/shard_map/ppermute | solution.py:349
  133.7 0.0 all-to-all-done.1
  133.7 1.6 combine_rows.1
  135.4 6.2 %all-to-all-start.2 = ((bf16[4,32,1664]{2,1,0:T(8,128)(2,1)}), bf16[4,32,1664]{2,1,0:T(8,128)(2,1)S(1)}, u32[]{:S(2)}, u32[]{:S(2)}) async-start(bf16[4,32,1664]{2,1,0:T(8,128)(2,1)} %bitcast.12), calls=%async_computation.2 | async-start | bytes 851968 | tf_op jit(solution)/shard_map/all_to_all | solution.py:361
  141.5 0.0 collective-permute-done.1.refs_0_
  141.5 6.3 %collective-permute-done.2.refs_1_ = bf16[288,768]{1,0:T(8,128)(2,1)} collective-permute-done((bf16[288,768]{1,0:T(8,128)(2,1)}, bf16[288,768]{1,0:T(8,128)(2,1)}, u32[]{:S(2)}, u32[]{:S(2)}) %collective-permute-start.2) | collective-permute-done | bytes 442400 | tf_op jit(solution)/shard_map/ppermute | solution.py:349
  147.8 0.0 collective-permute-done.3.refs_2_
  147.8 2.1 %weight_sums.1 = (f32[192,384]{1,0:T(8,128)}, f32[192,384]{1,0:T(8,128)}, f32[48,1536]{1,0:T(8,128)}) custom-call(bf16[288,768]{1,0:T(8,128)(2,1)S(1)} %collective-permute-done.1.refs_0_, bf16[288,768]{1,0:T(8,128)(2,1)} %collective-permute-done.2.refs_1_, bf16[288,768]{1,0:T(8,128)(2,1)} %collective-permute-done.3.refs_2_, ...), custom_call_target="tpu_custom_call" | custom-call | flops 99999997952 | bytes 3145728 | tf_op jit(solution)/shard_map/weight_sums/pallas_call | solution.py:363
  150.0 18.7 %all-to-all-done.2.sums_ref = bf16[4,32,1664]{2,1,0:T(8,128)(2,1)S(1)} async-done(((bf16[4,32,1664]{2,1,0:T(8,128)(2,1)}), bf16[4,32,1664]{2,1,0:T(8,128)(2,1)S(1)}, u32[]{:S(2)}, u32[]{:S(2)}) %all-to-all-start.2) | async-done | bytes 426016 | tf_op jit(solution)/shard_map/all_to_all | solution.py:361
  168.7 0.7 finish.1
  (1 shorter events, 0.0 us)
Async XLA Ops:
  39.9 53.9 %copy-start.1 = (bf16[1,1536,384]{2,1,0:T(8,128)(2,1)S(1)}, bf16[1,1536,384]{2,1,0:T(8,128)(2,1)}, u32[]{:S(2)}) copy-start(bf16[1,1536,384]{2,1,0:T(8,128)(2,1)} %param.11) | copy-start | bytes 3538948
  39.9 53.9 %copy-start.2 = (bf16[1,1536,384]{2,1,0:T(8,128)(2,1)S(1)}, bf16[1,1536,384]{2,1,0:T(8,128)(2,1)}, u32[]{:S(2)}) copy-start(bf16[1,1536,384]{2,1,0:T(8,128)(2,1)} %param.12) | copy-start | bytes 3538948
  39.9 53.9 %copy-start.3 = (bf16[1,384,1536]{2,1,0:T(8,128)(2,1)S(1)}, bf16[1,384,1536]{2,1,0:T(8,128)(2,1)}, u32[]{:S(2)}) copy-start(bf16[1,384,1536]{2,1,0:T(8,128)(2,1)} %param.13) | copy-start | bytes 3538948
  93.8 4.5 %copy-start = (bf16[16,24,3072]{2,1,0:T(8,128)(2,1)}, bf16[16,24,3072]{2,1,0:T(8,128)(2,1)S(1)}, u32[]{:S(2)}) copy-start(bf16[16,24,3072]{2,1,0:T(8,128)(2,1)S(1)} %all_to_all.15) | copy-start | bytes 7077892
  98.3 35.5 %all-to-all-start.1 = ((bf16[16,24,1664]{2,1,0:T(8,128)(2,1)}), bf16[16,24,1664]{2,1,0:T(8,128)(2,1)S(1)}, u32[]{:S(2)}, u32[]{:S(2)}) async-start(bf16[16,24,1664]{2,1,0:T(8,128)(2,1)} %bitcast.8), calls=%async_computation.1 | async-start | bytes 2555904 | tf_op jit(solution)/shard_map/all_to_all | solution.py:315
  113.7 5.9 %collective-permute-start = (bf16[4,288,768]{2,1,0:T(8,128)(2,1)}, bf16[4,288,768]{2,1,0:T(8,128)(2,1)}, u32[]{:S(2)}, u32[]{:S(2)}) collective-permute-start(bf16[4,288,768]{2,1,0:T(8,128)(2,1)} %get-tuple-element.27), channel_id=1, source_target_pairs={{0,64},{64,0},{1,65},{65,1},{2,66},{66,2},{3,67},{67,3},{4,68},{68... | collective-permute-start | bytes 5308424 | tf_op jit(solution)/shard_map/ppermute | solution.py:333
  122.5 19.0 %collective-permute-start.1 = (bf16[288,768]{1,0:T(8,128)(2,1)}, bf16[288,768]{1,0:T(8,128)(2,1)S(1)}, u32[]{:S(2)}, u32[]{:S(2)}) collective-permute-start(bf16[288,768]{1,0:T(8,128)(2,1)} %get-tuple-element.33), channel_id=1, source_target_pairs={{0,256},{128,384},{256,0},{384,128},{1,257},{129,385},{257,1},{385... | collective-permute-start | bytes 1327112 | tf_op jit(solution)/shard_map/ppermute | solution.py:349
  127.2 20.6 %collective-permute-start.2 = (bf16[288,768]{1,0:T(8,128)(2,1)}, bf16[288,768]{1,0:T(8,128)(2,1)}, u32[]{:S(2)}, u32[]{:S(2)}) collective-permute-start(bf16[288,768]{1,0:T(8,128)(2,1)} %get-tuple-element.34), channel_id=1, source_target_pairs={{0,128},{128,256},{256,384},{384,0},{1,129},{129,257},{257,385},{3... | collective-permute-start | bytes 1327112 | tf_op jit(solution)/shard_map/ppermute | solution.py:349
  129.4 18.4 %collective-permute-start.3 = (bf16[288,768]{1,0:T(8,128)(2,1)S(1)}, bf16[288,768]{1,0:T(8,128)(2,1)}, u32[]{:S(2)}, u32[]{:S(2)}) collective-permute-start(bf16[288,768]{1,0:T(8,128)(2,1)S(1)} %get-tuple-element.35), channel_id=1, source_target_pairs={{0,384},{128,0},{256,128},{384,256},{1,385},{129,1},{257,129},{385... | collective-permute-start | bytes 1327112 | tf_op jit(solution)/shard_map/ppermute | solution.py:349
  135.4 33.3 %all-to-all-start.2 = ((bf16[4,32,1664]{2,1,0:T(8,128)(2,1)}), bf16[4,32,1664]{2,1,0:T(8,128)(2,1)S(1)}, u32[]{:S(2)}, u32[]{:S(2)}) async-start(bf16[4,32,1664]{2,1,0:T(8,128)(2,1)} %bitcast.12), calls=%async_computation.2 | async-start | bytes 851968 | tf_op jit(solution)/shard_map/all_to_all | solution.py:361

commit v12 on v10

--- a/solution.py
+++ b/solution.py
@@ -275,7 +275,7 @@
 
     packed = pl.pallas_call(
         pack_kernel,
-        out_shape=shape(block, 2 * width + LANES),
+        out_shape=pltpu.VMEM((block, 2 * width + LANES), BF16),
         in_specs=[hbm] * 3 + whole(1),
         out_specs=whole(1)[0],
         scratch_shapes=[pltpu.VMEM((TOP, block), jnp.int32), pltpu.SemaphoreType.DMA((3,))],

time: 167 us -> 166 us (level)
  no operation moved by 1% of the time
where the time goes in v12:
time: 166 us; the launch traced here: 164 us
  blocking collectives  90.6 us (55%)
  waiting for transfers between devices  27.1 us (16%)
  starting transfers between devices  26.7 us (16%)
  Pallas kernels  18.8 us (11%)
    all_to_all x1, blocking collectives, per_device(): near_exchange(send.reshape(NEAR, FAR * CAP, 2 * width))  46.3 us
    all_gather x1, blocking collectives, per_device(): near_tokens = lax.all_gather(packed, 'far', tiled=True)  44.3 us
    ppermute x3, waiting for transfers between devices, per_device(): lax.ppermute(chip_sums[s], 'x', [(i, (i + s) % chips) for i in range(chip...  13 us
    all_to_all x1, waiting for transfers between devices, per_device(): near_exchange(back.reshape(NEAR, FAR * CAP, width + LANES))  10.4 us
    ppermute x3, starting transfers between devices, per_device(): lax.ppermute(chip_sums[s], 'x', [(i, (i + s) % chips) for i in range(chip...  9.22 us
    all_to_all x1, starting transfers between devices, per_device(): sums = exchange(sums.reshape(FAR, block, width + LANES), 'far')  7.15 us
    all_to_all x1, starting transfers between devices, per_device(): near_exchange(back.reshape(NEAR, FAR * CAP, width + LANES))  6.02 us
    pallas_call x1, Pallas kernels, per_device(): pl.pallas_call(part_kernel, out_shape=(shape(chips, part_rows, 2 * hidden...  5.73 us
  transfers between devices with their start and end apart: 6, of which 5 were waited for; matrix products, arithmetic and copies ran while one was open for 0% of the time, Pallas kernels for 5%

profile of v12, /device:TPU:6, one launch (start us, length us, event | category | flops | bytes accessed | tf_op | source)
XLA Modules:
  0.0 163.9 jit_solution(16833825090545505798)
XLA Ops:
  0.6 1.7 %pack_tokens.1 = bf16[32,3200]{1,0:T(8,128)(2,1)S(1)} custom-call(bf16[32,1536]{1,0:T(8,128)(2,1)} %layer_ref.1, bf16[32,1536]{1,0:T(8,128)(2,1)} %grad_ref.1, s32[8,32]{1,0:T(8,128)} %bitcast.24, bf16[8,32]{1,0:T(8,128)(2,1)} %bitcast.25), custom_call_target="tpu_custom_call" | custom-call | tf_op jit(solution)/shard_map/pack_tokens/pallas_call | solution.py:276
  2.3 44.3 %all_gather.3.tok_ref = bf16[128,3200]{1,0:T(8,128)(2,1)S(1)} all-gather(bf16[32,3200]{1,0:T(8,128)(2,1)S(1)} %pack_tokens.1), channel_id=1, replica_groups=mesh['x'=4,'core'=2,'far'=4,'near'=4,'y'=4] {'far'}, dimensions={0}, use_global_device_ids=true | all-gather | bytes 1024000 | tf_op jit(solution)/shard_map/all_gather | solution.py:285
  46.6 1.5 select_rows.1
  48.0 0.0 copy-start.1
  48.1 0.0 copy-start.2
  48.1 0.0 copy-start.3
  48.1 46.3 %all_to_all.15 = bf16[16,24,3072]{2,1,0:T(8,128)(2,1)S(1)} all-to-all(bf16[16,24,3072]{2,1,0:T(8,128)(2,1)S(1)} %bitcast.20), channel_id=1, replica_groups={{0,1,2,3,4,5,6,7,8,9,10,11,12,13,14,15},{16,17,18,19,20,21,22,23,24,25,..., dimensions={0} | all-to-all | bytes 4718592 | tf_op jit(solution)/shard_map/all_to_all | solution.py:302
  94.4 0.0 copy-start
  94.4 0.0 copy-done.1
  94.4 0.0 copy-done.2
  94.4 0.0 copy-done.3
  94.4 4.5 %expert_rows.1 = (bf16[384,1664]{1,0:T(8,128)(2,1)}, bf16[384,768]{1,0:T(8,128)(2,1)S(1)}, bf16[384,384]{1,0:T(8,128)(2,1)S(1)}) custom-call(bf16[384,3072]{1,0:T(8,128)(2,1)S(1)} %bitcast.18, bf16[1536,384]{1,0:T(8,128)(2,1)S(1)} %bitcast.21, bf16[1536,384]{1,0:T(8,128)(2,1)S(1)} %bitcast.22, bf16[384,1536]{1,0:T(8,128)(2,1)S(1)} %bitcast.23), custom_call_target="tpu_custom_call" | custom-call | flops 2264924160 | bytes 8388608 | tf_op jit(solution)/shard_map/expert_rows/pallas_call | solution.py:305
  98.9 0.0 copy-done
  98.9 6.0 %all-to-all-start.1 = ((bf16[16,24,1664]{2,1,0:T(8,128)(2,1)}), bf16[16,24,1664]{2,1,0:T(8,128)(2,1)S(1)}, u32[]{:S(2)}, u32[]{:S(2)}) async-start(bf16[16,24,1664]{2,1,0:T(8,128)(2,1)} %bitcast.8), calls=%async_computation.1 | async-start | bytes 2555904 | tf_op jit(solution)/shard_map/all_to_all | solution.py:314
  104.9 5.7 %weight_parts.1 = (bf16[4,288,768]{2,1,0:T(8,128)(2,1)}, bf16[4,288,768]{2,1,0:T(8,128)(2,1)}) custom-call(s32[1]{0:T(128)} %bitcast.11.core_ref, bf16[384,3072]{1,0:T(8,128)(2,1)} %bitcast.19, bf16[384,768]{1,0:T(8,128)(2,1)S(1)} %get-tuple-element.24.both_ref, bf16[384,384]{1,0:T(8,128)(2,1)S(1)} %get-tuple-element.25.hidden_ref), custom_call_target="tpu_custom_call" | custom-call | flops 1358954496 | bytes 8388608 | tf_op jit(solution)/shard_map/weight_parts/pallas_call | solution.py:316
  110.6 4.3 %collective-permute-start = (bf16[4,288,768]{2,1,0:T(8,128)(2,1)}, bf16[4,288,768]{2,1,0:T(8,128)(2,1)}, u32[]{:S(2)}, u32[]{:S(2)}) collective-permute-start(bf16[4,288,768]{2,1,0:T(8,128)(2,1)} %get-tuple-element.27), channel_id=1, source_target_pairs={{0,64},{64,0},{1,65},{65,1},{2,66},{66,2},{3,67},{67,3},{4,68},{68... | collective-permute-start | bytes 5308424 | tf_op jit(solution)/shard_map/ppermute | solution.py:332
  115.0 3.6 %collective-permute-done.got_hbm = bf16[4,288,768]{2,1,0:T(8,128)(2,1)} collective-permute-done((bf16[4,288,768]{2,1,0:T(8,128)(2,1)}, bf16[4,288,768]{2,1,0:T(8,128)(2,1)}, u32[]{:S(2)}, u32[]{:S(2)}) %collective-permute-start) | collective-permute-done | bytes 1769504 | tf_op jit(solution)/shard_map/ppermute | solution.py:332
  118.6 2.1 %chip_sums.1 = (bf16[288,768]{1,0:T(8,128)(2,1)S(1)}, bf16[288,768]{1,0:T(8,128)(2,1)S(1)}, bf16[288,768]{1,0:T(8,128)(2,1)S(1)}, bf16[288,768]{1,0:T(8,128)(2,1)S(1)}) custom-call(s32[1]{0:T(128)} %bitcast.10.chip_ref, bf16[4,288,768]{2,1,0:T(8,128)(2,1)} %get-tuple-element.26.keep_hbm, bf16[4,288,768]{2,1,0:T(8,128)(2,1)} %collective-permute-done.got_hbm), custom_call_target="tpu_custom_call" | custom-call | flops 1048576 | bytes 6291456 | tf_op jit(solution)/shard_map/chip_sums/pallas_call | solution.py:333
  120.7 10.4 %all-to-all-done.1 = bf16[16,24,1664]{2,1,0:T(8,128)(2,1)S(1)} async-done(((bf16[16,24,1664]{2,1,0:T(8,128)(2,1)}), bf16[16,24,1664]{2,1,0:T(8,128)(2,1)S(1)}, u32[]{:S(2)}, u32[]{:S(2)}) %all-to-all-start.1) | async-done | bytes 1277984 | tf_op jit(solution)/shard_map/all_to_all | solution.py:314
  131.2 1.6 combine_rows.1
  132.8 7.2 %all-to-all-start.2 = ((bf16[4,32,1664]{2,1,0:T(8,128)(2,1)}), bf16[4,32,1664]{2,1,0:T(8,128)(2,1)S(1)}, u32[]{:S(2)}, u32[]{:S(2)}) async-start(bf16[4,32,1664]{2,1,0:T(8,128)(2,1)} %bitcast.12), calls=%async_computation.2 | async-start | bytes 851968 | tf_op jit(solution)/shard_map/all_to_all | solution.py:360
  139.9 3.3 %collective-permute-start.1 = (bf16[288,768]{1,0:T(8,128)(2,1)S(1)}, bf16[288,768]{1,0:T(8,128)(2,1)S(1)}, u32[]{:S(2)}, u32[]{:S(2)}) collective-permute-start(bf16[288,768]{1,0:T(8,128)(2,1)S(1)} %get-tuple-element.33), channel_id=1, source_target_pairs={{0,256},{128,384},{256,0},{384,128},{1,257},{129,385},{257,1},{385... | collective-permute-start | bytes 1327112 | tf_op jit(solution)/shard_map/ppermute | solution.py:348
  143.2 4.0 %collective-permute-start.2 = (bf16[288,768]{1,0:T(8,128)(2,1)S(1)}, bf16[288,768]{1,0:T(8,128)(2,1)S(1)}, u32[]{:S(2)}, u32[]{:S(2)}) collective-permute-start(bf16[288,768]{1,0:T(8,128)(2,1)S(1)} %get-tuple-element.34), channel_id=1, source_target_pairs={{0,128},{128,256},{256,384},{384,0},{1,129},{129,257},{257,385},{3... | collective-permute-start | bytes 1327112 | tf_op jit(solution)/shard_map/ppermute | solution.py:348
  147.3 1.9 %collective-permute-start.3 = (bf16[288,768]{1,0:T(8,128)(2,1)S(1)}, bf16[288,768]{1,0:T(8,128)(2,1)S(1)}, u32[]{:S(2)}, u32[]{:S(2)}) collective-permute-start(bf16[288,768]{1,0:T(8,128)(2,1)S(1)} %get-tuple-element.35), channel_id=1, source_target_pairs={{0,384},{128,0},{256,128},{384,256},{1,385},{129,1},{257,129},{385... | collective-permute-start | bytes 1327112 | tf_op jit(solution)/shard_map/ppermute | solution.py:348
  149.2 7.1 %collective-permute-done.1.refs_0_ = bf16[288,768]{1,0:T(8,128)(2,1)S(1)} collective-permute-done((bf16[288,768]{1,0:T(8,128)(2,1)S(1)}, bf16[288,768]{1,0:T(8,128)(2,1)S(1)}, u32[]{:S(2)}, u32[]{:S(2)}) %collective-permute-start.1) | collective-permute-done | bytes 442400 | tf_op jit(solution)/shard_map/ppermute | solution.py:348
  156.3 3.1 %collective-permute-done.2.refs_1_ = bf16[288,768]{1,0:T(8,128)(2,1)S(1)} collective-permute-done((bf16[288,768]{1,0:T(8,128)(2,1)S(1)}, bf16[288,768]{1,0:T(8,128)(2,1)S(1)}, u32[]{:S(2)}, u32[]{:S(2)}) %collective-permute-start.2) | collective-permute-done | bytes 442400 | tf_op jit(solution)/shard_map/ppermute | solution.py:348
  159.4 2.8 %collective-permute-done.3.refs_2_ = bf16[288,768]{1,0:T(8,128)(2,1)S(1)} collective-permute-done((bf16[288,768]{1,0:T(8,128)(2,1)S(1)}, bf16[288,768]{1,0:T(8,128)(2,1)S(1)}, u32[]{:S(2)}, u32[]{:S(2)}) %collective-permute-start.3) | collective-permute-done | bytes 442400 | tf_op jit(solution)/shard_map/ppermute | solution.py:348
  162.2 1.0 weight_sums.1
  163.2 0.0 all-to-all-done.2.sums_ref
  163.2 0.7 finish.1
  (1 shorter events, 0.0 us)
Async XLA Ops:
  48.0 46.3 %copy-start.1 = (bf16[1,1536,384]{2,1,0:T(8,128)(2,1)S(1)}, bf16[1,1536,384]{2,1,0:T(8,128)(2,1)}, u32[]{:S(2)}) copy-start(bf16[1,1536,384]{2,1,0:T(8,128)(2,1)} %param.11) | copy-start | bytes 3538948
  48.1 46.3 %copy-start.2 = (bf16[1,1536,384]{2,1,0:T(8,128)(2,1)S(1)}, bf16[1,1536,384]{2,1,0:T(8,128)(2,1)}, u32[]{:S(2)}) copy-start(bf16[1,1536,384]{2,1,0:T(8,128)(2,1)} %param.12) | copy-start | bytes 3538948
  48.1 46.3 %copy-start.3 = (bf16[1,384,1536]{2,1,0:T(8,128)(2,1)S(1)}, bf16[1,384,1536]{2,1,0:T(8,128)(2,1)}, u32[]{:S(2)}) copy-start(bf16[1,384,1536]{2,1,0:T(8,128)(2,1)} %param.13) | copy-start | bytes 3538948
  94.4 4.5 %copy-start = (bf16[16,24,3072]{2,1,0:T(8,128)(2,1)}, bf16[16,24,3072]{2,1,0:T(8,128)(2,1)S(1)}, u32[]{:S(2)}) copy-start(bf16[16,24,3072]{2,1,0:T(8,128)(2,1)S(1)} %all_to_all.15) | copy-start | bytes 7077892
  98.9 32.3 %all-to-all-start.1 = ((bf16[16,24,1664]{2,1,0:T(8,128)(2,1)}), bf16[16,24,1664]{2,1,0:T(8,128)(2,1)S(1)}, u32[]{:S(2)}, u32[]{:S(2)}) async-start(bf16[16,24,1664]{2,1,0:T(8,128)(2,1)} %bitcast.8), calls=%async_computation.1 | async-start | bytes 2555904 | tf_op jit(solution)/shard_map/all_to_all | solution.py:314
  110.6 8.0 %collective-permute-start = (bf16[4,288,768]{2,1,0:T(8,128)(2,1)}, bf16[4,288,768]{2,1,0:T(8,128)(2,1)}, u32[]{:S(2)}, u32[]{:S(2)}) collective-permute-start(bf16[4,288,768]{2,1,0:T(8,128)(2,1)} %get-tuple-element.27), channel_id=1, source_target_pairs={{0,64},{64,0},{1,65},{65,1},{2,66},{66,2},{3,67},{67,3},{4,68},{68... | collective-permute-start | bytes 5308424 | tf_op jit(solution)/shard_map/ppermute | solution.py:332
  132.8 30.4 %all-to-all-start.2 = ((bf16[4,32,1664]{2,1,0:T(8,128)(2,1)}), bf16[4,32,1664]{2,1,0:T(8,128)(2,1)S(1)}, u32[]{:S(2)}, u32[]{:S(2)}) async-start(bf16[4,32,1664]{2,1,0:T(8,128)(2,1)} %bitcast.12), calls=%async_computation.2 | async-start | bytes 851968 | tf_op jit(solution)/shard_map/all_to_all | solution.py:360
  139.9 16.4 %collective-permute-start.1 = (bf16[288,768]{1,0:T(8,128)(2,1)S(1)}, bf16[288,768]{1,0:T(8,128)(2,1)S(1)}, u32[]{:S(2)}, u32[]{:S(2)}) collective-permute-start(bf16[288,768]{1,0:T(8,128)(2,1)S(1)} %get-tuple-element.33), channel_id=1, source_target_pairs={{0,256},{128,384},{256,0},{384,128},{1,257},{129,385},{257,1},{385... | collective-permute-start | bytes 1327112 | tf_op jit(solution)/shard_map/ppermute | solution.py:348
  143.2 16.2 %collective-permute-start.2 = (bf16[288,768]{1,0:T(8,128)(2,1)S(1)}, bf16[288,768]{1,0:T(8,128)(2,1)S(1)}, u32[]{:S(2)}, u32[]{:S(2)}) collective-permute-start(bf16[288,768]{1,0:T(8,128)(2,1)S(1)} %get-tuple-element.34), channel_id=1, source_target_pairs={{0,128},{128,256},{256,384},{384,0},{1,129},{129,257},{257,385},{3... | collective-permute-start | bytes 1327112 | tf_op jit(solution)/shard_map/ppermute | solution.py:348
  147.3 14.9 %collective-permute-start.3 = (bf16[288,768]{1,0:T(8,128)(2,1)S(1)}, bf16[288,768]{1,0:T(8,128)(2,1)S(1)}, u32[]{:S(2)}, u32[]{:S(2)}) collective-permute-start(bf16[288,768]{1,0:T(8,128)(2,1)S(1)} %get-tuple-element.35), channel_id=1, source_target_pairs={{0,384},{128,0},{256,128},{384,256},{1,385},{129,1},{257,129},{385... | collective-permute-start | bytes 1327112 | tf_op jit(solution)/shard_map/ppermute | solution.py:348

commit v13 on v12

--- a/solution.py
+++ b/solution.py
@@ -112,7 +112,7 @@
     pick_ref[...] = jnp.where(chosen, 1.0, 0.0).astype(BF16)
 
 
-def expert_kernel(rows_ref, gate_ref, up_ref, down_ref, ret_ref, both_ref, hidden_ref):
+def expert_kernel(rows_ref, gate_ref, up_ref, down_ref, ret_hbm, both_ref, hidden_ref, ret, sems):
     width, hidden_width = gate_ref.shape
     scaled = rows_ref[:, width:]
     rows = rows_ref[:, :width]
@@ -126,12 +126,21 @@
     prob_grad = jnp.sum(hidden.astype(F32) * grad_hidden, axis=1, keepdims=True)
     gate_grad = (grad_hidden * pre_up * sig * (1.0 + pre_gate * (1.0 - sig))).astype(BF16)
     up_grad = (grad_hidden * silu).astype(BF16)
-    back = dot(gate_grad, gate, ((1,), (1,))) + dot(up_grad, up, ((1,), (1,)))
-    ret_ref[:, :width] = back.astype(BF16)
-    ret_ref[:, width:] = jnp.broadcast_to(prob_grad, (rows.shape[0], LANES)).astype(BF16)
+    ret[:, width:] = jnp.broadcast_to(prob_grad, (rows.shape[0], LANES)).astype(BF16)
     both_ref[:, :hidden_width] = gate_grad
     both_ref[:, hidden_width:] = up_grad
     hidden_ref[...] = hidden
+    stores = []
+    third = width // 3
+    for i, low in enumerate((2 * third, third, 0)):
+        span = slice(low, low + third)
+        back = dot(gate_grad, gate_ref[span, :], ((1,), (1,))) + dot(up_grad, up_ref[span, :], ((1,), (1,)))
+        ret[:, span] = back.astype(BF16)
+        columns = pl.ds(low, third + LANES if i == 0 else third)
+        stores.append(pltpu.make_async_copy(ret.at[:, columns], ret_hbm.at[:, columns], sems.at[i]))
+        stores[-1].start()
+    for store in stores:
+        store.wait()
 
 
 def part_kernel(core_ref, rows_hbm, both_ref, hidden_ref, keep_hbm, give_hbm, rows, keep, give, in_sems, out_sems):
@@ -306,7 +315,8 @@
         expert_kernel,
         out_shape=(shape(slots, width + LANES), shape(slots, 2 * hidden_width), shape(slots, hidden_width)),
         in_specs=whole(4),
-        out_specs=tuple(whole(3)),
+        out_specs=(hbm,) + tuple(whole(2)),
+        scratch_shapes=[pltpu.VMEM((slots, width + LANES), BF16), pltpu.SemaphoreType.DMA((3,))],
         compiler_params=params(32),
         cost_estimate=cost(5 * matmul, 8 * MIB),
         name="expert_rows",

time: 166 us -> 166 us (level)
  no operation moved by 1% of the time
where the time goes in v13:
time: 166 us; the launch traced here: 164 us
  blocking collectives  90.6 us (55%)
  waiting for transfers between devices  27.1 us (16%)
  starting transfers between devices  26.7 us (16%)
  Pallas kernels  18.5 us (11%)
    all_to_all x1, blocking collectives, per_device(): near_exchange(send.reshape(NEAR, FAR * CAP, 2 * width))  46.3 us
    all_gather x1, blocking collectives, per_device(): near_tokens = lax.all_gather(packed, 'far', tiled=True)  44.3 us
    ppermute x3, waiting for transfers between devices, per_device(): lax.ppermute(chip_sums[s], 'x', [(i, (i + s) % chips) for i in range(chip...  13 us
    all_to_all x1, waiting for transfers between devices, per_device(): near_exchange(back.reshape(NEAR, FAR * CAP, width + LANES))  10.4 us
    ppermute x3, starting transfers between devices, per_device(): lax.ppermute(chip_sums[s], 'x', [(i, (i + s) % chips) for i in range(chip...  9.22 us
    all_to_all x1, starting transfers between devices, per_device(): sums = exchange(sums.reshape(FAR, block, width + LANES), 'far')  7.15 us
    all_to_all x1, starting transfers between devices, per_device(): near_exchange(back.reshape(NEAR, FAR * CAP, width + LANES))  6.03 us
    pallas_call x1, Pallas kernels, per_device(): pl.pallas_call(part_kernel, out_shape=(shape(chips, part_rows, 2 * hidden...  5.72 us
  transfers between devices with their start and end apart: 6, of which 5 were waited for; matrix products, arithmetic and copies ran while one was open for 0% of the time, Pallas kernels for 5%

profile of v13, /device:TPU:6, one launch (start us, length us, event | category | flops | bytes accessed | tf_op | source)
XLA Modules:
  0.0 163.7 jit_solution(5987238307930541565)
XLA Ops:
  0.6 1.7 %pack_tokens.1 = bf16[32,3200]{1,0:T(8,128)(2,1)S(1)} custom-call(bf16[32,1536]{1,0:T(8,128)(2,1)} %layer_ref.1, bf16[32,1536]{1,0:T(8,128)(2,1)} %grad_ref.1, s32[8,32]{1,0:T(8,128)} %bitcast.24, bf16[8,32]{1,0:T(8,128)(2,1)} %bitcast.25), custom_call_target="tpu_custom_call" | custom-call | tf_op jit(solution)/shard_map/pack_tokens/pallas_call | solution.py:285
  2.3 44.3 %all_gather.3.tok_ref = bf16[128,3200]{1,0:T(8,128)(2,1)S(1)} all-gather(bf16[32,3200]{1,0:T(8,128)(2,1)S(1)} %pack_tokens.1), channel_id=1, replica_groups=mesh['x'=4,'core'=2,'far'=4,'near'=4,'y'=4] {'far'}, dimensions={0}, use_global_device_ids=true | all-gather | bytes 1024000 | tf_op jit(solution)/shard_map/all_gather | solution.py:294
  46.6 1.5 select_rows.1
  48.0 0.0 copy-start.1
  48.1 0.0 copy-start.2
  48.1 0.0 copy-start.3
  48.1 46.3 %all_to_all.15 = bf16[16,24,3072]{2,1,0:T(8,128)(2,1)S(1)} all-to-all(bf16[16,24,3072]{2,1,0:T(8,128)(2,1)S(1)} %bitcast.20), channel_id=1, replica_groups={{0,1,2,3,4,5,6,7,8,9,10,11,12,13,14,15},{16,17,18,19,20,21,22,23,24,25,..., dimensions={0} | all-to-all | bytes 4718592 | tf_op jit(solution)/shard_map/all_to_all | solution.py:311
  94.4 0.0 copy-start
  94.4 0.0 copy-done.1
  94.4 0.0 copy-done.2
  94.4 0.0 copy-done.3
  94.4 4.2 %expert_rows.1 = (bf16[384,1664]{1,0:T(8,128)(2,1)}, bf16[384,768]{1,0:T(8,128)(2,1)S(1)}, bf16[384,384]{1,0:T(8,128)(2,1)S(1)}) custom-call(bf16[384,3072]{1,0:T(8,128)(2,1)S(1)} %bitcast.18, bf16[1536,384]{1,0:T(8,128)(2,1)S(1)} %bitcast.21, bf16[1536,384]{1,0:T(8,128)(2,1)S(1)} %bitcast.22, bf16[384,1536]{1,0:T(8,128)(2,1)S(1)} %bitcast.23), custom_call_target="tpu_custom_call" | custom-call | flops 2264924160 | bytes 8388608 | tf_op jit(solution)/shard_map/expert_rows/pallas_call | solution.py:314
  98.6 0.0 copy-done
  98.6 6.0 %all-to-all-start.1 = ((bf16[16,24,1664]{2,1,0:T(8,128)(2,1)}), bf16[16,24,1664]{2,1,0:T(8,128)(2,1)S(1)}, u32[]{:S(2)}, u32[]{:S(2)}) async-start(bf16[16,24,1664]{2,1,0:T(8,128)(2,1)} %bitcast.8), calls=%async_computation.1 | async-start | bytes 2555904 | tf_op jit(solution)/shard_map/all_to_all | solution.py:324
  104.6 5.7 %weight_parts.1 = (bf16[4,288,768]{2,1,0:T(8,128)(2,1)}, bf16[4,288,768]{2,1,0:T(8,128)(2,1)}) custom-call(s32[1]{0:T(128)} %bitcast.11.core_ref, bf16[384,3072]{1,0:T(8,128)(2,1)} %bitcast.19, bf16[384,768]{1,0:T(8,128)(2,1)S(1)} %get-tuple-element.24.both_ref, bf16[384,384]{1,0:T(8,128)(2,1)S(1)} %get-tuple-element.25.hidden_ref), custom_call_target="tpu_custom_call" | custom-call | flops 1358954496 | bytes 8388608 | tf_op jit(solution)/shard_map/weight_parts/pallas_call | solution.py:326
  110.4 4.3 %collective-permute-start = (bf16[4,288,768]{2,1,0:T(8,128)(2,1)}, bf16[4,288,768]{2,1,0:T(8,128)(2,1)}, u32[]{:S(2)}, u32[]{:S(2)}) collective-permute-start(bf16[4,288,768]{2,1,0:T(8,128)(2,1)} %get-tuple-element.27), channel_id=1, source_target_pairs={{0,64},{64,0},{1,65},{65,1},{2,66},{66,2},{3,67},{67,3},{4,68},{68... | collective-permute-start | bytes 5308424 | tf_op jit(solution)/shard_map/ppermute | solution.py:342
  114.7 3.6 %collective-permute-done.got_hbm = bf16[4,288,768]{2,1,0:T(8,128)(2,1)} collective-permute-done((bf16[4,288,768]{2,1,0:T(8,128)(2,1)}, bf16[4,288,768]{2,1,0:T(8,128)(2,1)}, u32[]{:S(2)}, u32[]{:S(2)}) %collective-permute-start) | collective-permute-done | bytes 1769504 | tf_op jit(solution)/shard_map/ppermute | solution.py:342
  118.3 2.1 %chip_sums.1 = (bf16[288,768]{1,0:T(8,128)(2,1)S(1)}, bf16[288,768]{1,0:T(8,128)(2,1)S(1)}, bf16[288,768]{1,0:T(8,128)(2,1)S(1)}, bf16[288,768]{1,0:T(8,128)(2,1)S(1)}) custom-call(s32[1]{0:T(128)} %bitcast.10.chip_ref, bf16[4,288,768]{2,1,0:T(8,128)(2,1)} %get-tuple-element.26.keep_hbm, bf16[4,288,768]{2,1,0:T(8,128)(2,1)} %collective-permute-done.got_hbm), custom_call_target="tpu_custom_call" | custom-call | flops 1048576 | bytes 6291456 | tf_op jit(solution)/shard_map/chip_sums/pallas_call | solution.py:343
  120.5 10.4 %all-to-all-done.1 = bf16[16,24,1664]{2,1,0:T(8,128)(2,1)S(1)} async-done(((bf16[16,24,1664]{2,1,0:T(8,128)(2,1)}), bf16[16,24,1664]{2,1,0:T(8,128)(2,1)S(1)}, u32[]{:S(2)}, u32[]{:S(2)}) %all-to-all-start.1) | async-done | bytes 1277984 | tf_op jit(solution)/shard_map/all_to_all | solution.py:324
  130.9 1.6 combine_rows.1
  132.5 7.1 %all-to-all-start.2 = ((bf16[4,32,1664]{2,1,0:T(8,128)(2,1)}), bf16[4,32,1664]{2,1,0:T(8,128)(2,1)S(1)}, u32[]{:S(2)}, u32[]{:S(2)}) async-start(bf16[4,32,1664]{2,1,0:T(8,128)(2,1)} %bitcast.12), calls=%async_computation.2 | async-start | bytes 851968 | tf_op jit(solution)/shard_map/all_to_all | solution.py:370
  139.7 3.3 %collective-permute-start.1 = (bf16[288,768]{1,0:T(8,128)(2,1)S(1)}, bf16[288,768]{1,0:T(8,128)(2,1)S(1)}, u32[]{:S(2)}, u32[]{:S(2)}) collective-permute-start(bf16[288,768]{1,0:T(8,128)(2,1)S(1)} %get-tuple-element.33), channel_id=1, source_target_pairs={{0,256},{128,384},{256,0},{384,128},{1,257},{129,385},{257,1},{385... | collective-permute-start | bytes 1327112 | tf_op jit(solution)/shard_map/ppermute | solution.py:358
  143.0 4.0 %collective-permute-start.2 = (bf16[288,768]{1,0:T(8,128)(2,1)S(1)}, bf16[288,768]{1,0:T(8,128)(2,1)S(1)}, u32[]{:S(2)}, u32[]{:S(2)}) collective-permute-start(bf16[288,768]{1,0:T(8,128)(2,1)S(1)} %get-tuple-element.34), channel_id=1, source_target_pairs={{0,128},{128,256},{256,384},{384,0},{1,129},{129,257},{257,385},{3... | collective-permute-start | bytes 1327112 | tf_op jit(solution)/shard_map/ppermute | solution.py:358
  147.0 1.9 %collective-permute-start.3 = (bf16[288,768]{1,0:T(8,128)(2,1)S(1)}, bf16[288,768]{1,0:T(8,128)(2,1)S(1)}, u32[]{:S(2)}, u32[]{:S(2)}) collective-permute-start(bf16[288,768]{1,0:T(8,128)(2,1)S(1)} %get-tuple-element.35), channel_id=1, source_target_pairs={{0,384},{128,0},{256,128},{384,256},{1,385},{129,1},{257,129},{385... | collective-permute-start | bytes 1327112 | tf_op jit(solution)/shard_map/ppermute | solution.py:358
  148.9 7.1 %collective-permute-done.1.refs_0_ = bf16[288,768]{1,0:T(8,128)(2,1)S(1)} collective-permute-done((bf16[288,768]{1,0:T(8,128)(2,1)S(1)}, bf16[288,768]{1,0:T(8,128)(2,1)S(1)}, u32[]{:S(2)}, u32[]{:S(2)}) %collective-permute-start.1) | collective-permute-done | bytes 442400 | tf_op jit(solution)/shard_map/ppermute | solution.py:358
  156.0 3.1 %collective-permute-done.2.refs_1_ = bf16[288,768]{1,0:T(8,128)(2,1)S(1)} collective-permute-done((bf16[288,768]{1,0:T(8,128)(2,1)S(1)}, bf16[288,768]{1,0:T(8,128)(2,1)S(1)}, u32[]{:S(2)}, u32[]{:S(2)}) %collective-permute-start.2) | collective-permute-done | bytes 442400 | tf_op jit(solution)/shard_map/ppermute | solution.py:358
  159.1 2.8 %collective-permute-done.3.refs_2_ = bf16[288,768]{1,0:T(8,128)(2,1)S(1)} collective-permute-done((bf16[288,768]{1,0:T(8,128)(2,1)S(1)}, bf16[288,768]{1,0:T(8,128)(2,1)S(1)}, u32[]{:S(2)}, u32[]{:S(2)}) %collective-permute-start.3) | collective-permute-done | bytes 442400 | tf_op jit(solution)/shard_map/ppermute | solution.py:358
  161.9 1.0 weight_sums.1
  163.0 0.0 all-to-all-done.2.sums_ref
  163.0 0.7 finish.1
  (1 shorter events, 0.0 us)
Async XLA Ops:
  48.0 46.3 %copy-start.1 = (bf16[1,1536,384]{2,1,0:T(8,128)(2,1)S(1)}, bf16[1,1536,384]{2,1,0:T(8,128)(2,1)}, u32[]{:S(2)}) copy-start(bf16[1,1536,384]{2,1,0:T(8,128)(2,1)} %param.11) | copy-start | bytes 3538948
  48.1 46.3 %copy-start.2 = (bf16[1,1536,384]{2,1,0:T(8,128)(2,1)S(1)}, bf16[1,1536,384]{2,1,0:T(8,128)(2,1)}, u32[]{:S(2)}) copy-start(bf16[1,1536,384]{2,1,0:T(8,128)(2,1)} %param.12) | copy-start | bytes 3538948
  48.1 46.3 %copy-start.3 = (bf16[1,384,1536]{2,1,0:T(8,128)(2,1)S(1)}, bf16[1,384,1536]{2,1,0:T(8,128)(2,1)}, u32[]{:S(2)}) copy-start(bf16[1,384,1536]{2,1,0:T(8,128)(2,1)} %param.13) | copy-start | bytes 3538948
  94.4 4.2 %copy-start = (bf16[16,24,3072]{2,1,0:T(8,128)(2,1)}, bf16[16,24,3072]{2,1,0:T(8,128)(2,1)S(1)}, u32[]{:S(2)}) copy-start(bf16[16,24,3072]{2,1,0:T(8,128)(2,1)S(1)} %all_to_all.15) | copy-start | bytes 7077892
  98.6 32.3 %all-to-all-start.1 = ((bf16[16,24,1664]{2,1,0:T(8,128)(2,1)}), bf16[16,24,1664]{2,1,0:T(8,128)(2,1)S(1)}, u32[]{:S(2)}, u32[]{:S(2)}) async-start(bf16[16,24,1664]{2,1,0:T(8,128)(2,1)} %bitcast.8), calls=%async_computation.1 | async-start | bytes 2555904 | tf_op jit(solution)/shard_map/all_to_all | solution.py:324
  110.4 8.0 %collective-permute-start = (bf16[4,288,768]{2,1,0:T(8,128)(2,1)}, bf16[4,288,768]{2,1,0:T(8,128)(2,1)}, u32[]{:S(2)}, u32[]{:S(2)}) collective-permute-start(bf16[4,288,768]{2,1,0:T(8,128)(2,1)} %get-tuple-element.27), channel_id=1, source_target_pairs={{0,64},{64,0},{1,65},{65,1},{2,66},{66,2},{3,67},{67,3},{4,68},{68... | collective-permute-start | bytes 5308424 | tf_op jit(solution)/shard_map/ppermute | solution.py:342
  132.5 30.4 %all-to-all-start.2 = ((bf16[4,32,1664]{2,1,0:T(8,128)(2,1)}), bf16[4,32,1664]{2,1,0:T(8,128)(2,1)S(1)}, u32[]{:S(2)}, u32[]{:S(2)}) async-start(bf16[4,32,1664]{2,1,0:T(8,128)(2,1)} %bitcast.12), calls=%async_computation.2 | async-start | bytes 851968 | tf_op jit(solution)/shard_map/all_to_all | solution.py:370
  139.7 16.4 %collective-permute-start.1 = (bf16[288,768]{1,0:T(8,128)(2,1)S(1)}, bf16[288,768]{1,0:T(8,128)(2,1)S(1)}, u32[]{:S(2)}, u32[]{:S(2)}) collective-permute-start(bf16[288,768]{1,0:T(8,128)(2,1)S(1)} %get-tuple-element.33), channel_id=1, source_target_pairs={{0,256},{128,384},{256,0},{384,128},{1,257},{129,385},{257,1},{385... | collective-permute-start | bytes 1327112 | tf_op jit(solution)/shard_map/ppermute | solution.py:358
  143.0 16.2 %collective-permute-start.2 = (bf16[288,768]{1,0:T(8,128)(2,1)S(1)}, bf16[288,768]{1,0:T(8,128)(2,1)S(1)}, u32[]{:S(2)}, u32[]{:S(2)}) collective-permute-start(bf16[288,768]{1,0:T(8,128)(2,1)S(1)} %get-tuple-element.34), channel_id=1, source_target_pairs={{0,128},{128,256},{256,384},{384,0},{1,129},{129,257},{257,385},{3... | collective-permute-start | bytes 1327112 | tf_op jit(solution)/shard_map/ppermute | solution.py:358
  147.0 14.9 %collective-permute-start.3 = (bf16[288,768]{1,0:T(8,128)(2,1)S(1)}, bf16[288,768]{1,0:T(8,128)(2,1)S(1)}, u32[]{:S(2)}, u32[]{:S(2)}) collective-permute-start(bf16[288,768]{1,0:T(8,128)(2,1)S(1)} %get-tuple-element.35), channel_id=1, source_target_pairs={{0,384},{128,0},{256,128},{384,256},{1,385},{129,1},{257,129},{385... | collective-permute-start | bytes 1327112 | tf_op jit(solution)/shard_map/ppermute | solution.py:358
